TPU v7x, 32 devices: a whole 2x2x4 slice. The times are simulated.
32 devices in a mesh: group: 2 (over y), tok: 8 (over z, x), col: 2 (over core).
Axes of the slice: x: 2, y: 2, z: 4, core: 2. Of those that a mesh axis runs over, the one named last changes fastest.
Arguments:
- hidden: bfloat16 [8192, 8192], P(('group', 'tok', 'col')), parts along dimension 0, may hold values from -120 to 120
- gain_table: bfloat16 [80, 8192], P(None, 'tok'), may hold values from 0.099609375 to 1.8984375
- layer_id: int32 [2], P('group'), parts along dimension 0, may hold values from 0 to 79
- w_key: bfloat16 [8192, 512], P('tok', 'col'), may hold values from -0.0625 to 0.0625
- w_value: bfloat16 [8192, 512], P('tok', 'col'), may hold values from -0.0625 to 0.0625
- offsets: int32 [16], P(('group', 'tok')), parts along dimension 0, may hold values from 0 to 130559
- owner_map: int32 [16], P('group'), parts along dimension 0, may hold values from 0 to 7, each once
Outputs:
- key_cache: bfloat16 [2, 16384, 128], P('col', ('group', 'tok')), parts along dimension 1
- value_cache: bfloat16 [2, 16384, 128], P('col', ('group', 'tok')), parts along dimension 1
There are 2 independent parts, one for each index of `group`. A program takes and returns all parts, laid end to end along the dimension named above; an argument that names none is the same for every part. Nothing has to cross between parts.
Inputs may be any that keep to these rules, and one draw needn't show every extreme that they name: `owner_map`: each tok index owns exactly one group.
All inputs are finite; a program needn't handle non-finite values.
Results may differ from a plain program's by a relative error of at most 0.006.
Values may be sent and summed in bfloat16 or wider, within the bound.
No kernel may reach another device: no remote copies, remote signals or barrier semaphores. Data moves between devices by JAX's collectives and lax.ppermute only.
A program may use at most 64 MiB of HBM per device.

v0:
```python
import math

import jax
import jax.numpy as jnp
from jax import lax
from jax.sharding import PartitionSpec as P

HD = 128


def rotate(unrotated, position):
    size_head = unrotated.shape[-1]
    half_size = size_head // 2
    frequency = jnp.power(
        jnp.float32(500000.0), -2.0 * jnp.arange(half_size, dtype=jnp.float32) / size_head
    )
    angle = jnp.mod(position.astype(jnp.float32)[:, None] * frequency[None, :], 2.0 * math.pi)
    cosine = jnp.cos(angle)[:, None, :]
    sine = jnp.sin(angle)[:, None, :]
    values = unrotated.astype(jnp.float32)
    first = values[..., :half_size]
    second = values[..., half_size:]
    return jnp.concatenate(
        [first * cosine - second * sine, second * cosine + first * sine], axis=-1
    ).astype(jnp.bfloat16)


def normalize(values, squares_total, gain, feature_count):
    scale = lax.rsqrt(squares_total / feature_count + 1e-05)
    return (values.astype(jnp.float32) * scale[:, None] * gain.astype(jnp.float32)[None, :]).astype(
        jnp.bfloat16
    )


def add_block(pieces, normed):
    return (
        jnp.dot(normed, pieces[0], preferred_element_type=jnp.float32),
        jnp.dot(normed, pieces[1], preferred_element_type=jnp.float32),
    )


def shards(hidden, gain_table, layer_id, w_key, w_value, offsets, owner_map):
    tok_count = lax.axis_size("tok")
    col_count = lax.axis_size("col")
    gain_piece = lax.dynamic_index_in_dim(gain_table, layer_id[0], 0, keepdims=False)
    gain_full = lax.all_gather(gain_piece, "tok", axis=0, tiled=True)
    feature_count = gain_full.shape[0]
    block_rows = hidden.shape[0] * col_count
    tok_rows = lax.all_gather(hidden, "col", axis=0, tiled=True)
    wide = tok_rows.astype(jnp.float32)
    normed = normalize(tok_rows, jnp.sum(wide * wide, axis=1), gain_full, feature_count)
    key_sum, value_sum = add_block(
        (
            lax.all_gather(w_key, "tok", axis=0, tiled=True),
            lax.all_gather(w_value, "tok", axis=0, tiled=True),
        ),
        normed=normed,
    )
    key_raw = key_sum.astype(jnp.bfloat16)
    value_new = value_sum.astype(jnp.bfloat16)
    heads_here = key_raw.shape[1] // HD
    classes = tok_count // heads_here
    page = block_rows // classes
    group_ids = jnp.arange(tok_count, dtype=jnp.int32)
    inverse = jnp.zeros((tok_count,), jnp.int32).at[owner_map].set(group_ids)

    def arrange_pages(values):
        grouped = (
            values.reshape(classes, page, heads_here, HD)
            .transpose(2, 0, 1, 3)
            .reshape(tok_count, page, HD)
        )
        return jnp.take(grouped, inverse, axis=0).reshape(tok_count * page, HD)

    position = offsets[0] + jnp.arange(block_rows, dtype=jnp.int32)
    key_new = rotate(key_raw.reshape(block_rows, heads_here, HD), position).reshape(block_rows, -1)
    key_out, value_out = (
        lax.all_to_all(arrange_pages(key_new), "tok", split_axis=0, concat_axis=0, tiled=True),
        lax.all_to_all(arrange_pages(value_new), "tok", split_axis=0, concat_axis=0, tiled=True),
    )
    return (key_out.reshape(1, -1, HD), value_out.reshape(1, -1, HD))


def solution(mesh):
    in_specs = (
        P(("group", "tok", "col"), None),
        P(None, "tok"),
        P("group"),
        P("tok", "col"),
        P("tok", "col"),
        P(("group", "tok")),
        P("group"),
    )
    out_specs = (P("col", ("group", "tok"), None), P("col", ("group", "tok"), None))
    return jax.shard_map(shards, mesh=mesh, in_specs=in_specs, out_specs=out_specs, check_vma=False)
```

profile of v0, /device:TPU:0, one launch (start us, length us, event | category | flops | bytes accessed | tf_op | source)
XLA Modules:
  0.0 223.8 jit_solution(4983314947426569411)
XLA Ops:
  7.2 0.0 copy-start
  7.2 0.0 all-gather.5.cloned.1.call-start
  7.2 0.7 all-gather.5.cloned.1.call-update
  7.9 0.0 all-gather.7.cloned.1.call-start
  8.0 0.7 all-gather.7.cloned.1.call-update
  8.7 0.0 all-gather.9.cloned.1.call-start
  8.7 0.7 all-gather.9.cloned.1.call-update
  10.0 0.0 copy-done
  10.1 32.2 %all-gather = bf16[1,8192]{1,0:T(2,128)(2,1)S(1)} all-gather(bf16[1,1024]{1,0:T(2,128)(2,1)S(1)} %constant_dynamic-slice_fusion), channel_id=2, replica_groups=mesh['group'=2,'tok'=8,'col'=2] {'tok'}, dimensions={1}, use_global_device_ids=true | all-gather | bytes 18432 | tf_op jit(solution)/shard_map/all_gather | solution.py:46
  43.0 0.7 compare_select_fusion.1
  43.6 0.6 scatter_custom_fusion
  44.3 0.6 fusion.16
  44.9 0.0 all-gather.5.cloned.1.call-done
  44.9 5.1 %fusion = f32[512]{0:T(512)S(1)} fusion(bf16[512,8192]{1,0:T(8,128)(2,1)} %all-gather.5.cloned.1.call-done), kind=kLoop, calls=%fused_computation.5 | loop fusion | flops 12582400 | bytes 8390656 | tf_op jit(solution)/shard_map/reduce_sum | solution.py:51
  50.0 58.8 %all-gather.7.cloned.1.call-done = bf16[8192,256]{1,0:T(8,128)(2,1)} async-done(((bf16[1024,256]{1,0:T(8,128)(2,1)}), bf16[8192,256]{1,0:T(8,128)(2,1)}) %all-gather.7.cloned.1.call-update) | async-done | bytes 4194320 | tf_op jit(solution)/shard_map/all_gather | solution.py:54
  108.9 7.4 %fusion.7 = bf16[512,256]{0,1:T(8,128)(2,1)S(1)} fusion(bf16[8192,256]{1,0:T(8,128)(2,1)} %all-gather.7.cloned.1.call-done, bf16[512,8192]{1,0:T(8,128)(2,1)} %all-gather.5.cloned.1.call-done, f32[8192]{0:T(1024)S(1)} %bitcast.28, f32[512]{0:T(512)S(1)} %add_rsqrt_fusion), kind=kOutput, calls=%fused_computation.10 | convolution fusion | flops 2164391936 | bytes 12879872 | tf_op jit(solution)/shard_map/dot_general | solution.py:37
  116.3 0.1 convert.11
  116.3 0.1 subtract_convert_fusion
  116.4 0.2 copy.9
  116.6 0.2 copy.10
  116.8 65.9 %all-gather.9.cloned.1.call-done = bf16[8192,256]{1,0:T(8,128)(2,1)} async-done(((bf16[1024,256]{1,0:T(8,128)(2,1)}), bf16[8192,256]{1,0:T(8,128)(2,1)}) %all-gather.9.cloned.1.call-update) | async-done | bytes 4194320 | tf_op jit(solution)/shard_map/all_gather | solution.py:55
  182.7 7.0 %fusion.10 = bf16[512,256]{1,0:T(8,128)(2,1)S(1)} fusion(bf16[8192,256]{1,0:T(8,128)(2,1)} %all-gather.9.cloned.1.call-done, bf16[512,8192]{1,0:T(8,128)(2,1)} %all-gather.5.cloned.1.call-done, f32[8192]{0:T(1024)S(1)} %bitcast.29, f32[512]{0:T(512)S(1)} %add_rsqrt_fusion), kind=kOutput, calls=%fused_computation.11 | convolution fusion | flops 2164391936 | bytes 12879872 | tf_op jit(solution)/shard_map/dot_general | solution.py:38
  189.6 0.1 reshape.112
  189.8 0.1 pad_maximum_fusion
  189.9 0.6 gather_fusion
  190.5 0.6 gather_fusion.1
  191.1 0.8 broadcast_select_fusion
  192.0 11.7 %all_to_all.12 = bf16[8,128,128]{2,1,0:T(8,128)(2,1)S(1)} all-to-all(bf16[8,128,128]{2,1,0:T(8,128)(2,1)S(1)} %get-tuple-element.8), channel_id=1, replica_groups=mesh['group'=2,'tok'=8,'col'=2] {'tok'}, dimensions={0} | all-to-all | bytes 524288 | tf_op jit(solution)/shard_map/all_to_all | solution.py:78
  203.7 3.6 %all-to-all-start.1 = ((bf16[8,128,128]{2,1,0:T(8,128)(2,1)}), bf16[8,128,128]{2,1,0:T(8,128)(2,1)S(1)}, u32[]{:S(2)}, u32[]{:S(2)}) async-start(bf16[8,128,128]{2,1,0:T(8,128)(2,1)} %get-tuple-element.7), calls=%async_computation.1 | async-start | bytes 524288 | tf_op jit(solution)/shard_map/all_to_all | solution.py:79
  207.3 8.6 %all-to-all-done.1 = bf16[8,128,128]{2,1,0:T(8,128)(2,1)S(1)} async-done(((bf16[8,128,128]{2,1,0:T(8,128)(2,1)}), bf16[8,128,128]{2,1,0:T(8,128)(2,1)S(1)}, u32[]{:S(2)}, u32[]{:S(2)}) %all-to-all-start.1) | async-done | bytes 262176 | tf_op jit(solution)/shard_map/all_to_all | solution.py:79
  215.8 0.7 copy.16
  216.5 0.7 copy.17
  (10 shorter events, 0.1 us)
Async XLA Ops:
  7.2 2.9 %copy-start = (bf16[80,1024]{1,0:T(8,128)(2,1)S(1)}, bf16[80,1024]{1,0:T(8,128)(2,1)}, u32[]{:S(2)}) copy-start(bf16[80,1024]{1,0:T(8,128)(2,1)} %param.10) | copy-start | bytes 491524
  7.2 37.7 %all-gather.5.cloned.1.call-start = ((), (), s32[]{:S(2)}) async-start(), calls=%async_computation.2 | async-start | bytes 12582912 | tf_op jit(solution)/shard_map/all_gather | solution.py:49
  7.9 101.0 %all-gather.7.cloned.1.call-start = ((), (), s32[]{:S(2)}) async-start(), calls=%async_computation.3 | async-start | bytes 4718592 | tf_op jit(solution)/shard_map/all_gather | solution.py:54
  8.7 174.0 %all-gather.9.cloned.1.call-start = ((), (), s32[]{:S(2)}) async-start(), calls=%async_computation.4 | async-start | bytes 4718592 | tf_op jit(solution)/shard_map/all_gather | solution.py:55
  203.7 12.2 %all-to-all-start.1 = ((bf16[8,128,128]{2,1,0:T(8,128)(2,1)}), bf16[8,128,128]{2,1,0:T(8,128)(2,1)S(1)}, u32[]{:S(2)}, u32[]{:S(2)}) async-start(bf16[8,128,128]{2,1,0:T(8,128)(2,1)} %get-tuple-element.7), calls=%async_computation.1 | async-start | bytes 524288 | tf_op jit(solution)/shard_map/all_to_all | solution.py:79
Sparse Core Ops, SparseCore 0:
  9.6 22.5 all-gather.4
  34.3 74.5 all-gather.6
  111.0 71.6 all-gather.8
where the time goes:
time: 224 us
  waiting for transfers between devices  135 us (60%)
  blocking collectives  43.9 us (20%)
  between operations  15.2 us (7%)
  matrix products  14.4 us (6%)
  other arithmetic  7.55 us (3%)
  starting transfers between devices  3.7 us (2%)
  local copies, waits for them, and re-layouts  3.67 us (2%)
    all_gather x1, waiting for transfers between devices, shards(): lax.all_gather(w_value, 'tok', axis=0, tiled=True)  65.9 us
    all_gather x1, waiting for transfers between devices, shards(): lax.all_gather(w_key, 'tok', axis=0, tiled=True)  58.8 us
    all_gather x1, blocking collectives, shards(): gain_full = lax.all_gather(gain_piece, 'tok', axis=0, tiled=True)  32.2 us
    all_to_all x1, blocking collectives, shards(): lax.all_to_all(arrange_pages(key_new), 'tok', split_axis=0, concat_axis=0...  11.7 us
    all_to_all x1, waiting for transfers between devices, shards(): lax.all_to_all(arrange_pages(value_new), 'tok', split_axis=0, concat_axis...  8.57 us
    dot_general x1, matrix products, add_block(): jnp.dot(normed, pieces[0], preferred_element_type=jnp.float32)  7.42 us
    dot_general x1, matrix products, add_block(): jnp.dot(normed, pieces[1], preferred_element_type=jnp.float32)  6.95 us
    reduce_sum x1, other arithmetic, shards(): jnp.sum(wide * wide, axis=1)  5.1 us
  transfers between devices with their start and end apart: 4, of which 3 were waited for; matrix products, arithmetic and copies ran while one was open for 7% of the time, Pallas kernels for 0%

commit v1 on v0

v1 whole, which is shorter than its diff:
```python
import functools
import math

import jax
import jax.numpy as jnp
from jax import lax
from jax.experimental import pallas as pl
from jax.experimental.pallas import tpu as pltpu
from jax.sharding import PartitionSpec as P

HD = 128
GAIN_ROWS = 16
VMEM_LIMIT = 56 * 2**20


def rotary_table(position, size_head):
    half_size = size_head // 2
    frequency = jnp.power(
        jnp.float32(500000.0), -2.0 * jnp.arange(half_size, dtype=jnp.float32) / size_head
    )
    angle = jnp.mod(position.astype(jnp.float32)[:, None] * frequency[None, :], 2.0 * math.pi)
    return jnp.cos(angle), jnp.sin(angle)


def rotate(unrotated, position):
    half_size = unrotated.shape[-1] // 2
    cosine, sine = rotary_table(position, unrotated.shape[-1])
    cosine, sine = cosine[:, None, :], sine[:, None, :]
    values = unrotated.astype(jnp.float32)
    first = values[..., :half_size]
    second = values[..., half_size:]
    return jnp.concatenate(
        [first * cosine - second * sine, second * cosine + first * sine], axis=-1
    ).astype(jnp.bfloat16)


def normalize(values, squares_total, gain, feature_count):
    scale = lax.rsqrt(squares_total / feature_count + 1e-05)
    return (values.astype(jnp.float32) * scale[:, None] * gain.astype(jnp.float32)[None, :]).astype(
        jnp.bfloat16
    )


def general_shards(hidden, gain_table, layer_id, w_key, w_value, offsets, owner_map):
    tok_count = lax.axis_size("tok")
    col_count = lax.axis_size("col")
    gain_piece = lax.dynamic_index_in_dim(gain_table, layer_id[0], 0, keepdims=False)
    gain_full = lax.all_gather(gain_piece, "tok", axis=0, tiled=True)
    feature_count = gain_full.shape[0]
    block_rows = hidden.shape[0] * col_count
    tok_rows = lax.all_gather(hidden, "col", axis=0, tiled=True)
    wide = tok_rows.astype(jnp.float32)
    normed = normalize(tok_rows, jnp.sum(wide * wide, axis=1), gain_full, feature_count)
    key_raw, value_new = (
        jnp.dot(
            normed,
            lax.all_gather(weight, "tok", axis=0, tiled=True),
            preferred_element_type=jnp.float32,
        ).astype(jnp.bfloat16)
        for weight in (w_key, w_value)
    )
    heads_here = key_raw.shape[1] // HD
    classes = tok_count // heads_here
    page = block_rows // classes
    group_ids = jnp.arange(tok_count, dtype=jnp.int32)
    inverse = jnp.zeros((tok_count,), jnp.int32).at[owner_map].set(group_ids)

    def arrange_pages(values):
        grouped = (
            values.reshape(classes, page, heads_here, HD)
            .transpose(2, 0, 1, 3)
            .reshape(tok_count, page, HD)
        )
        return jnp.take(grouped, inverse, axis=0).reshape(tok_count * page, HD)

    position = offsets[0] + jnp.arange(block_rows, dtype=jnp.int32)
    key_new = rotate(key_raw.reshape(block_rows, heads_here, HD), position).reshape(block_rows, -1)
    key_out, value_out = (
        lax.all_to_all(arrange_pages(values), "tok", split_axis=0, concat_axis=0, tiled=True)
        for values in (key_new, value_new)
    )
    return (key_out.reshape(1, -1, HD), value_out.reshape(1, -1, HD))


def half_kernel(parity_ref, hidden_ref, half_ref):
    half_ref[...] = hidden_ref[...]


def feature_half(hidden, parity, shard, row_block, rows):
    count = hidden.shape[1] // shard // 2
    return pl.pallas_call(
        half_kernel,
        grid_spec=pltpu.PrefetchScalarGridSpec(
            num_scalar_prefetch=1,
            grid=(count,),
            in_specs=[pl.BlockSpec((rows, shard), lambda i, par: (row_block, 2 * i + par[0]))],
            out_specs=pl.BlockSpec((rows, shard), lambda i, par: (0, i)),
        ),
        out_shape=jax.ShapeDtypeStruct((rows, count * shard), hidden.dtype),
    )(parity, hidden)


def pack_kernel(scalars_ref, key_ref, value_ref, gain_ref, *piece_refs):
    rows = piece_refs[0].shape[0] - GAIN_ROWS
    columns = key_ref.shape[1]
    width = 2 * columns
    table = gain_ref[...].astype(jnp.float32)
    pick = lax.broadcasted_iota(jnp.int32, table.shape, 0) == scalars_ref[1]
    gain = jnp.sum(jnp.where(pick, table, 0.0), axis=0, keepdims=True)
    for p, piece_ref in enumerate(piece_refs):
        piece_ref[:rows, :columns] = key_ref[p * rows : (p + 1) * rows, :]
        piece_ref[:rows, columns:] = value_ref[p * rows : (p + 1) * rows, :]
        piece_ref[rows:, :] = jnp.broadcast_to(
            gain[:, p * width : (p + 1) * width], (GAIN_ROWS, width)
        ).astype(piece_ref.dtype)


def pack_weights(w_key, w_value, gain_table, group_index, layer, pieces):
    shard, columns = w_key.shape
    half = shard // 2
    rows = half // pieces
    return pl.pallas_call(
        pack_kernel,
        grid_spec=pltpu.PrefetchScalarGridSpec(
            num_scalar_prefetch=1,
            grid=(1,),
            in_specs=[
                pl.BlockSpec((half, columns), lambda i, s: (s[0], 0)),
                pl.BlockSpec((half, columns), lambda i, s: (s[0], 0)),
                pl.BlockSpec(gain_table.shape, lambda i, s: (0, 0)),
            ],
            out_specs=[
                pl.BlockSpec((rows + GAIN_ROWS, 2 * columns), lambda i, s: (0, 0))
                for _ in range(pieces)
            ],
        ),
        out_shape=[
            jax.ShapeDtypeStruct((rows + GAIN_ROWS, 2 * columns), w_key.dtype)
            for _ in range(pieces)
        ],
    )(jnp.stack([group_index, layer]), w_key, w_value, gain_table)


def multiply_kernel(line, pieces, shard, *refs):
    refs = list(refs)
    scalars_ref = refs.pop(0)
    own_ref, other_ref = refs.pop(0), refs.pop(0)
    own_pair = [refs.pop(0) for _ in range(2)]
    other_pair = [refs.pop(0) for _ in range(2)]
    scale_ref, key_ref, value_ref = refs.pop(0), refs.pop(0), refs.pop(0)
    mine = [[refs.pop(0) for _ in range(pieces)] for _ in range(line)]
    theirs = [None] + [[refs.pop(0) for _ in range(pieces)] for _ in range(line - 1)]
    key_keep, key_send, value_keep, value_send, weights, gains, rows_ref = refs
    y, x, z, c = (scalars_ref[i] for i in range(4))
    columns = key_ref.shape[1]
    width = 2 * columns
    half = shard // 2
    rows = half // pieces
    for d in range(line):
        base = jnp.bitwise_xor(z, d) * shard
        for p in range(pieces):
            gain = mine[d][p][rows : rows + 8, :].astype(jnp.float32)
            gains[:, pl.ds(pl.multiple_of(base + p * width, 128), width)] = gain
        if d == 0:
            start = pl.multiple_of(base, shard)
            weights[pl.ds(start, shard), :columns] = key_ref[...]
            weights[pl.ds(start, shard), columns:] = value_ref[...]
            continue
        for blocks, side in ((mine[d], y), (theirs[d], 1 - y)):
            for p in range(pieces):
                start = pl.multiple_of(base + side * half + p * rows, rows)
                weights[pl.ds(start, rows), :] = blocks[p][:rows, :]
    page = own_ref.shape[0] // 2
    for pair_side in range(2):
        for core_side in range(2):
            for i in range(line):
                lanes = pl.ds(i * shard, shard)
                gain = gains[0:1, lanes]
                if pair_side == 0:
                    source = (own_ref, other_ref)[core_side]
                    picked = pl.ds(pl.multiple_of((2 * i + x) * shard, shard), shard)
                    rows_ref[:, lanes] = (source[:, picked].astype(jnp.float32) * gain).astype(
                        jnp.bfloat16
                    )
                else:
                    for chunk in range(2):
                        source = (own_pair, other_pair)[core_side][chunk]
                        rows_ref[chunk * page : (chunk + 1) * page, lanes] = (
                            source[:, lanes].astype(jnp.float32) * gain
                        ).astype(jnp.bfloat16)
            product = jnp.dot(rows_ref[...], weights[...], preferred_element_type=jnp.float32)
            scale = scale_ref[pair_side * 2 + core_side]
            source_x = jnp.bitwise_xor(x, pair_side)
            core = jnp.bitwise_xor(c, core_side)
            for j in range(columns // HD):
                for part in range(2):
                    group = j * 4 + core * 2 + part
                    owner = scalars_ref[4 + group]
                    owner_z, owner_x = owner // 2, owner % 2
                    page_rows = slice(part * page, (part + 1) * page)
                    results = [
                        product[page_rows, k * columns + j * HD : k * columns + (j + 1) * HD]
                        * scale[page_rows, :]
                        for k in range(2)
                    ]

                    @pl.when(owner_x == x)
                    def _():
                        key_keep[owner_z, source_x] = results[0]
                        value_keep[owner_z, source_x] = results[1]

                    @pl.when(owner_x != x)
                    def _():
                        key_send[owner_z, source_x] = results[0].astype(jnp.bfloat16)
                        value_send[owner_z, source_x] = results[1].astype(jnp.bfloat16)


def multiply(scalars, own, other, own_pair, other_pair, scale, w_key, w_value, mine, theirs):
    line, pieces = len(mine), len(mine[0])
    shard, columns = w_key.shape
    page = own.shape[0] // 2
    operands = [
        own, other, *own_pair, *other_pair, scale, w_key, w_value,
        *[piece for blocks in mine for piece in blocks],
        *[piece for blocks in theirs[1:] for piece in blocks],
    ]
    vmem = pl.BlockSpec(memory_space=pltpu.VMEM)
    keep = jax.ShapeDtypeStruct((line, 2, page, HD), jnp.float32)
    send = jax.ShapeDtypeStruct((line, 2, page, HD), jnp.bfloat16)
    features = line * shard
    return pl.pallas_call(
        functools.partial(multiply_kernel, line, pieces, shard),
        in_specs=[pl.BlockSpec(memory_space=pltpu.SMEM)] + [vmem] * len(operands),
        out_specs=[vmem] * 4,
        out_shape=[keep, send, keep, send],
        scratch_shapes=[
            pltpu.VMEM((features, 2 * columns), jnp.bfloat16),
            pltpu.VMEM((8, features), jnp.float32),
            pltpu.VMEM((2 * page, features), jnp.bfloat16),
        ],
        compiler_params=pltpu.CompilerParams(vmem_limit_bytes=VMEM_LIMIT),
    )(scalars, *operands)


def finish_key_kernel(scalars_ref, keep_ref, came_ref, cos_ref, sin_ref, *out_refs):
    x, z = scalars_ref[1], scalars_ref[2]
    page = keep_ref.shape[2]
    for d, out_ref in enumerate(out_refs):
        owner_z = jnp.bitwise_xor(z, d)
        owner = owner_z * 2 + x
        group = jnp.int32(0)
        for g in range(2 * len(out_refs)):
            group = jnp.where(scalars_ref[4 + g] == owner, g, group)
        page_class = group % 4
        for s in range(2):
            raw = keep_ref[owner_z, s] + came_ref[owner_z, s].astype(jnp.float32)
            raw = raw.astype(jnp.bfloat16).astype(jnp.float32)
            turned = pltpu.roll(raw, HD // 2, 1)
            rotated = raw * cos_ref[s * 4 + page_class] + turned * sin_ref[s * 4 + page_class]
            out_ref[s * page : (s + 1) * page, :] = rotated.astype(jnp.bfloat16)


def finish_value_kernel(scalars_ref, keep_ref, came_ref, *out_refs):
    z = scalars_ref[2]
    page = keep_ref.shape[2]
    for d, out_ref in enumerate(out_refs):
        owner_z = jnp.bitwise_xor(z, d)
        for s in range(2):
            raw = keep_ref[owner_z, s] + came_ref[owner_z, s].astype(jnp.float32)
            out_ref[s * page : (s + 1) * page, :] = raw.astype(jnp.bfloat16)


def finish(kernel, scalars, keep, came, *tables):
    vmem = pl.BlockSpec(memory_space=pltpu.VMEM)
    line, _, page, _ = keep.shape
    return pl.pallas_call(
        kernel,
        in_specs=[pl.BlockSpec(memory_space=pltpu.SMEM)] + [vmem] * (2 + len(tables)),
        out_specs=[vmem] * line,
        out_shape=[jax.ShapeDtypeStruct((2 * page, HD), jnp.bfloat16)] * line,
        compiler_params=pltpu.CompilerParams(vmem_limit_bytes=VMEM_LIMIT),
    )(scalars, keep, came, *tables)


def place_kernel(scalars_ref, *refs):
    out_ref = refs[-1]
    z = scalars_ref[2]
    rows = refs[0].shape[0]
    for d, block_ref in enumerate(refs[:-1]):
        start = pl.multiple_of(jnp.bitwise_xor(z, d) * rows, rows)
        out_ref[pl.ds(start, rows), :] = block_ref[...]


def place(scalars, blocks):
    vmem = pl.BlockSpec(memory_space=pltpu.VMEM)
    return pl.pallas_call(
        place_kernel,
        in_specs=[pl.BlockSpec(memory_space=pltpu.SMEM)] + [vmem] * len(blocks),
        out_specs=vmem,
        out_shape=jax.ShapeDtypeStruct((len(blocks) * blocks[0].shape[0], HD), jnp.bfloat16),
    )(scalars, *blocks)


def paired_shards(hidden, gain_table, layer_id, w_key, w_value, offsets, owner_map):
    tok_count = lax.axis_size("tok")
    line = tok_count // 2
    pieces = 2
    y, tok, c = lax.axis_index("group"), lax.axis_index("tok"), lax.axis_index("col")
    x, z = tok % 2, tok // 2
    shard = w_key.shape[0]
    device_rows = hidden.shape[0]
    scalars = jnp.concatenate([jnp.stack([y, x, z, c]).astype(jnp.int32), owner_map])

    def over_x(values):
        return lax.ppermute(values, "tok", [(t, t ^ 1) for t in range(tok_count)])

    def over_z(values, distance):
        return lax.ppermute(values, "tok", [(t, t ^ (2 * distance)) for t in range(tok_count)])

    def over_y(values):
        return lax.ppermute(values, "group", [(0, 1), (1, 0)])

    def over_c(values):
        return lax.ppermute(values, "col", [(0, 1), (1, 0)])

    chunk = device_rows // 2
    away = jnp.reshape(1 - x, (1,)).astype(jnp.int32)
    own_pair = [over_x(feature_half(hidden, away, shard, i, chunk)) for i in range(2)]
    packed = pack_weights(w_key, w_value, gain_table, y.astype(jnp.int32), layer_id[0], pieces)
    mine = [packed, None, None, None]
    mine[2] = [over_z(piece, 2) for piece in packed]
    mine[1] = [over_z(piece, 1) for piece in packed]
    other = over_c(hidden)
    mine[3] = [over_z(piece, 1) for piece in mine[2]]
    theirs = [None] + [[over_y(piece) for piece in blocks] for blocks in mine[1:]]
    other_pair = [over_c(values) for values in own_pair]

    def squares(values):
        wide = values.astype(jnp.float32)
        return jnp.sum(wide * wide, axis=1)

    facts = jnp.stack(
        [
            jnp.concatenate([squares(hidden), squares(other)]),
            jnp.broadcast_to(offsets[0].astype(jnp.float32), (2 * device_rows,)),
        ]
    )
    pair_facts = over_x(facts)
    totals = jnp.concatenate([facts[0], pair_facts[0]])
    scale = lax.rsqrt(totals / hidden.shape[1] + 1e-05).reshape(4, device_rows, 1)
    scale = jnp.broadcast_to(scale, (4, device_rows, HD))
    starts = jnp.stack([facts[1, 0], pair_facts[1, 0]]).astype(jnp.int32)
    starts = jnp.where(x == 0, starts, starts[::-1])
    block = jnp.arange(2 * device_rows, dtype=jnp.int32)
    cosine, sine = rotary_table((starts[:, None] + block[None, :]).reshape(-1), HD)
    cosine = jnp.concatenate([cosine, cosine], axis=1).reshape(8, chunk, HD)
    sine = jnp.concatenate([-sine, sine], axis=1).reshape(8, chunk, HD)

    key_keep, key_send, value_keep, value_send = multiply(
        scalars, hidden, other, own_pair, other_pair, scale, w_key, w_value, mine, theirs
    )
    key_came, value_came = over_x(key_send), over_x(value_send)
    keys = finish(finish_key_kernel, scalars, key_keep, key_came, cosine, sine)
    values = finish(finish_value_kernel, scalars, value_keep, value_came)
    outs = []
    for blocks in (keys, values):
        blocks = [blocks[0]] + [over_z(blocks[d], d) for d in range(1, line)]
        outs.append(place(scalars, blocks)[None])
    return tuple(outs)


def solution(mesh):
    in_specs = (
        P(("group", "tok", "col"), None),
        P(None, "tok"),
        P("group"),
        P("tok", "col"),
        P("tok", "col"),
        P(("group", "tok")),
        P("group"),
    )
    out_specs = (P("col", ("group", "tok"), None), P("col", ("group", "tok"), None))
    paired = mesh.shape["group"] == 2 and mesh.shape["tok"] == 8 and mesh.shape["col"] == 2
    shards = paired_shards if paired else general_shards
    return jax.shard_map(shards, mesh=mesh, in_specs=in_specs, out_specs=out_specs, check_vma=False)
```

time: 224 us -> 143 us (0.64)
  waiting for transfers between devices: 135 us -> 60.1 us
  blocking collectives: 43.9 us -> 0 us
  Pallas kernels: 0 us -> 29.9 us
  starting transfers between devices: 3.7 us -> 33.5 us
  matrix products: 14.4 us -> 0 us
  between operations: 15.2 us -> 2.07 us
  other arithmetic: 7.55 us -> 11.9 us
    all_gather x3 -> x0, waiting for transfers between devices: 125 us -> none  [the longest x1 65.9 us: shards(): lax.all_gather(w_value, 'tok', axis=0, tiled=True)]
    ppermute x0 -> x26, waiting for transfers between devices: none -> 60.1 us  [the longest x12 22.5 us: over_z(): lax.ppermute(values, 'tok', [(t, t ^ 2 * distance) for t in range(tok_cou...]
    ppermute x0 -> x26, starting transfers between devices: none -> 33.5 us  [the longest x12 19 us: over_z(): lax.ppermute(values, 'tok', [(t, t ^ 2 * distance) for t in range(tok_cou...]
    all_gather x1 -> x0, blocking collectives: 32.2 us -> none  [shards(): gain_full = lax.all_gather(gain_piece, 'tok', axis=0, tiled=True)]
    pallas_call x0 -> x8, Pallas kernels: none -> 29.9 us  [the longest x1 13 us: multiply(): pl.pallas_call(functools.partial(multiply_kernel, line, pieces, shard), i...]
    dot_general x2 -> x0, matrix products: 14.4 us -> none  [the longest x1 7.42 us: add_block(): jnp.dot(normed, pieces[0], preferred_element_type=jnp.float32)]
    all_to_all x1 -> x0, blocking collectives: 11.7 us -> none  [shards(): lax.all_to_all(arrange_pages(key_new), 'tok', split_axis=0, concat_axis=0...]
    all_to_all x1 -> x0, waiting for transfers between devices: 8.57 us -> none  [shards(): lax.all_to_all(arrange_pages(value_new), 'tok', split_axis=0, concat_axis...]
  transfers between devices with their start and end apart: 4 -> 26, of which waited for: 3 -> 11; matrix products, arithmetic and copies ran while one was open for 7% -> 9% of each run, Pallas kernels for 0% -> 11%
where the time goes in v1:
time: 143 us
  waiting for transfers between devices  60.1 us (42%)
  starting transfers between devices  33.5 us (23%)
  Pallas kernels  29.9 us (21%)
  other arithmetic  11.9 us (8%)
  local copies, waits for them, and re-layouts  5.3 us (4%)
  between operations  2.07 us (1%)
    ppermute x12, waiting for transfers between devices, over_z(): lax.ppermute(values, 'tok', [(t, t ^ 2 * distance) for t in range(tok_cou...  22.5 us
    ppermute x6, waiting for transfers between devices, over_y(): return lax.ppermute(values, 'group', [(0, 1), (1, 0)])  22.2 us
    ppermute x12, starting transfers between devices, over_z(): lax.ppermute(values, 'tok', [(t, t ^ 2 * distance) for t in range(tok_cou...  19 us
    ppermute x5, waiting for transfers between devices, over_x(): return lax.ppermute(values, 'tok', [(t, t ^ 1) for t in range(tok_count)])  15.4 us
    pallas_call x1, Pallas kernels, multiply(): pl.pallas_call(functools.partial(multiply_kernel, line, pieces, shard), i...  13 us
    ppermute x6, starting transfers between devices, over_y(): return lax.ppermute(values, 'group', [(0, 1), (1, 0)])  7.06 us
    pallas_call x2, Pallas kernels, feature_half(): pl.pallas_call(half_kernel, grid_spec=pltpu.PrefetchScalarGridSpec(num_sc...  6.79 us
    ppermute x5, starting transfers between devices, over_x(): return lax.ppermute(values, 'tok', [(t, t ^ 1) for t in range(tok_count)])  6.43 us
  transfers between devices with their start and end apart: 26, of which 11 were waited for; matrix products, arithmetic and copies ran while one was open for 9% of the time, Pallas kernels for 11%

profile of v1, /device:TPU:0, one launch (start us, length us, event | category | flops | bytes accessed | tf_op | source)
XLA Modules:
  0.0 142.8 jit_solution(5920913784505400893)
XLA Ops:
  0.6 0.5 collective-permute-start
  1.1 3.4 %shard_map.86 = bf16[128,4096]{1,0:T(8,128)(2,1)} custom-call(s32[1]{0:T(128)} %bitcast.4.parity_ref, bf16[256,8192]{1,0:T(8,128)(2,1)} %refs_1_.1), custom_call_target="tpu_custom_call" | custom-call | tf_op jit(solution)/shard_map/pallas_call | solution.py:91
  4.5 2.5 %collective-permute-start.1 = (bf16[128,4096]{1,0:T(8,128)(2,1)}, bf16[128,4096]{1,0:T(8,128)(2,1)S(1)}, u32[]{:S(2)}, u32[]{:S(2)}) collective-permute-start(bf16[128,4096]{1,0:T(8,128)(2,1)} %shard_map.86), channel_id=1, source_target_pairs={{0,2},{2,0},{4,6},{6,4},{8,10},{10,8},{12,14},{14,12},{1,3},{3,1},... | collective-permute-start | bytes 3145736 | tf_op jit(solution)/shard_map/ppermute | solution.py:315
  7.1 3.4 %shard_map.87 = bf16[128,4096]{1,0:T(8,128)(2,1)} custom-call(s32[1]{0:T(128)} %bitcast.4.parity_ref, bf16[256,8192]{1,0:T(8,128)(2,1)} %refs_1_.1), custom_call_target="tpu_custom_call" | custom-call | tf_op jit(solution)/shard_map/pallas_call | solution.py:91
  11.1 0.6 pad_add_fusion.scalars_ref
  11.7 2.6 %shard_map.88 = (bf16[272,512]{1,0:T(8,128)(2,1)}, bf16[272,512]{1,0:T(8,128)(2,1)}) custom-call(s32[2]{0:T(128)} %pad_add_fusion.scalars_ref, bf16[1024,256]{1,0:T(8,128)(2,1)} %refs_8_.1, bf16[1024,256]{1,0:T(8,128)(2,1)} %refs_9_.1, bf16[80,1024]{1,0:T(8,128)(2,1)} %gain_ref.1), custom_call_target="tpu_custom_call" | custom-call | tf_op jit(solution)/shard_map/pallas_call | solution.py:122
  14.3 3.1 %collective-permute-start.8 = (bf16[272,512]{1,0:T(8,128)(2,1)}, bf16[272,512]{1,0:T(8,128)(2,1)S(1)}, u32[]{:S(2)}, u32[]{:S(2)}) collective-permute-start(bf16[272,512]{1,0:T(8,128)(2,1)} %get-tuple-element.16.refs_10_), channel_id=1, source_target_pairs={{0,8},{2,10},{4,12},{6,14},{8,0},{10,2},{12,4},{14,6},{1,9},{3,11}... | collective-permute-start | bytes 835592 | tf_op jit(solution)/shard_map/ppermute | solution.py:318
  17.4 1.6 %collective-permute-start.6 = (bf16[272,512]{1,0:T(8,128)(2,1)}, bf16[272,512]{1,0:T(8,128)(2,1)}, u32[]{:S(2)}, u32[]{:S(2)}) collective-permute-start(bf16[272,512]{1,0:T(8,128)(2,1)} %get-tuple-element.16.refs_10_), channel_id=1, source_target_pairs={{0,4},{2,6},{4,0},{6,2},{8,12},{10,14},{12,8},{14,10},{1,5},{3,7},... | collective-permute-start | bytes 835592 | tf_op jit(solution)/shard_map/ppermute | solution.py:318
  19.6 10.8 %collective-permute-done.8.refs_14_ = bf16[272,512]{1,0:T(8,128)(2,1)S(1)} collective-permute-done((bf16[272,512]{1,0:T(8,128)(2,1)}, bf16[272,512]{1,0:T(8,128)(2,1)S(1)}, u32[]{:S(2)}, u32[]{:S(2)}) %collective-permute-start.8) | collective-permute-done | bytes 278560 | tf_op jit(solution)/shard_map/ppermute | solution.py:318
  30.4 3.2 %multiply_reduce_fusion.1 = f32[256]{0:T(256)S(1)} fusion(bf16[256,8192]{1,0:T(8,128)(2,1)} %refs_1_.1), kind=kLoop, calls=%fused_computation.1 | loop fusion | flops 6291200 | bytes 4195328 | tf_op jit(solution)/shard_map/reduce_sum | solution.py:340
  33.7 3.9 %collective-permute-start.7 = (bf16[272,512]{1,0:T(8,128)(2,1)S(1)}, bf16[272,512]{1,0:T(8,128)(2,1)S(1)}, u32[]{:S(2)}, u32[]{:S(2)}) collective-permute-start(bf16[272,512]{1,0:T(8,128)(2,1)S(1)} %copy-done.3), channel_id=1, source_target_pairs={{0,4},{2,6},{4,0},{6,2},{8,12},{10,14},{12,8},{14,10},{1,5},{3,7},... | collective-permute-start | bytes 835592 | tf_op jit(solution)/shard_map/ppermute | solution.py:318
  37.6 8.0 %collective-permute-done.9.refs_15_ = bf16[272,512]{1,0:T(8,128)(2,1)} collective-permute-done((bf16[272,512]{1,0:T(8,128)(2,1)}, bf16[272,512]{1,0:T(8,128)(2,1)}, u32[]{:S(2)}, u32[]{:S(2)}) %collective-permute-start.9) | collective-permute-done | bytes 278560 | tf_op jit(solution)/shard_map/ppermute | solution.py:318
  45.6 1.3 collective-permute-start.14
  46.8 6.7 %collective-permute-done.2.refs_4_ = bf16[128,4096]{1,0:T(8,128)(2,1)S(1)} collective-permute-done((bf16[128,4096]{1,0:T(8,128)(2,1)}, bf16[128,4096]{1,0:T(8,128)(2,1)S(1)}, u32[]{:S(2)}, u32[]{:S(2)}) %collective-permute-start.2) | collective-permute-done | bytes 1048608 | tf_op jit(solution)/shard_map/ppermute | solution.py:315
  54.0 3.1 %multiply_reduce_fusion = f32[256]{0:T(256)S(1)} fusion(bf16[256,8192]{1,0:T(8,128)(2,1)} %collective-permute-done.refs_2_), kind=kLoop, calls=%fused_computation | loop fusion | flops 6291200 | bytes 4195328 | tf_op jit(solution)/shard_map/reduce_sum | solution.py:340
  57.2 1.8 %collective-permute-start.5 = (f32[2,512]{1,0:T(2,128)S(1)}, f32[2,512]{1,0:T(2,128)S(1)}, u32[]{:S(2)}, u32[]{:S(2)}) collective-permute-start(f32[2,512]{1,0:T(2,128)S(1)} %stack.30), channel_id=1, source_target_pairs={{0,2},{2,0},{4,6},{6,4},{8,10},{10,8},{12,14},{14,12},{1,3},{3,1},... | collective-permute-start | bytes 12296 | tf_op jit(solution)/shard_map/ppermute | solution.py:315
  59.0 1.5 %collective-permute-start.12 = (bf16[272,512]{1,0:T(8,128)(2,1)}, bf16[272,512]{1,0:T(8,128)(2,1)}, u32[]{:S(2)}, u32[]{:S(2)}) collective-permute-start(bf16[272,512]{1,0:T(8,128)(2,1)} %collective-permute-done.6.refs_12_), channel_id=1, source_target_pairs={{0,16},{16,0},{1,17},{17,1},{2,18},{18,2},{3,19},{19,3},{4,20},{20... | collective-permute-start | bytes 835592 | tf_op jit(solution)/shard_map/ppermute | solution.py:321
  60.5 0.7 collective-permute-start.15
  61.3 1.6 %collective-permute-start.11 = (bf16[272,512]{1,0:T(8,128)(2,1)}, bf16[272,512]{1,0:T(8,128)(2,1)}, u32[]{:S(2)}, u32[]{:S(2)}) collective-permute-start(bf16[272,512]{1,0:T(8,128)(2,1)} %collective-permute-done.9.refs_15_), channel_id=1, source_target_pairs={{0,4},{2,6},{4,0},{6,2},{8,12},{10,14},{12,8},{14,10},{1,5},{3,7},... | collective-permute-start | bytes 835592 | tf_op jit(solution)/shard_map/ppermute | solution.py:318
  62.9 0.6 concatenate.18.refs_0_.scalars_ref
  64.1 4.8 %collective-permute-done.12.refs_18_ = bf16[272,512]{1,0:T(8,128)(2,1)} collective-permute-done((bf16[272,512]{1,0:T(8,128)(2,1)}, bf16[272,512]{1,0:T(8,128)(2,1)}, u32[]{:S(2)}, u32[]{:S(2)}) %collective-permute-start.12) | collective-permute-done | bytes 278560 | tf_op jit(solution)/shard_map/ppermute | solution.py:321
  68.9 1.5 %collective-permute-start.13 = (bf16[272,512]{1,0:T(8,128)(2,1)S(1)}, bf16[272,512]{1,0:T(8,128)(2,1)}, u32[]{:S(2)}, u32[]{:S(2)}) collective-permute-start(bf16[272,512]{1,0:T(8,128)(2,1)S(1)} %collective-permute-done.7.refs_13_), channel_id=1, source_target_pairs={{0,16},{16,0},{1,17},{17,1},{2,18},{18,2},{3,19},{19,3},{4,20},{20... | collective-permute-start | bytes 835592 | tf_op jit(solution)/shard_map/ppermute | solution.py:321
  70.4 4.4 %collective-permute-done.15.refs_21_ = bf16[272,512]{1,0:T(8,128)(2,1)} collective-permute-done((bf16[272,512]{1,0:T(8,128)(2,1)}, bf16[272,512]{1,0:T(8,128)(2,1)}, u32[]{:S(2)}, u32[]{:S(2)}) %collective-permute-start.15) | collective-permute-done | bytes 278560 | tf_op jit(solution)/shard_map/ppermute | solution.py:321
  74.9 1.5 %collective-permute-start.16 = (bf16[272,512]{1,0:T(8,128)(2,1)}, bf16[272,512]{1,0:T(8,128)(2,1)}, u32[]{:S(2)}, u32[]{:S(2)}) collective-permute-start(bf16[272,512]{1,0:T(8,128)(2,1)} %copy-done.7), channel_id=1, source_target_pairs={{0,16},{16,0},{1,17},{17,1},{2,18},{18,2},{3,19},{19,3},{4,20},{20... | collective-permute-start | bytes 835592 | tf_op jit(solution)/shard_map/ppermute | solution.py:321
  76.9 0.7 maximum_convert_fusion
  77.7 0.7 broadcast_select_fusion
  78.6 2.2 %collective-permute-done.13.refs_19_ = bf16[272,512]{1,0:T(8,128)(2,1)} collective-permute-done((bf16[272,512]{1,0:T(8,128)(2,1)S(1)}, bf16[272,512]{1,0:T(8,128)(2,1)}, u32[]{:S(2)}, u32[]{:S(2)}) %collective-permute-start.13) | collective-permute-done | bytes 278560 | tf_op jit(solution)/shard_map/ppermute | solution.py:321
  80.8 6.0 %collective-permute-done.16.refs_22_ = bf16[272,512]{1,0:T(8,128)(2,1)} collective-permute-done((bf16[272,512]{1,0:T(8,128)(2,1)}, bf16[272,512]{1,0:T(8,128)(2,1)}, u32[]{:S(2)}, u32[]{:S(2)}) %collective-permute-start.16) | collective-permute-done | bytes 278560 | tf_op jit(solution)/shard_map/ppermute | solution.py:321
  86.8 4.8 %collective-permute-done.17.refs_23_ = bf16[272,512]{1,0:T(8,128)(2,1)} collective-permute-done((bf16[272,512]{1,0:T(8,128)(2,1)}, bf16[272,512]{1,0:T(8,128)(2,1)}, u32[]{:S(2)}, u32[]{:S(2)}) %collective-permute-start.17) | collective-permute-done | bytes 278560 | tf_op jit(solution)/shard_map/ppermute | solution.py:321
  91.6 1.2 broadcast_in_dim.6.refs_7_
  92.8 13.0 %shard_map.89 = (f32[4,2,128,128]{3,2,1,0:T(8,128)}, bf16[4,2,128,128]{3,2,1,0:T(8,128)(2,1)}, f32[4,2,128,128]{3,2,1,0:T(8,128)}, bf16[4,2,128,128]{3,2,1,0:T(8,128)(2,1)}) custom-call(s32[12]{0:T(128)} %concatenate.18.refs_0_.scalars_ref, bf16[256,8192]{1,0:T(8,128)(2,1)} %refs_1_.1, bf16[256,8192]{1,0:T(8,128)(2,1)} %collective-permute-done.refs_2_, ...), custom_call_target="tpu_custom_call" | custom-call | tf_op jit(solution)/shard_map/pallas_call | solution.py:231
  106.2 1.6 %collective-permute-start.22 = (bf16[4,2,128,128]{3,2,1,0:T(8,128)(2,1)}, bf16[4,2,128,128]{3,2,1,0:T(8,128)(2,1)S(1)}, u32[]{:S(2)}, u32[]{:S(2)}) collective-permute-start(bf16[4,2,128,128]{3,2,1,0:T(8,128)(2,1)} %get-tuple-element.25), channel_id=1, source_target_pairs={{0,2},{2,0},{4,6},{6,4},{8,10},{10,8},{12,14},{14,12},{1,3},{3,1},... | collective-permute-start | bytes 786440 | tf_op jit(solution)/shard_map/ppermute | solution.py:315
  108.0 2.2 %fusion.5 = (f32[8,128,64]{2,1,0:T(8,128)S(1)}, f32[8,128,64]{2,1,0:T(8,128)S(1)}, f32[8,128,64]{2,1,0:T(8,128)S(1)}) fusion(f32[64]{0:T(128)S(1)} %multiply_power_fusion, f32[8,128]{1,0:T(8,128)S(1)} %add_convert_fusion), kind=kLoop, calls=%fused_computation.11 | loop fusion | flops 524288 | bytes 790784 | tf_op jit(solution)/shard_map/neg | solution.py:357
  110.1 8.7 %collective-permute-done.22.came_ref = bf16[4,2,128,128]{3,2,1,0:T(8,128)(2,1)S(1)} collective-permute-done((bf16[4,2,128,128]{3,2,1,0:T(8,128)(2,1)}, bf16[4,2,128,128]{3,2,1,0:T(8,128)(2,1)S(1)}, u32[]{:S(2)}, u32[]{:S(2)}) %collective-permute-start.22) | collective-permute-done | bytes 262176 | tf_op jit(solution)/shard_map/ppermute | solution.py:315
  118.8 0.7 copy-done.9
  119.5 1.8 %shard_map.92 = (bf16[256,128]{1,0:T(8,128)(2,1)}, bf16[256,128]{1,0:T(8,128)(2,1)}, bf16[256,128]{1,0:T(8,128)(2,1)}, bf16[256,128]{1,0:T(8,128)(2,1)}) custom-call(s32[12]{0:T(128)} %concatenate.18.refs_0_.scalars_ref, f32[4,2,128,128]{3,2,1,0:T(8,128)} %get-tuple-element.24.keep_ref, bf16[4,2,128,128]{3,2,1,0:T(8,128)(2,1)} %copy-done.9), custom_call_target="tpu_custom_call" | custom-call | tf_op jit(solution)/shard_map/pallas_call | solution.py:276
  121.4 1.6 %collective-permute-start.23 = (bf16[256,128]{1,0:T(8,128)(2,1)}, bf16[256,128]{1,0:T(8,128)(2,1)S(1)}, u32[]{:S(2)}, u32[]{:S(2)}) collective-permute-start(bf16[256,128]{1,0:T(8,128)(2,1)} %get-tuple-element.27), channel_id=1, source_target_pairs={{0,4},{2,6},{4,0},{6,2},{8,12},{10,14},{12,8},{14,10},{1,5},{3,7},... | collective-permute-start | bytes 196616 | tf_op jit(solution)/shard_map/ppermute | solution.py:318
  122.9 1.3 pad_maximum_fusion
  124.3 2.6 %collective-permute-start.24 = (bf16[256,128]{1,0:T(8,128)(2,1)}, bf16[256,128]{1,0:T(8,128)(2,1)S(1)}, u32[]{:S(2)}, u32[]{:S(2)}) collective-permute-start(bf16[256,128]{1,0:T(8,128)(2,1)} %get-tuple-element.28), channel_id=1, source_target_pairs={{0,8},{2,10},{4,12},{6,14},{8,0},{10,2},{12,4},{14,6},{1,9},{3,11}... | collective-permute-start | bytes 196616 | tf_op jit(solution)/shard_map/ppermute | solution.py:318
  127.1 0.7 copy-done.8
  127.8 2.2 %shard_map.90 = (bf16[256,128]{1,0:T(8,128)(2,1)}, bf16[256,128]{1,0:T(8,128)(2,1)}, bf16[256,128]{1,0:T(8,128)(2,1)}, bf16[256,128]{1,0:T(8,128)(2,1)}) custom-call(s32[12]{0:T(128)} %concatenate.18.refs_0_.scalars_ref, f32[4,2,128,128]{3,2,1,0:T(8,128)} %get-tuple-element.18.keep_ref, bf16[4,2,128,128]{3,2,1,0:T(8,128)(2,1)} %copy-done.8, ...), custom_call_target="tpu_custom_call" | custom-call | tf_op jit(solution)/shard_map/pallas_call | solution.py:276
  130.0 0.7 collective-permute-start.19
  130.7 3.5 %collective-permute-start.20 = (bf16[256,128]{1,0:T(8,128)(2,1)}, bf16[256,128]{1,0:T(8,128)(2,1)S(1)}, u32[]{:S(2)}, u32[]{:S(2)}) collective-permute-start(bf16[256,128]{1,0:T(8,128)(2,1)} %get-tuple-element.22), channel_id=1, source_target_pairs={{0,8},{2,10},{4,12},{6,14},{8,0},{10,2},{12,4},{14,6},{1,9},{3,11}... | collective-permute-start | bytes 196616 | tf_op jit(solution)/shard_map/ppermute | solution.py:318
  135.1 1.7 %shard_map.93 = bf16[1024,128]{1,0:T(8,128)(2,1)} custom-call(s32[12]{0:T(128)} %concatenate.18.refs_0_.scalars_ref, bf16[256,128]{1,0:T(8,128)(2,1)} %get-tuple-element.26.refs_0_, bf16[256,128]{1,0:T(8,128)(2,1)} %copy-done.10, bf16[256,128]{1,0:T(8,128)(2,1)} %copy-done.11, bf16[256,128]{1,0:T(8,128)(2,1)} %copy-done.12), custom_call_target="tpu_custom_call" | custom-call | tf_op jit(solution)/shard_map/pallas_call | solution.py:296
  136.7 1.0 collective-permute-done.20.refs_2_
  137.8 2.7 %collective-permute-done.21.refs_3_ = bf16[256,128]{1,0:T(8,128)(2,1)S(1)} collective-permute-done((bf16[256,128]{1,0:T(8,128)(2,1)}, bf16[256,128]{1,0:T(8,128)(2,1)S(1)}, u32[]{:S(2)}, u32[]{:S(2)}) %collective-permute-start.21) | collective-permute-done | bytes 65568 | tf_op jit(solution)/shard_map/ppermute | solution.py:318
  140.5 0.6 copy-done.15
  141.1 1.7 %shard_map.91 = bf16[1024,128]{1,0:T(8,128)(2,1)} custom-call(s32[12]{0:T(128)} %concatenate.18.refs_0_.scalars_ref, bf16[256,128]{1,0:T(8,128)(2,1)} %get-tuple-element.20.refs_0_, bf16[256,128]{1,0:T(8,128)(2,1)} %copy-done.13, bf16[256,128]{1,0:T(8,128)(2,1)} %copy-done.14, bf16[256,128]{1,0:T(8,128)(2,1)} %copy-done.15), custom_call_target="tpu_custom_call" | custom-call | tf_op jit(solution)/shard_map/pallas_call | solution.py:296
  (68 shorter events, 3.5 us)
Async XLA Ops:
  0.6 52.9 %collective-permute-start = (bf16[256,8192]{1,0:T(8,128)(2,1)}, bf16[256,8192]{1,0:T(8,128)(2,1)}, u32[]{:S(2)}, u32[]{:S(2)}) collective-permute-start(bf16[256,8192]{1,0:T(8,128)(2,1)} %refs_1_.1), channel_id=1, source_target_pairs={{0,1},{1,0},{2,3},{3,2},{4,5},{5,4},{6,7},{7,6},{8,9},{9,8},{10,11... | collective-permute-start | bytes 12582920 | tf_op jit(solution)/shard_map/ppermute | solution.py:324
  4.5 42.3 %collective-permute-start.1 = (bf16[128,4096]{1,0:T(8,128)(2,1)}, bf16[128,4096]{1,0:T(8,128)(2,1)S(1)}, u32[]{:S(2)}, u32[]{:S(2)}) collective-permute-start(bf16[128,4096]{1,0:T(8,128)(2,1)} %shard_map.86), channel_id=1, source_target_pairs={{0,2},{2,0},{4,6},{6,4},{8,10},{10,8},{12,14},{14,12},{1,3},{3,1},... | collective-permute-start | bytes 3145736 | tf_op jit(solution)/shard_map/ppermute | solution.py:315
  10.5 43.1 %collective-permute-start.2 = (bf16[128,4096]{1,0:T(8,128)(2,1)}, bf16[128,4096]{1,0:T(8,128)(2,1)S(1)}, u32[]{:S(2)}, u32[]{:S(2)}) collective-permute-start(bf16[128,4096]{1,0:T(8,128)(2,1)} %shard_map.87), channel_id=1, source_target_pairs={{0,2},{2,0},{4,6},{6,4},{8,10},{10,8},{12,14},{14,12},{1,3},{3,1},... | collective-permute-start | bytes 3145736 | tf_op jit(solution)/shard_map/ppermute | solution.py:315
  14.3 19.4 %copy-start.3 = (bf16[272,512]{1,0:T(8,128)(2,1)S(1)}, bf16[272,512]{1,0:T(8,128)(2,1)}, u32[]{:S(2)}) copy-start(bf16[272,512]{1,0:T(8,128)(2,1)} %get-tuple-element.17.refs_11_) | copy-start | bytes 835588
  14.3 16.1 %collective-permute-start.8 = (bf16[272,512]{1,0:T(8,128)(2,1)}, bf16[272,512]{1,0:T(8,128)(2,1)S(1)}, u32[]{:S(2)}, u32[]{:S(2)}) collective-permute-start(bf16[272,512]{1,0:T(8,128)(2,1)} %get-tuple-element.16.refs_10_), channel_id=1, source_target_pairs={{0,8},{2,10},{4,12},{6,14},{8,0},{10,2},{12,4},{14,6},{1,9},{3,11}... | collective-permute-start | bytes 835592 | tf_op jit(solution)/shard_map/ppermute | solution.py:318
  17.4 16.2 %collective-permute-start.6 = (bf16[272,512]{1,0:T(8,128)(2,1)}, bf16[272,512]{1,0:T(8,128)(2,1)}, u32[]{:S(2)}, u32[]{:S(2)}) collective-permute-start(bf16[272,512]{1,0:T(8,128)(2,1)} %get-tuple-element.16.refs_10_), channel_id=1, source_target_pairs={{0,4},{2,6},{4,0},{6,2},{8,12},{10,14},{12,8},{14,10},{1,5},{3,7},... | collective-permute-start | bytes 835592 | tf_op jit(solution)/shard_map/ppermute | solution.py:318
  30.4 26.7 %copy-start.4 = (bf16[272,512]{1,0:T(8,128)(2,1)}, bf16[272,512]{1,0:T(8,128)(2,1)S(1)}, u32[]{:S(2)}) copy-start(bf16[272,512]{1,0:T(8,128)(2,1)S(1)} %collective-permute-done.8.refs_14_) | copy-start | bytes 835588
  30.4 32.5 %copy-start.16 = (s32[8]{0:T(128)S(1)}, s32[8]{0:T(128)}, u32[]{:S(2)}) copy-start(s32[8]{0:T(128)} %param.13) | copy-start | bytes 100
  30.4 15.1 %collective-permute-start.9 = (bf16[272,512]{1,0:T(8,128)(2,1)}, bf16[272,512]{1,0:T(8,128)(2,1)}, u32[]{:S(2)}, u32[]{:S(2)}) collective-permute-start(bf16[272,512]{1,0:T(8,128)(2,1)} %get-tuple-element.17.refs_11_), channel_id=1, source_target_pairs={{0,8},{2,10},{4,12},{6,14},{8,0},{10,2},{12,4},{14,6},{1,9},{3,11}... | collective-permute-start | bytes 835592 | tf_op jit(solution)/shard_map/ppermute | solution.py:318
  33.7 23.5 %collective-permute-start.7 = (bf16[272,512]{1,0:T(8,128)(2,1)S(1)}, bf16[272,512]{1,0:T(8,128)(2,1)S(1)}, u32[]{:S(2)}, u32[]{:S(2)}) collective-permute-start(bf16[272,512]{1,0:T(8,128)(2,1)S(1)} %copy-done.3), channel_id=1, source_target_pairs={{0,4},{2,6},{4,0},{6,2},{8,12},{10,14},{12,8},{14,10},{1,5},{3,7},... | collective-permute-start | bytes 835592 | tf_op jit(solution)/shard_map/ppermute | solution.py:318
  45.6 13.4 %collective-permute-start.14 = (bf16[272,512]{1,0:T(8,128)(2,1)S(1)}, bf16[272,512]{1,0:T(8,128)(2,1)S(1)}, u32[]{:S(2)}, u32[]{:S(2)}) collective-permute-start(bf16[272,512]{1,0:T(8,128)(2,1)S(1)} %collective-permute-done.8.refs_14_), channel_id=1, source_target_pairs={{0,16},{16,0},{1,17},{17,1},{2,18},{18,2},{3,19},{19,3},{4,20},{20... | collective-permute-start | bytes 835592 | tf_op jit(solution)/shard_map/ppermute | solution.py:321
  46.8 45.9 %copy-start = (bf16[128,4096]{1,0:T(8,128)(2,1)}, bf16[128,4096]{1,0:T(8,128)(2,1)S(1)}, u32[]{:S(2)}) copy-start(bf16[128,4096]{1,0:T(8,128)(2,1)S(1)} %collective-permute-done.1.refs_3_) | copy-start | bytes 3145732
  46.8 13.7 %collective-permute-start.10 = (bf16[272,512]{1,0:T(8,128)(2,1)S(1)}, bf16[272,512]{1,0:T(8,128)(2,1)S(1)}, u32[]{:S(2)}, u32[]{:S(2)}) collective-permute-start(bf16[272,512]{1,0:T(8,128)(2,1)S(1)} %collective-permute-done.8.refs_14_), channel_id=1, source_target_pairs={{0,4},{2,6},{4,0},{6,2},{8,12},{10,14},{12,8},{14,10},{1,5},{3,7},... | collective-permute-start | bytes 835592 | tf_op jit(solution)/shard_map/ppermute | solution.py:318
  53.5 39.2 %copy-start.1 = (bf16[128,4096]{1,0:T(8,128)(2,1)}, bf16[128,4096]{1,0:T(8,128)(2,1)S(1)}, u32[]{:S(2)}) copy-start(bf16[128,4096]{1,0:T(8,128)(2,1)S(1)} %collective-permute-done.2.refs_4_) | copy-start | bytes 3145732
  53.5 38.0 %collective-permute-start.3 = (bf16[128,4096]{1,0:T(8,128)(2,1)S(1)}, bf16[128,4096]{1,0:T(8,128)(2,1)S(1)}, u32[]{:S(2)}, u32[]{:S(2)}) collective-permute-start(bf16[128,4096]{1,0:T(8,128)(2,1)S(1)} %collective-permute-done.1.refs_3_), channel_id=1, source_target_pairs={{0,1},{1,0},{2,3},{3,2},{4,5},{5,4},{6,7},{7,6},{8,9},{9,8},{10,11... | collective-permute-start | bytes 3145736 | tf_op jit(solution)/shard_map/ppermute | solution.py:324
  53.5 38.0 %collective-permute-start.4 = (bf16[128,4096]{1,0:T(8,128)(2,1)S(1)}, bf16[128,4096]{1,0:T(8,128)(2,1)}, u32[]{:S(2)}, u32[]{:S(2)}) collective-permute-start(bf16[128,4096]{1,0:T(8,128)(2,1)S(1)} %collective-permute-done.2.refs_4_), channel_id=1, source_target_pairs={{0,1},{1,0},{2,3},{3,2},{4,5},{5,4},{6,7},{7,6},{8,9},{9,8},{10,11... | collective-permute-start | bytes 3145736 | tf_op jit(solution)/shard_map/ppermute | solution.py:324
  57.2 35.6 %copy-start.5 = (bf16[272,512]{1,0:T(8,128)(2,1)}, bf16[272,512]{1,0:T(8,128)(2,1)S(1)}, u32[]{:S(2)}) copy-start(bf16[272,512]{1,0:T(8,128)(2,1)S(1)} %collective-permute-done.7.refs_13_) | copy-start | bytes 835588
  57.2 4.1 %collective-permute-start.5 = (f32[2,512]{1,0:T(2,128)S(1)}, f32[2,512]{1,0:T(2,128)S(1)}, u32[]{:S(2)}, u32[]{:S(2)}) collective-permute-start(f32[2,512]{1,0:T(2,128)S(1)} %stack.30), channel_id=1, source_target_pairs={{0,2},{2,0},{4,6},{6,4},{8,10},{10,8},{12,14},{14,12},{1,3},{3,1},... | collective-permute-start | bytes 12296 | tf_op jit(solution)/shard_map/ppermute | solution.py:315
  59.0 1.5 %copy-start.6 = (bf16[272,512]{1,0:T(8,128)(2,1)}, bf16[272,512]{1,0:T(8,128)(2,1)S(1)}, u32[]{:S(2)}) copy-start(bf16[272,512]{1,0:T(8,128)(2,1)S(1)} %collective-permute-done.14.refs_20_) | copy-start | bytes 835588
  59.0 9.9 %collective-permute-start.12 = (bf16[272,512]{1,0:T(8,128)(2,1)}, bf16[272,512]{1,0:T(8,128)(2,1)}, u32[]{:S(2)}, u32[]{:S(2)}) collective-permute-start(bf16[272,512]{1,0:T(8,128)(2,1)} %collective-permute-done.6.refs_12_), channel_id=1, source_target_pairs={{0,16},{16,0},{1,17},{17,1},{2,18},{18,2},{3,19},{19,3},{4,20},{20... | collective-permute-start | bytes 835592 | tf_op jit(solution)/shard_map/ppermute | solution.py:321
  60.5 0.7 copy-start.7
  60.5 14.3 %collective-permute-start.15 = (bf16[272,512]{1,0:T(8,128)(2,1)}, bf16[272,512]{1,0:T(8,128)(2,1)}, u32[]{:S(2)}, u32[]{:S(2)}) collective-permute-start(bf16[272,512]{1,0:T(8,128)(2,1)} %collective-permute-done.9.refs_15_), channel_id=1, source_target_pairs={{0,16},{16,0},{1,17},{17,1},{2,18},{18,2},{3,19},{19,3},{4,20},{20... | collective-permute-start | bytes 835592 | tf_op jit(solution)/shard_map/ppermute | solution.py:321
  61.3 15.1 %collective-permute-start.11 = (bf16[272,512]{1,0:T(8,128)(2,1)}, bf16[272,512]{1,0:T(8,128)(2,1)}, u32[]{:S(2)}, u32[]{:S(2)}) collective-permute-start(bf16[272,512]{1,0:T(8,128)(2,1)} %collective-permute-done.9.refs_15_), channel_id=1, source_target_pairs={{0,4},{2,6},{4,0},{6,2},{8,12},{10,14},{12,8},{14,10},{1,5},{3,7},... | collective-permute-start | bytes 835592 | tf_op jit(solution)/shard_map/ppermute | solution.py:318
  68.9 11.9 %collective-permute-start.13 = (bf16[272,512]{1,0:T(8,128)(2,1)S(1)}, bf16[272,512]{1,0:T(8,128)(2,1)}, u32[]{:S(2)}, u32[]{:S(2)}) collective-permute-start(bf16[272,512]{1,0:T(8,128)(2,1)S(1)} %collective-permute-done.7.refs_13_), channel_id=1, source_target_pairs={{0,16},{16,0},{1,17},{17,1},{2,18},{18,2},{3,19},{19,3},{4,20},{20... | collective-permute-start | bytes 835592 | tf_op jit(solution)/shard_map/ppermute | solution.py:321
  74.9 11.9 %collective-permute-start.16 = (bf16[272,512]{1,0:T(8,128)(2,1)}, bf16[272,512]{1,0:T(8,128)(2,1)}, u32[]{:S(2)}, u32[]{:S(2)}) collective-permute-start(bf16[272,512]{1,0:T(8,128)(2,1)} %copy-done.7), channel_id=1, source_target_pairs={{0,16},{16,0},{1,17},{17,1},{2,18},{18,2},{3,19},{19,3},{4,20},{20... | collective-permute-start | bytes 835592 | tf_op jit(solution)/shard_map/ppermute | solution.py:321
  76.4 15.2 %collective-permute-start.17 = (bf16[272,512]{1,0:T(8,128)(2,1)}, bf16[272,512]{1,0:T(8,128)(2,1)}, u32[]{:S(2)}, u32[]{:S(2)}) collective-permute-start(bf16[272,512]{1,0:T(8,128)(2,1)} %collective-permute-done.11.refs_17_), channel_id=1, source_target_pairs={{0,16},{16,0},{1,17},{17,1},{2,18},{18,2},{3,19},{19,3},{4,20},{20... | collective-permute-start | bytes 835592 | tf_op jit(solution)/shard_map/ppermute | solution.py:321
  91.6 1.2 copy-start.2
  105.8 21.3 %collective-permute-start.18 = (bf16[4,2,128,128]{3,2,1,0:T(8,128)(2,1)}, bf16[4,2,128,128]{3,2,1,0:T(8,128)(2,1)S(1)}, u32[]{:S(2)}, u32[]{:S(2)}) collective-permute-start(bf16[4,2,128,128]{3,2,1,0:T(8,128)(2,1)} %get-tuple-element.19), channel_id=1, source_target_pairs={{0,2},{2,0},{4,6},{6,4},{8,10},{10,8},{12,14},{14,12},{1,3},{3,1},... | collective-permute-start | bytes 786440 | tf_op jit(solution)/shard_map/ppermute | solution.py:315
  106.2 12.6 %collective-permute-start.22 = (bf16[4,2,128,128]{3,2,1,0:T(8,128)(2,1)}, bf16[4,2,128,128]{3,2,1,0:T(8,128)(2,1)S(1)}, u32[]{:S(2)}, u32[]{:S(2)}) collective-permute-start(bf16[4,2,128,128]{3,2,1,0:T(8,128)(2,1)} %get-tuple-element.25), channel_id=1, source_target_pairs={{0,2},{2,0},{4,6},{6,4},{8,10},{10,8},{12,14},{14,12},{1,3},{3,1},... | collective-permute-start | bytes 786440 | tf_op jit(solution)/shard_map/ppermute | solution.py:315
  118.8 0.7 copy-start.9
  121.4 12.8 %collective-permute-start.23 = (bf16[256,128]{1,0:T(8,128)(2,1)}, bf16[256,128]{1,0:T(8,128)(2,1)S(1)}, u32[]{:S(2)}, u32[]{:S(2)}) collective-permute-start(bf16[256,128]{1,0:T(8,128)(2,1)} %get-tuple-element.27), channel_id=1, source_target_pairs={{0,4},{2,6},{4,0},{6,2},{8,12},{10,14},{12,8},{14,10},{1,5},{3,7},... | collective-permute-start | bytes 196616 | tf_op jit(solution)/shard_map/ppermute | solution.py:318
  124.3 10.2 %collective-permute-start.24 = (bf16[256,128]{1,0:T(8,128)(2,1)}, bf16[256,128]{1,0:T(8,128)(2,1)S(1)}, u32[]{:S(2)}, u32[]{:S(2)}) collective-permute-start(bf16[256,128]{1,0:T(8,128)(2,1)} %get-tuple-element.28), channel_id=1, source_target_pairs={{0,8},{2,10},{4,12},{6,14},{8,0},{10,2},{12,4},{14,6},{1,9},{3,11}... | collective-permute-start | bytes 196616 | tf_op jit(solution)/shard_map/ppermute | solution.py:318
  126.9 7.6 %collective-permute-start.25 = (bf16[256,128]{1,0:T(8,128)(2,1)}, bf16[256,128]{1,0:T(8,128)(2,1)S(1)}, u32[]{:S(2)}, u32[]{:S(2)}) collective-permute-start(bf16[256,128]{1,0:T(8,128)(2,1)} %get-tuple-element.29), channel_id=1, source_target_pairs={{0,12},{2,14},{4,8},{6,10},{8,4},{10,6},{12,0},{14,2},{1,13},{3,15... | collective-permute-start | bytes 196616 | tf_op jit(solution)/shard_map/ppermute | solution.py:318
  127.1 0.7 copy-start.8
  130.0 6.7 %collective-permute-start.19 = (bf16[256,128]{1,0:T(8,128)(2,1)}, bf16[256,128]{1,0:T(8,128)(2,1)S(1)}, u32[]{:S(2)}, u32[]{:S(2)}) collective-permute-start(bf16[256,128]{1,0:T(8,128)(2,1)} %get-tuple-element.21), channel_id=1, source_target_pairs={{0,4},{2,6},{4,0},{6,2},{8,12},{10,14},{12,8},{14,10},{1,5},{3,7},... | collective-permute-start | bytes 196616 | tf_op jit(solution)/shard_map/ppermute | solution.py:318
  130.7 7.1 %collective-permute-start.20 = (bf16[256,128]{1,0:T(8,128)(2,1)}, bf16[256,128]{1,0:T(8,128)(2,1)S(1)}, u32[]{:S(2)}, u32[]{:S(2)}) collective-permute-start(bf16[256,128]{1,0:T(8,128)(2,1)} %get-tuple-element.22), channel_id=1, source_target_pairs={{0,8},{2,10},{4,12},{6,14},{8,0},{10,2},{12,4},{14,6},{1,9},{3,11}... | collective-permute-start | bytes 196616 | tf_op jit(solution)/shard_map/ppermute | solution.py:318
  134.2 0.6 copy-start.10
  134.2 6.3 %collective-permute-start.21 = (bf16[256,128]{1,0:T(8,128)(2,1)}, bf16[256,128]{1,0:T(8,128)(2,1)S(1)}, u32[]{:S(2)}, u32[]{:S(2)}) collective-permute-start(bf16[256,128]{1,0:T(8,128)(2,1)} %get-tuple-element.23), channel_id=1, source_target_pairs={{0,12},{2,14},{4,8},{6,10},{8,4},{10,6},{12,0},{14,2},{1,13},{3,15... | collective-permute-start | bytes 196616 | tf_op jit(solution)/shard_map/ppermute | solution.py:318
  134.4 0.6 copy-start.11
  134.4 0.6 copy-start.12
  136.7 3.7 %copy-start.13 = (bf16[256,128]{1,0:T(8,128)(2,1)}, bf16[256,128]{1,0:T(8,128)(2,1)S(1)}, u32[]{:S(2)}) copy-start(bf16[256,128]{1,0:T(8,128)(2,1)S(1)} %collective-permute-done.19.refs_1_) | copy-start | bytes 196612
  137.8 2.7 %copy-start.14 = (bf16[256,128]{1,0:T(8,128)(2,1)}, bf16[256,128]{1,0:T(8,128)(2,1)S(1)}, u32[]{:S(2)}) copy-start(bf16[256,128]{1,0:T(8,128)(2,1)S(1)} %collective-permute-done.20.refs_2_) | copy-start | bytes 196612
  140.5 0.6 copy-start.15

commit v2 on v1

v2 whole, which is shorter than its diff:
```python
import functools
import math

import jax
import jax.numpy as jnp
from jax import lax
from jax.experimental import pallas as pl
from jax.experimental.pallas import tpu as pltpu
from jax.sharding import PartitionSpec as P

HD = 128
GAIN_ROWS = 16
VMEM_LIMIT = 58 * 2**20
SMALL_VMEM_LIMIT = 8 * 2**20


def rotary_table(position, size_head):
    half_size = size_head // 2
    frequency = jnp.power(
        jnp.float32(500000.0), -2.0 * jnp.arange(half_size, dtype=jnp.float32) / size_head
    )
    angle = jnp.mod(position.astype(jnp.float32)[:, None] * frequency[None, :], 2.0 * math.pi)
    return jnp.cos(angle), jnp.sin(angle)


def rotate(unrotated, position):
    half_size = unrotated.shape[-1] // 2
    cosine, sine = rotary_table(position, unrotated.shape[-1])
    cosine, sine = cosine[:, None, :], sine[:, None, :]
    values = unrotated.astype(jnp.float32)
    first = values[..., :half_size]
    second = values[..., half_size:]
    return jnp.concatenate(
        [first * cosine - second * sine, second * cosine + first * sine], axis=-1
    ).astype(jnp.bfloat16)


def normalize(values, squares_total, gain, feature_count):
    scale = lax.rsqrt(squares_total / feature_count + 1e-05)
    return (values.astype(jnp.float32) * scale[:, None] * gain.astype(jnp.float32)[None, :]).astype(
        jnp.bfloat16
    )


def general_shards(hidden, gain_table, layer_id, w_key, w_value, offsets, owner_map):
    tok_count = lax.axis_size("tok")
    col_count = lax.axis_size("col")
    gain_piece = lax.dynamic_index_in_dim(gain_table, layer_id[0], 0, keepdims=False)
    gain_full = lax.all_gather(gain_piece, "tok", axis=0, tiled=True)
    feature_count = gain_full.shape[0]
    block_rows = hidden.shape[0] * col_count
    tok_rows = lax.all_gather(hidden, "col", axis=0, tiled=True)
    wide = tok_rows.astype(jnp.float32)
    normed = normalize(tok_rows, jnp.sum(wide * wide, axis=1), gain_full, feature_count)
    key_raw, value_new = (
        jnp.dot(
            normed,
            lax.all_gather(weight, "tok", axis=0, tiled=True),
            preferred_element_type=jnp.float32,
        ).astype(jnp.bfloat16)
        for weight in (w_key, w_value)
    )
    heads_here = key_raw.shape[1] // HD
    classes = tok_count // heads_here
    page = block_rows // classes
    group_ids = jnp.arange(tok_count, dtype=jnp.int32)
    inverse = jnp.zeros((tok_count,), jnp.int32).at[owner_map].set(group_ids)

    def arrange_pages(values):
        grouped = (
            values.reshape(classes, page, heads_here, HD)
            .transpose(2, 0, 1, 3)
            .reshape(tok_count, page, HD)
        )
        return jnp.take(grouped, inverse, axis=0).reshape(tok_count * page, HD)

    position = offsets[0] + jnp.arange(block_rows, dtype=jnp.int32)
    key_new = rotate(key_raw.reshape(block_rows, heads_here, HD), position).reshape(block_rows, -1)
    key_out, value_out = (
        lax.all_to_all(arrange_pages(values), "tok", split_axis=0, concat_axis=0, tiled=True)
        for values in (key_new, value_new)
    )
    return (key_out.reshape(1, -1, HD), value_out.reshape(1, -1, HD))


def run_copies(pairs, sems):
    copies = [
        pltpu.make_async_copy(source, target, sems.at[i])
        for i, (source, target) in enumerate(pairs)
    ]
    for copy in copies:
        copy.start()
    return copies


def wait_all(copies):
    for copy in copies:
        copy.wait()


SMEM = pl.BlockSpec(memory_space=pltpu.SMEM)
VMEM = pl.BlockSpec(memory_space=pltpu.VMEM)
HBM = pl.BlockSpec(memory_space=pltpu.HBM)


def half_kernel(shard, parity_ref, hidden_ref, *refs):
    half_refs, sems = refs[:-1], refs[-1]
    pairs = []
    first = 0
    for half_ref in half_refs:
        rows = half_ref.shape[0]
        for i in range(half_ref.shape[1] // shard):
            lanes = pl.ds(pl.multiple_of((2 * i + parity_ref[0]) * shard, shard), shard)
            pairs.append(
                (hidden_ref.at[pl.ds(first, rows), lanes], half_ref.at[:, pl.ds(i * shard, shard)])
            )
        first += rows
    wait_all(run_copies(pairs, sems))


def feature_half(hidden, parity, shard, chunks):
    count = hidden.shape[1] // shard // 2
    return pl.pallas_call(
        functools.partial(half_kernel, shard),
        in_specs=[SMEM, HBM],
        out_specs=[VMEM for _ in chunks],
        out_shape=[jax.ShapeDtypeStruct((rows, count * shard), hidden.dtype) for rows in chunks],
        scratch_shapes=[pltpu.SemaphoreType.DMA((count * len(chunks),))],
    )(parity, hidden)


def pack_kernel(scalars_ref, layer_ref, key_ref, value_ref, gain_ref, *refs):
    *piece_refs, table, sems = refs
    rows = piece_refs[0].shape[0] - GAIN_ROWS
    columns = key_ref.shape[1]
    width = 2 * columns
    layer = layer_ref[0]
    block = pl.multiple_of(layer // GAIN_ROWS * GAIN_ROWS, GAIN_ROWS)
    pairs = [(gain_ref.at[pl.ds(block, GAIN_ROWS), :], table)]
    for p, piece_ref in enumerate(piece_refs):
        first = (scalars_ref[0] * len(piece_refs) + p) * rows
        picked = pl.ds(pl.multiple_of(first, rows), rows)
        for k, weight_ref in enumerate((key_ref, value_ref)):
            pairs.append(
                (
                    weight_ref.at[picked, :],
                    piece_ref.at[pl.ds(0, rows), pl.ds(k * columns, columns)],
                )
            )
    copies = run_copies(pairs, sems)
    copies[0].wait()
    found = table[...].astype(jnp.float32)
    pick = lax.broadcasted_iota(jnp.int32, found.shape, 0) == layer % GAIN_ROWS
    gain = jnp.sum(jnp.where(pick, found, 0.0), axis=0, keepdims=True)
    for p, piece_ref in enumerate(piece_refs):
        piece_ref[rows:, :] = jnp.broadcast_to(
            gain[:, p * width : (p + 1) * width], (GAIN_ROWS, width)
        ).astype(piece_ref.dtype)
    wait_all(copies[1:])


def pack_weights(scalars, layer_id, w_key, w_value, gain_table, pieces):
    shard, columns = w_key.shape
    rows = shard // 2 // pieces
    piece = jax.ShapeDtypeStruct((rows + GAIN_ROWS, 2 * columns), w_key.dtype)
    return pl.pallas_call(
        pack_kernel,
        in_specs=[SMEM, SMEM, HBM, HBM, HBM],
        out_specs=[VMEM] * pieces,
        out_shape=[piece] * pieces,
        scratch_shapes=[
            pltpu.VMEM((GAIN_ROWS, gain_table.shape[1]), gain_table.dtype),
            pltpu.SemaphoreType.DMA((1 + 2 * pieces,)),
        ],
    )(scalars, layer_id, w_key, w_value, gain_table)


def row_pairs(scalars_ref, source_ref, whole, shard, raw_ref):
    if not whole:
        return [(source_ref, raw_ref)]
    x = scalars_ref[1]
    pairs = []
    for i in range(raw_ref.shape[1] // shard):
        lanes = pl.ds(pl.multiple_of((2 * i + x) * shard, shard), shard)
        pairs.append((source_ref.at[:, lanes], raw_ref.at[:, pl.ds(i * shard, shard)]))
    return pairs


def multiply_kernel(shard, line, pieces, *refs):
    refs = list(refs)
    scalars_ref = refs.pop(0)
    sources = [[refs.pop(0) for _ in range(2 if i > 1 else 1)] for i in range(4)]
    key_ref, value_ref = refs.pop(0), refs.pop(0)
    mine = [[refs.pop(0) for _ in range(pieces)] for _ in range(line)]
    theirs = [None] + [[refs.pop(0) for _ in range(pieces)] for _ in range(line - 1)]
    scale_ref = refs.pop(0)
    key_keep, key_send, value_keep, value_send = refs[:4]
    weights, gains, parts, raw, sems = refs[4:]
    y, x, z, c = (scalars_ref[i] for i in range(4))
    half = shard // 2
    rows = half // pieces
    columns = key_ref.shape[1]
    width = 2 * columns
    pairs = []
    for d in range(line):
        for p in range(pieces):
            pairs.append((mine[d][p].at[pl.ds(rows, GAIN_ROWS), :], parts.at[d * pieces + p]))
        first = jnp.bitwise_xor(z, d) * shard
        if d == 0:
            for i, weight_ref in enumerate((key_ref, value_ref)):
                target = weights.at[
                    pl.ds(pl.multiple_of(first, shard), shard), pl.ds(i * columns, columns)
                ]
                pairs.append((weight_ref, target))
            continue
        for blocks, side in ((mine[d], y), (theirs[d], 1 - y)):
            for p, piece in enumerate(blocks):
                start = pl.multiple_of(first + side * half + p * rows, rows)
                pairs.append((piece.at[pl.ds(0, rows), :], weights.at[pl.ds(start, rows), :]))
    ends = [len(pairs)]
    for i, source in enumerate(sources):
        first = 0
        for chunk in source:
            target = raw.at[i, pl.ds(first, chunk.shape[0]), :]
            pairs += row_pairs(scalars_ref, chunk, i < 2, shard, target)
            first += chunk.shape[0]
        ends.append(len(pairs))
    copies = run_copies(pairs, sems)
    wait_all(copies[: ends[0]])
    for d in range(line):
        first = jnp.bitwise_xor(z, d) * shard
        for p in range(pieces):
            lanes = pl.ds(pl.multiple_of(first + p * width, width), width)
            gains[:, lanes] = parts[d * pieces + p]
    page = scale_ref.shape[1] // 2
    for i in range(4):
        if i % 2 == 0:
            wait_all(copies[ends[i] : ends[i + 2]])
            both = raw[i : i + 2].reshape(-1, raw.shape[2])
            products = jnp.dot(
                both * gains[0:1, :], weights[...], preferred_element_type=jnp.float32
            )
        product = products[(i % 2) * 2 * page : (i % 2 + 1) * 2 * page, :]
        source_x = jnp.bitwise_xor(x, i // 2)
        core = jnp.bitwise_xor(c, i % 2)
        for part in range(2):
            page_rows = slice(part * page, (part + 1) * page)
            scale = scale_ref[i, page_rows, :]
            for j in range(columns // HD):
                group = j * 4 + core * 2 + part
                owner = scalars_ref[4 + group]
                owner_z, owner_x = owner // 2, owner % 2
                results = [
                    product[page_rows, k * columns + j * HD : k * columns + (j + 1) * HD] * scale
                    for k in range(2)
                ]

                @pl.when(owner_x == x)
                def _():
                    key_keep[owner_z, source_x] = results[0]
                    value_keep[owner_z, source_x] = results[1]

                @pl.when(owner_x != x)
                def _():
                    key_send[owner_z, source_x] = results[0].astype(jnp.bfloat16)
                    value_send[owner_z, source_x] = results[1].astype(jnp.bfloat16)


def multiply(scalars, sources, w_key, w_value, mine, theirs, scale):
    shard, columns = w_key.shape
    line = len(mine)
    device_rows = scale.shape[1]
    pieces = len(mine[0])
    operands = [
        *[chunk for source in sources for chunk in source], w_key, w_value,
        *[piece for blocks in mine for piece in blocks],
        *[piece for blocks in theirs for piece in blocks],
    ]
    keep = jax.ShapeDtypeStruct((line, 2, device_rows // 2, HD), jnp.float32)
    send = jax.ShapeDtypeStruct((line, 2, device_rows // 2, HD), jnp.bfloat16)
    copies = line * pieces + 2 + 2 * (line - 1) * pieces + 2 * line + 4
    return pl.pallas_call(
        functools.partial(multiply_kernel, shard, line, pieces),
        in_specs=[SMEM] + [HBM] * len(operands) + [VMEM],
        out_specs=[VMEM] * 4,
        out_shape=[keep, send, keep, send],
        scratch_shapes=[
            pltpu.VMEM((line * shard, 2 * columns), jnp.bfloat16),
            pltpu.VMEM((GAIN_ROWS, line * shard), jnp.bfloat16),
            pltpu.VMEM((line * pieces, GAIN_ROWS, 2 * columns), jnp.bfloat16),
            pltpu.VMEM((4, device_rows, line * shard), jnp.bfloat16),
            pltpu.SemaphoreType.DMA((copies,)),
        ],
        compiler_params=pltpu.CompilerParams(vmem_limit_bytes=VMEM_LIMIT),
    )(scalars, *operands, scale)


def finish_key_kernel(scalars_ref, keep_ref, came_ref, cos_ref, sin_ref, *out_refs):
    x, z = scalars_ref[1], scalars_ref[2]
    page = keep_ref.shape[2]
    for d, out_ref in enumerate(out_refs):
        owner_z = jnp.bitwise_xor(z, d)
        owner = owner_z * 2 + x
        group = jnp.int32(0)
        for g in range(2 * len(out_refs)):
            group = jnp.where(scalars_ref[4 + g] == owner, g, group)
        page_class = group % 4
        for s in range(2):
            raw = keep_ref[owner_z, s] + came_ref[owner_z, s].astype(jnp.float32)
            raw = raw.astype(jnp.bfloat16).astype(jnp.float32)
            turned = pltpu.roll(raw, HD // 2, 1)
            rotated = raw * cos_ref[s * 4 + page_class] + turned * sin_ref[s * 4 + page_class]
            out_ref[s * page : (s + 1) * page, :] = rotated.astype(jnp.bfloat16)


def finish_value_kernel(scalars_ref, keep_ref, came_ref, *out_refs):
    z = scalars_ref[2]
    page = keep_ref.shape[2]
    for d, out_ref in enumerate(out_refs):
        owner_z = jnp.bitwise_xor(z, d)
        for s in range(2):
            raw = keep_ref[owner_z, s] + came_ref[owner_z, s].astype(jnp.float32)
            out_ref[s * page : (s + 1) * page, :] = raw.astype(jnp.bfloat16)


def finish(kernel, scalars, keep, came, *tables):
    vmem = pl.BlockSpec(memory_space=pltpu.VMEM)
    line, _, page, _ = keep.shape
    return pl.pallas_call(
        kernel,
        in_specs=[pl.BlockSpec(memory_space=pltpu.SMEM)] + [vmem] * (2 + len(tables)),
        out_specs=[vmem] * line,
        out_shape=[jax.ShapeDtypeStruct((2 * page, HD), jnp.bfloat16)] * line,
        compiler_params=pltpu.CompilerParams(vmem_limit_bytes=SMALL_VMEM_LIMIT),
    )(scalars, keep, came, *tables)


def place_kernel(scalars_ref, *refs):
    out_ref = refs[-1]
    z = scalars_ref[2]
    rows = refs[0].shape[0]
    for d, block_ref in enumerate(refs[:-1]):
        start = pl.multiple_of(jnp.bitwise_xor(z, d) * rows, rows)
        out_ref[pl.ds(start, rows), :] = block_ref[...]


def place(scalars, blocks):
    vmem = pl.BlockSpec(memory_space=pltpu.VMEM)
    return pl.pallas_call(
        place_kernel,
        in_specs=[pl.BlockSpec(memory_space=pltpu.SMEM)] + [vmem] * len(blocks),
        out_specs=vmem,
        out_shape=jax.ShapeDtypeStruct((len(blocks) * blocks[0].shape[0], HD), jnp.bfloat16),
    )(scalars, *blocks)


def after(value, *others):
    return lax.optimization_barrier((value, *others))[0]


def paired_shards(hidden, gain_table, layer_id, w_key, w_value, offsets, owner_map):
    tok_count = lax.axis_size("tok")
    line = tok_count // 2
    pieces = 2
    y, tok, c = lax.axis_index("group"), lax.axis_index("tok"), lax.axis_index("col")
    x, z = tok % 2, tok // 2
    shard = w_key.shape[0]
    device_rows = hidden.shape[0]
    page = device_rows // 2
    chunks = (page, device_rows - page)
    scalars = jnp.concatenate([jnp.stack([y, x, z, c]).astype(jnp.int32), owner_map])

    def over_x(values):
        return lax.ppermute(values, "tok", [(t, t ^ 1) for t in range(tok_count)])

    def over_z(values, distance):
        return lax.ppermute(values, "tok", [(t, t ^ (2 * distance)) for t in range(tok_count)])

    def over_y(values):
        return lax.ppermute(values, "group", [(0, 1), (1, 0)])

    def over_c(values):
        return lax.ppermute(values, "col", [(0, 1), (1, 0)])

    def squares(values):
        wide = values.astype(jnp.float32)
        return jnp.sum(wide * wide, axis=1)

    away = jnp.reshape(1 - x, (1,)).astype(jnp.int32)
    packed = pack_weights(scalars, layer_id, w_key, w_value, gain_table, pieces)
    head, tail = feature_half(hidden, away, shard, chunks)
    own_head = over_x(head)
    other = over_c(hidden)
    far = [over_z(piece, 2) for piece in packed]
    near = [over_z(packed[0], 1), over_z(after(packed[1], other), 1)]

    facts = jnp.stack(
        [
            jnp.concatenate([squares(hidden), squares(other)]),
            jnp.broadcast_to(offsets[0].astype(jnp.float32), (2 * device_rows,)),
        ]
    )
    near_y_0 = over_y(near[0])
    corner_0 = over_z(after(far[0], near[0], facts), 1)
    far_y_0 = over_y(after(far[0], near[0]))
    near_y_1 = over_y(after(near[1], far[0]))
    corner_1 = over_z(after(far[1], near[1], near_y_0), 1)
    far_y_1 = over_y(after(far[1], near[1], own_head))
    corner_y_0 = over_y(after(corner_0, near_y_1, far_y_0))
    pair_facts = over_x(facts)
    corner_y_1 = over_y(after(corner_1, far_y_1, pair_facts))
    near_y, far_y = [near_y_0, near_y_1], [far_y_0, far_y_1]
    corner, corner_y = [corner_0, corner_1], [corner_y_0, corner_y_1]
    own_tail = over_x(after(tail, near[0]))
    totals = jnp.concatenate([facts[0], pair_facts[0]])
    scale = lax.rsqrt(totals / hidden.shape[1] + 1e-05).reshape(4, device_rows, 1)
    scale = jnp.broadcast_to(scale, (4, device_rows, HD))
    starts = jnp.stack([facts[1, 0], pair_facts[1, 0]]).astype(jnp.int32)
    starts = jnp.where(x == 0, starts, starts[::-1])
    block = jnp.arange(2 * device_rows, dtype=jnp.int32)
    cosine, sine = rotary_table((starts[:, None] + block[None, :]).reshape(-1), HD)
    cosine = jnp.concatenate([cosine, cosine], axis=1).reshape(8, page, HD)
    sine = jnp.concatenate([-sine, sine], axis=1).reshape(8, page, HD)

    other_head = over_c(after(own_head, *corner_y))
    other_tail = over_c(after(own_tail, *corner_y))

    key_keep, key_send, value_keep, value_send = multiply(
        scalars, [[hidden], [other], [own_head, own_tail], [other_head, other_tail]], w_key, w_value,
        [packed, near, far, corner], [near_y, far_y, corner_y], scale,
    )
    key_came = over_x(key_send)
    value_came = over_x(after(value_send, key_came))
    keys = finish(finish_key_kernel, scalars, key_keep, key_came, cosine, sine)
    values = finish(finish_value_kernel, scalars, value_keep, value_came)
    outs = []
    for blocks in (keys, values):
        blocks = [blocks[0]] + [over_z(blocks[d], d) for d in range(1, line)]
        outs.append(place(scalars, blocks)[None])
    return tuple(outs)


def solution(mesh):
    in_specs = (
        P(("group", "tok", "col"), None),
        P(None, "tok"),
        P("group"),
        P("tok", "col"),
        P("tok", "col"),
        P(("group", "tok")),
        P("group"),
    )
    out_specs = (P("col", ("group", "tok"), None), P("col", ("group", "tok"), None))
    paired = mesh.shape["group"] == 2 and mesh.shape["tok"] == 8 and mesh.shape["col"] == 2
    shards = paired_shards if paired else general_shards
    return jax.shard_map(shards, mesh=mesh, in_specs=in_specs, out_specs=out_specs, check_vma=False)
```

time: 143 us -> 119 us (0.83)
  waiting for transfers between devices: 60.1 us -> 46.9 us
  Pallas kernels: 29.9 us -> 21.2 us
  other arithmetic: 11.9 us -> 10.3 us
  starting transfers between devices: 33.5 us -> 32 us
    ppermute x6, waiting for transfers between devices: 22.2 us -> 13 us  [over_y(): return lax.ppermute(values, 'group', [(0, 1), (1, 0)])]
    ppermute x5, waiting for transfers between devices: 15.4 us -> 7 us  [over_x(): return lax.ppermute(values, 'tok', [(t, t ^ 1) for t in range(tok_count)])]
    pallas_call x4 -> x3, Pallas kernels: 22.4 us -> 16.6 us  [the longest x1 11 us: multiply(): pl.pallas_call(functools.partial(multiply_kernel, shard, line, pieces), i...]
    pallas_call x2, Pallas kernels: 4.09 us -> 1.32 us  [finish(): pl.pallas_call(kernel, in_specs=[pl.BlockSpec(memory_space=pltpu.SMEM)] +...]
    ppermute x12, starting transfers between devices: 19 us -> 16.4 us  [over_z(): lax.ppermute(values, 'tok', [(t, t ^ 2 * distance) for t in range(tok_cou...]
    ppermute x12, waiting for transfers between devices: 22.5 us -> 24.7 us  [over_z(): lax.ppermute(values, 'tok', [(t, t ^ 2 * distance) for t in range(tok_cou...]
    ppermute x3, waiting for transfers between devices: 0.01 us -> 2.2 us  [over_c(): return lax.ppermute(values, 'col', [(0, 1), (1, 0)])]
    ppermute x5, starting transfers between devices: 6.43 us -> 7.95 us  [over_x(): return lax.ppermute(values, 'tok', [(t, t ^ 1) for t in range(tok_count)])]
  transfers between devices with their start and end apart: 26 -> 26, of which waited for: 11 -> 14; matrix products, arithmetic and copies ran while one was open for 9% -> 11% of each run, Pallas kernels for 11% -> 7%
where the time goes in v2:
time: 119 us
  waiting for transfers between devices  46.9 us (39%)
  starting transfers between devices  32 us (27%)
  Pallas kernels  21.2 us (18%)
  other arithmetic  10.3 us (9%)
  local copies, waits for them, and re-layouts  5.77 us (5%)
  between operations  2.24 us (2%)
    ppermute x12, waiting for transfers between devices, over_z(): lax.ppermute(values, 'tok', [(t, t ^ 2 * distance) for t in range(tok_cou...  24.7 us
    ppermute x12, starting transfers between devices, over_z(): lax.ppermute(values, 'tok', [(t, t ^ 2 * distance) for t in range(tok_cou...  16.4 us
    ppermute x6, waiting for transfers between devices, over_y(): return lax.ppermute(values, 'group', [(0, 1), (1, 0)])  13 us
    pallas_call x1, Pallas kernels, multiply(): pl.pallas_call(functools.partial(multiply_kernel, shard, line, pieces), i...  11 us
    ppermute x5, starting transfers between devices, over_x(): return lax.ppermute(values, 'tok', [(t, t ^ 1) for t in range(tok_count)])  7.95 us
    ppermute x6, starting transfers between devices, over_y(): return lax.ppermute(values, 'group', [(0, 1), (1, 0)])  7.16 us
    ppermute x5, waiting for transfers between devices, over_x(): return lax.ppermute(values, 'tok', [(t, t ^ 1) for t in range(tok_count)])  7 us
    reduce_sum x2, other arithmetic, squares(): return jnp.sum(wide * wide, axis=1)  6.31 us
  transfers between devices with their start and end apart: 26, of which 14 were waited for; matrix products, arithmetic and copies ran while one was open for 11% of the time, Pallas kernels for 7%

profile of v2, /device:TPU:0, one launch (start us, length us, event | category | flops | bytes accessed | tf_op | source)
XLA Modules:
  0.0 118.5 jit_solution(4325968464342138985)
XLA Ops:
  1.8 1.3 %concatenate.18.scalars_ref.refs_0_ = s32[12]{0:T(128)} concatenate(s32[1]{0:T(128)} %bitcast, s32[1]{0:T(128)} %bitcast.1, s32[1]{0:T(128)} %bitcast.2, s32[1]{0:T(128)} %bitcast.3, s32[8]{0:T(128)} %param.13), dimensions={0} | concatenate | bytes 96 | tf_op jit(solution)/shard_map/concatenate | solution.py:371
  3.1 2.6 %shard_map.87 = (bf16[272,512]{1,0:T(8,128)(2,1)}, bf16[272,512]{1,0:T(8,128)(2,1)}) custom-call(s32[12]{0:T(128)} %concatenate.18.scalars_ref.refs_0_, s32[1]{0:T(128)S(6)} %copy.9.layer_ref, bf16[1024,256]{1,0:T(8,128)(2,1)} %refs_7_.1, bf16[1024,256]{1,0:T(8,128)(2,1)} %refs_8_.1, bf16[80,1024]{1,0:T(8,128)(2,1)} %gain_ref.1), custom_call_target="tpu_custom_call" | custom-call | tf_op jit(solution)/shard_map/pallas_call | solution.py:166
  5.8 2.7 %collective-permute-start.2 = (bf16[272,512]{1,0:T(8,128)(2,1)}, bf16[272,512]{1,0:T(8,128)(2,1)S(1)}, u32[]{:S(2)}, u32[]{:S(2)}) collective-permute-start(bf16[272,512]{1,0:T(8,128)(2,1)} %get-tuple-element.32.refs_9_), channel_id=1, source_target_pairs={{0,4},{2,6},{4,0},{6,2},{8,12},{10,14},{12,8},{14,10},{1,5},{3,7},... | collective-permute-start | bytes 835592 | tf_op jit(solution)/shard_map/ppermute | solution.py:377
  8.5 2.9 %shard_map.86 = (bf16[128,4096]{1,0:T(8,128)(2,1)}, bf16[128,4096]{1,0:T(8,128)(2,1)}) custom-call(s32[1]{0:T(128)} %bitcast.4.parity_ref, bf16[256,8192]{1,0:T(8,128)(2,1)} %refs_1_.1), custom_call_target="tpu_custom_call" | custom-call | tf_op jit(solution)/shard_map/pallas_call | solution.py:123
  11.4 1.6 %collective-permute-start.1 = (bf16[128,4096]{1,0:T(8,128)(2,1)}, bf16[128,4096]{1,0:T(8,128)(2,1)S(1)}, u32[]{:S(2)}, u32[]{:S(2)}) collective-permute-start(bf16[128,4096]{1,0:T(8,128)(2,1)} %get-tuple-element.30), channel_id=1, source_target_pairs={{0,2},{2,0},{4,6},{6,4},{8,10},{10,8},{12,14},{14,12},{1,3},{3,1},... | collective-permute-start | bytes 3145736 | tf_op jit(solution)/shard_map/ppermute | solution.py:374
  13.0 2.6 %collective-permute-start.4 = (bf16[272,512]{1,0:T(8,128)(2,1)S(1)}, bf16[272,512]{1,0:T(8,128)(2,1)S(1)}, u32[]{:S(2)}, u32[]{:S(2)}) collective-permute-start(bf16[272,512]{1,0:T(8,128)(2,1)S(1)} %copy-done.8), channel_id=1, source_target_pairs={{0,8},{2,10},{4,12},{6,14},{8,0},{10,2},{12,4},{14,6},{1,9},{3,11}... | collective-permute-start | bytes 835592 | tf_op jit(solution)/shard_map/ppermute | solution.py:377
  16.0 4.4 %collective-permute-start.3 = (bf16[128,4096]{1,0:T(8,128)(2,1)}, bf16[128,4096]{1,0:T(8,128)(2,1)S(1)}, u32[]{:S(2)}, u32[]{:S(2)}) collective-permute-start(bf16[128,4096]{1,0:T(8,128)(2,1)} %get-tuple-element.33), channel_id=1, source_target_pairs={{0,2},{2,0},{4,6},{6,4},{8,10},{10,8},{12,14},{14,12},{1,3},{3,1},... | collective-permute-start | bytes 3145736 | tf_op jit(solution)/shard_map/ppermute | solution.py:374
  20.4 3.1 %multiply_reduce_fusion.1 = f32[256]{0:T(256)S(1)} fusion(bf16[256,8192]{1,0:T(8,128)(2,1)} %refs_1_.1), kind=kLoop, calls=%fused_computation.1 | loop fusion | flops 6291200 | bytes 4195328 | tf_op jit(solution)/shard_map/reduce_sum | solution.py:387
  24.2 11.2 %collective-permute-done.4.refs_13_ = bf16[272,512]{1,0:T(8,128)(2,1)S(1)} collective-permute-done((bf16[272,512]{1,0:T(8,128)(2,1)S(1)}, bf16[272,512]{1,0:T(8,128)(2,1)S(1)}, u32[]{:S(2)}, u32[]{:S(2)}) %collective-permute-start.4) | collective-permute-done | bytes 278560 | tf_op jit(solution)/shard_map/ppermute | solution.py:377
  35.3 1.5 %collective-permute-start.8 = (bf16[272,512]{1,0:T(8,128)(2,1)S(1)}, bf16[272,512]{1,0:T(8,128)(2,1)S(1)}, u32[]{:S(2)}, u32[]{:S(2)}) collective-permute-start(bf16[272,512]{1,0:T(8,128)(2,1)S(1)} %collective-permute-done.4.refs_13_), channel_id=1, source_target_pairs={{0,16},{16,0},{1,17},{17,1},{2,18},{18,2},{3,19},{19,3},{4,20},{20... | collective-permute-start | bytes 835592 | tf_op jit(solution)/shard_map/ppermute | solution.py:380
  37.4 2.9 %collective-permute-done.10.refs_14_ = bf16[272,512]{1,0:T(8,128)(2,1)S(1)} collective-permute-done((bf16[272,512]{1,0:T(8,128)(2,1)S(1)}, bf16[272,512]{1,0:T(8,128)(2,1)S(1)}, u32[]{:S(2)}, u32[]{:S(2)}) %collective-permute-start.10) | collective-permute-done | bytes 278560 | tf_op jit(solution)/shard_map/ppermute | solution.py:377
  40.3 3.2 %multiply_reduce_fusion = f32[256]{0:T(256)S(1)} fusion(bf16[256,8192]{1,0:T(8,128)(2,1)} %collective-permute-done.refs_2_), kind=kLoop, calls=%fused_computation | loop fusion | flops 6291200 | bytes 4195328 | tf_op jit(solution)/shard_map/reduce_sum | solution.py:387
  43.5 2.0 %collective-permute-start.5 = (bf16[272,512]{1,0:T(8,128)(2,1)S(1)}, bf16[272,512]{1,0:T(8,128)(2,1)S(1)}, u32[]{:S(2)}, u32[]{:S(2)}) collective-permute-start(bf16[272,512]{1,0:T(8,128)(2,1)S(1)} %collective-permute-done.4.refs_13_), channel_id=1, source_target_pairs={{0,4},{2,6},{4,0},{6,2},{8,12},{10,14},{12,8},{14,10},{1,5},{3,7},... | collective-permute-start | bytes 835592 | tf_op jit(solution)/shard_map/ppermute | solution.py:377
  45.5 4.3 %collective-permute-done.6.refs_12_ = bf16[272,512]{1,0:T(8,128)(2,1)S(1)} collective-permute-done((bf16[272,512]{1,0:T(8,128)(2,1)S(1)}, bf16[272,512]{1,0:T(8,128)(2,1)S(1)}, u32[]{:S(2)}, u32[]{:S(2)}) %collective-permute-start.6) | collective-permute-done | bytes 278560 | tf_op jit(solution)/shard_map/ppermute | solution.py:377
  49.9 1.5 %collective-permute-start.7 = (bf16[272,512]{1,0:T(8,128)(2,1)S(1)}, bf16[272,512]{1,0:T(8,128)(2,1)S(1)}, u32[]{:S(2)}, u32[]{:S(2)}) collective-permute-start(bf16[272,512]{1,0:T(8,128)(2,1)S(1)} %collective-permute-done.6.refs_12_), channel_id=1, source_target_pairs={{0,16},{16,0},{1,17},{17,1},{2,18},{18,2},{3,19},{19,3},{4,20},{20... | collective-permute-start | bytes 835592 | tf_op jit(solution)/shard_map/ppermute | solution.py:380
  52.0 3.8 %collective-permute-done.5.refs_15_ = bf16[272,512]{1,0:T(8,128)(2,1)S(1)} collective-permute-done((bf16[272,512]{1,0:T(8,128)(2,1)S(1)}, bf16[272,512]{1,0:T(8,128)(2,1)S(1)}, u32[]{:S(2)}, u32[]{:S(2)}) %collective-permute-start.5) | collective-permute-done | bytes 278560 | tf_op jit(solution)/shard_map/ppermute | solution.py:377
  55.8 0.6 collective-permute-start.14
  56.4 3.0 %collective-permute-done.7.refs_18_ = bf16[272,512]{1,0:T(8,128)(2,1)S(1)} collective-permute-done((bf16[272,512]{1,0:T(8,128)(2,1)S(1)}, bf16[272,512]{1,0:T(8,128)(2,1)S(1)}, u32[]{:S(2)}, u32[]{:S(2)}) %collective-permute-start.7) | collective-permute-done | bytes 278560 | tf_op jit(solution)/shard_map/ppermute | solution.py:380
  59.5 1.5 %collective-permute-start.9 = (bf16[272,512]{1,0:T(8,128)(2,1)S(1)}, bf16[272,512]{1,0:T(8,128)(2,1)S(1)}, u32[]{:S(2)}, u32[]{:S(2)}) collective-permute-start(bf16[272,512]{1,0:T(8,128)(2,1)S(1)} %collective-permute-done.5.refs_15_), channel_id=1, source_target_pairs={{0,16},{16,0},{1,17},{17,1},{2,18},{18,2},{3,19},{19,3},{4,20},{20... | collective-permute-start | bytes 835592 | tf_op jit(solution)/shard_map/ppermute | solution.py:380
  61.0 4.4 %collective-permute-done.13.refs_20_ = bf16[272,512]{1,0:T(8,128)(2,1)S(1)} collective-permute-done((bf16[272,512]{1,0:T(8,128)(2,1)S(1)}, bf16[272,512]{1,0:T(8,128)(2,1)S(1)}, u32[]{:S(2)}, u32[]{:S(2)}) %collective-permute-start.13) | collective-permute-done | bytes 278560 | tf_op jit(solution)/shard_map/ppermute | solution.py:380
  65.4 1.5 %collective-permute-start.15 = (bf16[272,512]{1,0:T(8,128)(2,1)S(1)}, bf16[272,512]{1,0:T(8,128)(2,1)S(1)}, u32[]{:S(2)}, u32[]{:S(2)}) collective-permute-start(bf16[272,512]{1,0:T(8,128)(2,1)S(1)} %collective-permute-done.12.refs_16_), channel_id=1, source_target_pairs={{0,16},{16,0},{1,17},{17,1},{2,18},{18,2},{3,19},{19,3},{4,20},{20... | collective-permute-start | bytes 835592 | tf_op jit(solution)/shard_map/ppermute | solution.py:380
  66.9 2.6 %collective-permute-done.9.refs_21_ = bf16[272,512]{1,0:T(8,128)(2,1)S(1)} collective-permute-done((bf16[272,512]{1,0:T(8,128)(2,1)S(1)}, bf16[272,512]{1,0:T(8,128)(2,1)S(1)}, u32[]{:S(2)}, u32[]{:S(2)}) %collective-permute-start.9) | collective-permute-done | bytes 278560 | tf_op jit(solution)/shard_map/ppermute | solution.py:380
  69.5 3.0 %collective-permute-done.15.refs_22_ = bf16[272,512]{1,0:T(8,128)(2,1)S(1)} collective-permute-done((bf16[272,512]{1,0:T(8,128)(2,1)S(1)}, bf16[272,512]{1,0:T(8,128)(2,1)S(1)}, u32[]{:S(2)}, u32[]{:S(2)}) %collective-permute-start.15) | collective-permute-done | bytes 278560 | tf_op jit(solution)/shard_map/ppermute | solution.py:380
  72.6 0.6 copy-done.21
  73.8 0.7 maximum_convert_fusion
  74.6 0.6 collective-permute-done.16.refs_5_
  75.2 1.6 %collective-permute-done.17.refs_6_ = bf16[128,4096]{1,0:T(8,128)(2,1)} collective-permute-done((bf16[128,4096]{1,0:T(8,128)(2,1)S(1)}, bf16[128,4096]{1,0:T(8,128)(2,1)}, u32[]{:S(2)}, u32[]{:S(2)}) %collective-permute-start.17) | collective-permute-done | bytes 1048608 | tf_op jit(solution)/shard_map/ppermute | solution.py:383
  76.8 1.0 broadcast_in_dim.6.refs_23_
  77.8 11.0 %shard_map.88 = (f32[4,2,128,128]{3,2,1,0:T(8,128)}, bf16[4,2,128,128]{3,2,1,0:T(8,128)(2,1)}, f32[4,2,128,128]{3,2,1,0:T(8,128)}, bf16[4,2,128,128]{3,2,1,0:T(8,128)(2,1)}) custom-call(s32[12]{0:T(128)} %concatenate.18.scalars_ref.refs_0_, bf16[256,8192]{1,0:T(8,128)(2,1)} %refs_1_.1, bf16[256,8192]{1,0:T(8,128)(2,1)} %collective-permute-done.refs_2_, ...), custom_call_target="tpu_custom_call" | custom-call | tf_op jit(solution)/shard_map/pallas_call | solution.py:282
  88.9 0.7 collective-permute-start.18
  89.6 0.7 broadcast_select_fusion
  90.5 7.0 %collective-permute-done.18.came_ref = bf16[4,2,128,128]{3,2,1,0:T(8,128)(2,1)S(1)} collective-permute-done((bf16[4,2,128,128]{3,2,1,0:T(8,128)(2,1)}, bf16[4,2,128,128]{3,2,1,0:T(8,128)(2,1)S(1)}, u32[]{:S(2)}, u32[]{:S(2)}) %collective-permute-start.18) | collective-permute-done | bytes 262176 | tf_op jit(solution)/shard_map/ppermute | solution.py:374
  97.5 0.7 collective-permute-start.22
  98.1 2.2 %fusion.5 = (f32[8,128,64]{2,1,0:T(8,128)S(1)}, f32[8,128,64]{2,1,0:T(8,128)S(1)}, f32[8,128,64]{2,1,0:T(8,128)S(1)}) fusion(f32[64]{0:T(128)S(1)} %multiply_power_fusion, f32[8,128]{1,0:T(8,128)S(1)} %add_convert_fusion), kind=kLoop, calls=%fused_computation.11 | loop fusion | flops 524288 | bytes 790784 | tf_op jit(solution)/shard_map/neg | solution.py:423
  100.7 0.7 shard_map.89
  101.4 0.6 collective-permute-start.19
  102.0 2.5 %collective-permute-start.20 = (bf16[256,128]{1,0:T(8,128)(2,1)S(1)}, bf16[256,128]{1,0:T(8,128)(2,1)S(1)}, u32[]{:S(2)}, u32[]{:S(2)}) collective-permute-start(bf16[256,128]{1,0:T(8,128)(2,1)S(1)} %get-tuple-element.49), channel_id=1, source_target_pairs={{0,8},{2,10},{4,12},{6,14},{8,0},{10,2},{12,4},{14,6},{1,9},{3,11}... | collective-permute-start | bytes 196616 | tf_op jit(solution)/shard_map/ppermute | solution.py:377
  104.5 1.3 %collective-permute-start.21 = (bf16[256,128]{1,0:T(8,128)(2,1)S(1)}, bf16[256,128]{1,0:T(8,128)(2,1)S(1)}, u32[]{:S(2)}, u32[]{:S(2)}) collective-permute-start(bf16[256,128]{1,0:T(8,128)(2,1)S(1)} %get-tuple-element.50), channel_id=1, source_target_pairs={{0,12},{2,14},{4,8},{6,10},{8,4},{10,6},{12,0},{14,2},{1,13},{3,15... | collective-permute-start | bytes 196616 | tf_op jit(solution)/shard_map/ppermute | solution.py:377
  105.9 0.6 shard_map.91
  106.5 0.6 copy-done.3
  107.1 3.0 %collective-permute-start.24 = (bf16[256,128]{1,0:T(8,128)(2,1)S(1)}, bf16[256,128]{1,0:T(8,128)(2,1)S(1)}, u32[]{:S(2)}, u32[]{:S(2)}) collective-permute-start(bf16[256,128]{1,0:T(8,128)(2,1)S(1)} %get-tuple-element.56), channel_id=1, source_target_pairs={{0,8},{2,10},{4,12},{6,14},{8,0},{10,2},{12,4},{14,6},{1,9},{3,11}... | collective-permute-start | bytes 196616 | tf_op jit(solution)/shard_map/ppermute | solution.py:377
  110.2 1.3 %collective-permute-start.25 = (bf16[256,128]{1,0:T(8,128)(2,1)S(1)}, bf16[256,128]{1,0:T(8,128)(2,1)S(1)}, u32[]{:S(2)}, u32[]{:S(2)}) collective-permute-start(bf16[256,128]{1,0:T(8,128)(2,1)S(1)} %get-tuple-element.57), channel_id=1, source_target_pairs={{0,12},{2,14},{4,8},{6,10},{8,4},{10,6},{12,0},{14,2},{1,13},{3,15... | collective-permute-start | bytes 196616 | tf_op jit(solution)/shard_map/ppermute | solution.py:377
  111.5 0.6 copy-done.23
  112.2 1.7 %shard_map.90 = bf16[1024,128]{1,0:T(8,128)(2,1)} custom-call(s32[12]{0:T(128)} %concatenate.18.scalars_ref.refs_0_, bf16[256,128]{1,0:T(8,128)(2,1)} %copy-done.2, bf16[256,128]{1,0:T(8,128)(2,1)} %copy-done.22, bf16[256,128]{1,0:T(8,128)(2,1)} %copy-done.23, bf16[256,128]{1,0:T(8,128)(2,1)} %copy-done.25), custom_call_target="tpu_custom_call" | custom-call | tf_op jit(solution)/shard_map/pallas_call | solution.py:349
  113.8 0.6 collective-permute-done.24.refs_2_
  114.4 1.8 %collective-permute-done.25.refs_3_ = bf16[256,128]{1,0:T(8,128)(2,1)S(1)} collective-permute-done((bf16[256,128]{1,0:T(8,128)(2,1)S(1)}, bf16[256,128]{1,0:T(8,128)(2,1)S(1)}, u32[]{:S(2)}, u32[]{:S(2)}) %collective-permute-start.25) | collective-permute-done | bytes 65568 | tf_op jit(solution)/shard_map/ppermute | solution.py:377
  116.2 0.6 copy-done.27
  116.9 1.7 %shard_map.92 = bf16[1024,128]{1,0:T(8,128)(2,1)} custom-call(s32[12]{0:T(128)} %concatenate.18.scalars_ref.refs_0_, bf16[256,128]{1,0:T(8,128)(2,1)} %copy-done.3, bf16[256,128]{1,0:T(8,128)(2,1)} %copy-done.24, bf16[256,128]{1,0:T(8,128)(2,1)} %copy-done.26, bf16[256,128]{1,0:T(8,128)(2,1)} %copy-done.27), custom_call_target="tpu_custom_call" | custom-call | tf_op jit(solution)/shard_map/pallas_call | solution.py:349
  (88 shorter events, 3.5 us)
Async XLA Ops:
  0.6 36.2 %collective-permute-start = (bf16[256,8192]{1,0:T(8,128)(2,1)}, bf16[256,8192]{1,0:T(8,128)(2,1)}, u32[]{:S(2)}, u32[]{:S(2)}) collective-permute-start(bf16[256,8192]{1,0:T(8,128)(2,1)} %refs_1_.1), channel_id=1, source_target_pairs={{0,1},{1,0},{2,3},{3,2},{4,5},{5,4},{6,7},{7,6},{8,9},{9,8},{10,11... | collective-permute-start | bytes 12582920 | tf_op jit(solution)/shard_map/ppermute | solution.py:383
  5.8 7.2 %copy-start.8 = (bf16[272,512]{1,0:T(8,128)(2,1)S(1)}, bf16[272,512]{1,0:T(8,128)(2,1)}, u32[]{:S(2)}) copy-start(bf16[272,512]{1,0:T(8,128)(2,1)} %get-tuple-element.32.refs_9_) | copy-start | bytes 835588
  5.8 9.8 %copy-start.9 = (bf16[272,512]{1,0:T(8,128)(2,1)S(1)}, bf16[272,512]{1,0:T(8,128)(2,1)}, u32[]{:S(2)}) copy-start(bf16[272,512]{1,0:T(8,128)(2,1)} %get-tuple-element.36.refs_10_) | copy-start | bytes 835588
  5.8 10.2 %collective-permute-start.2 = (bf16[272,512]{1,0:T(8,128)(2,1)}, bf16[272,512]{1,0:T(8,128)(2,1)S(1)}, u32[]{:S(2)}, u32[]{:S(2)}) collective-permute-start(bf16[272,512]{1,0:T(8,128)(2,1)} %get-tuple-element.32.refs_9_), channel_id=1, source_target_pairs={{0,4},{2,6},{4,0},{6,2},{8,12},{10,14},{12,8},{14,10},{1,5},{3,7},... | collective-permute-start | bytes 835592 | tf_op jit(solution)/shard_map/ppermute | solution.py:377
  11.4 32.1 %collective-permute-start.1 = (bf16[128,4096]{1,0:T(8,128)(2,1)}, bf16[128,4096]{1,0:T(8,128)(2,1)S(1)}, u32[]{:S(2)}, u32[]{:S(2)}) collective-permute-start(bf16[128,4096]{1,0:T(8,128)(2,1)} %get-tuple-element.30), channel_id=1, source_target_pairs={{0,2},{2,0},{4,6},{6,4},{8,10},{10,8},{12,14},{14,12},{1,3},{3,1},... | collective-permute-start | bytes 3145736 | tf_op jit(solution)/shard_map/ppermute | solution.py:374
  13.0 22.4 %collective-permute-start.4 = (bf16[272,512]{1,0:T(8,128)(2,1)S(1)}, bf16[272,512]{1,0:T(8,128)(2,1)S(1)}, u32[]{:S(2)}, u32[]{:S(2)}) collective-permute-start(bf16[272,512]{1,0:T(8,128)(2,1)S(1)} %copy-done.8), channel_id=1, source_target_pairs={{0,8},{2,10},{4,12},{6,14},{8,0},{10,2},{12,4},{14,6},{1,9},{3,11}... | collective-permute-start | bytes 835592 | tf_op jit(solution)/shard_map/ppermute | solution.py:377
  15.6 24.7 %collective-permute-start.10 = (bf16[272,512]{1,0:T(8,128)(2,1)S(1)}, bf16[272,512]{1,0:T(8,128)(2,1)S(1)}, u32[]{:S(2)}, u32[]{:S(2)}) collective-permute-start(bf16[272,512]{1,0:T(8,128)(2,1)S(1)} %copy-done.9), channel_id=1, source_target_pairs={{0,8},{2,10},{4,12},{6,14},{8,0},{10,2},{12,4},{14,6},{1,9},{3,11}... | collective-permute-start | bytes 835592 | tf_op jit(solution)/shard_map/ppermute | solution.py:377
  16.0 27.5 %copy-start.10 = (bf16[272,512]{1,0:T(8,128)(2,1)}, bf16[272,512]{1,0:T(8,128)(2,1)S(1)}, u32[]{:S(2)}) copy-start(bf16[272,512]{1,0:T(8,128)(2,1)S(1)} %collective-permute-done.2.refs_11_) | copy-start | bytes 835588
  16.0 51.0 %collective-permute-start.3 = (bf16[128,4096]{1,0:T(8,128)(2,1)}, bf16[128,4096]{1,0:T(8,128)(2,1)S(1)}, u32[]{:S(2)}, u32[]{:S(2)}) collective-permute-start(bf16[128,4096]{1,0:T(8,128)(2,1)} %get-tuple-element.33), channel_id=1, source_target_pairs={{0,2},{2,0},{4,6},{6,4},{8,10},{10,8},{12,14},{14,12},{1,3},{3,1},... | collective-permute-start | bytes 3145736 | tf_op jit(solution)/shard_map/ppermute | solution.py:374
  35.3 34.2 %copy-start.11 = (bf16[272,512]{1,0:T(8,128)(2,1)}, bf16[272,512]{1,0:T(8,128)(2,1)S(1)}, u32[]{:S(2)}) copy-start(bf16[272,512]{1,0:T(8,128)(2,1)S(1)} %collective-permute-done.4.refs_13_) | copy-start | bytes 835588
  35.3 16.1 %collective-permute-start.8 = (bf16[272,512]{1,0:T(8,128)(2,1)S(1)}, bf16[272,512]{1,0:T(8,128)(2,1)S(1)}, u32[]{:S(2)}, u32[]{:S(2)}) collective-permute-start(bf16[272,512]{1,0:T(8,128)(2,1)S(1)} %collective-permute-done.4.refs_13_), channel_id=1, source_target_pairs={{0,16},{16,0},{1,17},{17,1},{2,18},{18,2},{3,19},{19,3},{4,20},{20... | collective-permute-start | bytes 835592 | tf_op jit(solution)/shard_map/ppermute | solution.py:380
  36.9 14.5 %collective-permute-start.11 = (bf16[272,512]{1,0:T(8,128)(2,1)S(1)}, bf16[272,512]{1,0:T(8,128)(2,1)S(1)}, u32[]{:S(2)}, u32[]{:S(2)}) collective-permute-start(bf16[272,512]{1,0:T(8,128)(2,1)S(1)} %collective-permute-done.2.refs_11_), channel_id=1, source_target_pairs={{0,16},{16,0},{1,17},{17,1},{2,18},{18,2},{3,19},{19,3},{4,20},{20... | collective-permute-start | bytes 835592 | tf_op jit(solution)/shard_map/ppermute | solution.py:380
  40.3 32.2 %copy-start.12 = (bf16[272,512]{1,0:T(8,128)(2,1)}, bf16[272,512]{1,0:T(8,128)(2,1)S(1)}, u32[]{:S(2)}) copy-start(bf16[272,512]{1,0:T(8,128)(2,1)S(1)} %collective-permute-done.10.refs_14_) | copy-start | bytes 835588
  40.3 9.6 %collective-permute-start.6 = (bf16[272,512]{1,0:T(8,128)(2,1)S(1)}, bf16[272,512]{1,0:T(8,128)(2,1)S(1)}, u32[]{:S(2)}, u32[]{:S(2)}) collective-permute-start(bf16[272,512]{1,0:T(8,128)(2,1)S(1)} %copy-done.9), channel_id=1, source_target_pairs={{0,4},{2,6},{4,0},{6,2},{8,12},{10,14},{12,8},{14,10},{1,5},{3,7},... | collective-permute-start | bytes 835592 | tf_op jit(solution)/shard_map/ppermute | solution.py:377
  43.5 34.3 %copy-start.5 = (bf16[128,4096]{1,0:T(8,128)(2,1)}, bf16[128,4096]{1,0:T(8,128)(2,1)S(1)}, u32[]{:S(2)}) copy-start(bf16[128,4096]{1,0:T(8,128)(2,1)S(1)} %collective-permute-done.1.refs_3_) | copy-start | bytes 3145732
  43.5 12.3 %collective-permute-start.5 = (bf16[272,512]{1,0:T(8,128)(2,1)S(1)}, bf16[272,512]{1,0:T(8,128)(2,1)S(1)}, u32[]{:S(2)}, u32[]{:S(2)}) collective-permute-start(bf16[272,512]{1,0:T(8,128)(2,1)S(1)} %collective-permute-done.4.refs_13_), channel_id=1, source_target_pairs={{0,4},{2,6},{4,0},{6,2},{8,12},{10,14},{12,8},{14,10},{1,5},{3,7},... | collective-permute-start | bytes 835592 | tf_op jit(solution)/shard_map/ppermute | solution.py:377
  49.9 22.7 %copy-start.15 = (bf16[272,512]{1,0:T(8,128)(2,1)}, bf16[272,512]{1,0:T(8,128)(2,1)S(1)}, u32[]{:S(2)}) copy-start(bf16[272,512]{1,0:T(8,128)(2,1)S(1)} %collective-permute-done.6.refs_12_) | copy-start | bytes 835588
  49.9 9.6 %collective-permute-start.7 = (bf16[272,512]{1,0:T(8,128)(2,1)S(1)}, bf16[272,512]{1,0:T(8,128)(2,1)S(1)}, u32[]{:S(2)}, u32[]{:S(2)}) collective-permute-start(bf16[272,512]{1,0:T(8,128)(2,1)S(1)} %collective-permute-done.6.refs_12_), channel_id=1, source_target_pairs={{0,16},{16,0},{1,17},{17,1},{2,18},{18,2},{3,19},{19,3},{4,20},{20... | collective-permute-start | bytes 835592 | tf_op jit(solution)/shard_map/ppermute | solution.py:380
  51.4 21.1 %copy-start.14 = (bf16[272,512]{1,0:T(8,128)(2,1)}, bf16[272,512]{1,0:T(8,128)(2,1)S(1)}, u32[]{:S(2)}) copy-start(bf16[272,512]{1,0:T(8,128)(2,1)S(1)} %collective-permute-done.11.refs_17_) | copy-start | bytes 835588
  51.4 9.6 %collective-permute-start.12 = (bf16[272,512]{1,0:T(8,128)(2,1)S(1)}, bf16[272,512]{1,0:T(8,128)(2,1)S(1)}, u32[]{:S(2)}, u32[]{:S(2)}) collective-permute-start(bf16[272,512]{1,0:T(8,128)(2,1)S(1)} %collective-permute-done.10.refs_14_), channel_id=1, source_target_pairs={{0,4},{2,6},{4,0},{6,2},{8,12},{10,14},{12,8},{14,10},{1,5},{3,7},... | collective-permute-start | bytes 835592 | tf_op jit(solution)/shard_map/ppermute | solution.py:377
  51.4 26.4 %copy-start.13 = (bf16[272,512]{1,0:T(8,128)(2,1)}, bf16[272,512]{1,0:T(8,128)(2,1)S(1)}, u32[]{:S(2)}) copy-start(bf16[272,512]{1,0:T(8,128)(2,1)S(1)} %collective-permute-done.8.refs_19_) | copy-start | bytes 835588
  51.4 14.0 %collective-permute-start.13 = (bf16[272,512]{1,0:T(8,128)(2,1)S(1)}, bf16[272,512]{1,0:T(8,128)(2,1)S(1)}, u32[]{:S(2)}, u32[]{:S(2)}) collective-permute-start(bf16[272,512]{1,0:T(8,128)(2,1)S(1)} %collective-permute-done.10.refs_14_), channel_id=1, source_target_pairs={{0,16},{16,0},{1,17},{17,1},{2,18},{18,2},{3,19},{19,3},{4,20},{20... | collective-permute-start | bytes 835592 | tf_op jit(solution)/shard_map/ppermute | solution.py:380
  55.8 16.7 %copy-start.16 = (bf16[272,512]{1,0:T(8,128)(2,1)}, bf16[272,512]{1,0:T(8,128)(2,1)S(1)}, u32[]{:S(2)}) copy-start(bf16[272,512]{1,0:T(8,128)(2,1)S(1)} %collective-permute-done.5.refs_15_) | copy-start | bytes 835588
  55.8 5.2 %collective-permute-start.14 = (f32[2,512]{1,0:T(2,128)S(1)}, f32[2,512]{1,0:T(2,128)S(1)}, u32[]{:S(2)}, u32[]{:S(2)}) collective-permute-start(f32[2,512]{1,0:T(2,128)S(1)} %stack.26), channel_id=1, source_target_pairs={{0,2},{2,0},{4,6},{6,4},{8,10},{10,8},{12,14},{14,12},{1,3},{3,1},... | collective-permute-start | bytes 12296 | tf_op jit(solution)/shard_map/ppermute | solution.py:374
  59.5 10.1 %copy-start.17 = (bf16[272,512]{1,0:T(8,128)(2,1)}, bf16[272,512]{1,0:T(8,128)(2,1)S(1)}, u32[]{:S(2)}) copy-start(bf16[272,512]{1,0:T(8,128)(2,1)S(1)} %collective-permute-done.7.refs_18_) | copy-start | bytes 835588
  59.5 10.1 %collective-permute-start.9 = (bf16[272,512]{1,0:T(8,128)(2,1)S(1)}, bf16[272,512]{1,0:T(8,128)(2,1)S(1)}, u32[]{:S(2)}, u32[]{:S(2)}) collective-permute-start(bf16[272,512]{1,0:T(8,128)(2,1)S(1)} %collective-permute-done.5.refs_15_), channel_id=1, source_target_pairs={{0,16},{16,0},{1,17},{17,1},{2,18},{18,2},{3,19},{19,3},{4,20},{20... | collective-permute-start | bytes 835592 | tf_op jit(solution)/shard_map/ppermute | solution.py:380
  61.0 8.5 %copy-start.18 = (bf16[272,512]{1,0:T(8,128)(2,1)}, bf16[272,512]{1,0:T(8,128)(2,1)S(1)}, u32[]{:S(2)}) copy-start(bf16[272,512]{1,0:T(8,128)(2,1)S(1)} %collective-permute-done.12.refs_16_) | copy-start | bytes 835588
  65.4 7.1 %copy-start.19 = (bf16[272,512]{1,0:T(8,128)(2,1)}, bf16[272,512]{1,0:T(8,128)(2,1)S(1)}, u32[]{:S(2)}) copy-start(bf16[272,512]{1,0:T(8,128)(2,1)S(1)} %collective-permute-done.13.refs_20_) | copy-start | bytes 835588
  65.4 7.1 %collective-permute-start.15 = (bf16[272,512]{1,0:T(8,128)(2,1)S(1)}, bf16[272,512]{1,0:T(8,128)(2,1)S(1)}, u32[]{:S(2)}, u32[]{:S(2)}) collective-permute-start(bf16[272,512]{1,0:T(8,128)(2,1)S(1)} %collective-permute-done.12.refs_16_), channel_id=1, source_target_pairs={{0,16},{16,0},{1,17},{17,1},{2,18},{18,2},{3,19},{19,3},{4,20},{20... | collective-permute-start | bytes 835592 | tf_op jit(solution)/shard_map/ppermute | solution.py:380
  66.9 10.9 %copy-start.6 = (bf16[128,4096]{1,0:T(8,128)(2,1)}, bf16[128,4096]{1,0:T(8,128)(2,1)S(1)}, u32[]{:S(2)}) copy-start(bf16[128,4096]{1,0:T(8,128)(2,1)S(1)} %collective-permute-done.3.refs_4_) | copy-start | bytes 3145732
  69.5 3.0 %copy-start.20 = (bf16[272,512]{1,0:T(8,128)(2,1)}, bf16[272,512]{1,0:T(8,128)(2,1)S(1)}, u32[]{:S(2)}) copy-start(bf16[272,512]{1,0:T(8,128)(2,1)S(1)} %collective-permute-done.9.refs_21_) | copy-start | bytes 835588
  72.5 2.7 %collective-permute-start.16 = (bf16[128,4096]{1,0:T(8,128)(2,1)S(1)}, bf16[128,4096]{1,0:T(8,128)(2,1)S(1)}, u32[]{:S(2)}, u32[]{:S(2)}) collective-permute-start(bf16[128,4096]{1,0:T(8,128)(2,1)S(1)} %collective-permute-done.1.refs_3_), channel_id=1, source_target_pairs={{0,1},{1,0},{2,3},{3,2},{4,5},{5,4},{6,7},{7,6},{8,9},{9,8},{10,11... | collective-permute-start | bytes 3145736 | tf_op jit(solution)/shard_map/ppermute | solution.py:383
  73.2 3.6 %collective-permute-start.17 = (bf16[128,4096]{1,0:T(8,128)(2,1)S(1)}, bf16[128,4096]{1,0:T(8,128)(2,1)}, u32[]{:S(2)}, u32[]{:S(2)}) collective-permute-start(bf16[128,4096]{1,0:T(8,128)(2,1)S(1)} %collective-permute-done.3.refs_4_), channel_id=1, source_target_pairs={{0,1},{1,0},{2,3},{3,2},{4,5},{5,4},{6,7},{7,6},{8,9},{9,8},{10,11... | collective-permute-start | bytes 3145736 | tf_op jit(solution)/shard_map/ppermute | solution.py:383
  75.2 2.7 %copy-start.7 = (bf16[128,4096]{1,0:T(8,128)(2,1)}, bf16[128,4096]{1,0:T(8,128)(2,1)S(1)}, u32[]{:S(2)}) copy-start(bf16[128,4096]{1,0:T(8,128)(2,1)S(1)} %collective-permute-done.16.refs_5_) | copy-start | bytes 3145732
  88.8 11.8 %copy-start.1 = (f32[4,2,128,128]{3,2,1,0:T(8,128)S(1)}, f32[4,2,128,128]{3,2,1,0:T(8,128)}, u32[]{:S(2)}) copy-start(f32[4,2,128,128]{3,2,1,0:T(8,128)} %get-tuple-element.45.keep_ref) | copy-start | bytes 1572868
  88.8 11.8 %copy-start.4 = (s32[12]{0:T(128)S(1)}, s32[12]{0:T(128)}, u32[]{:S(2)}) copy-start(s32[12]{0:T(128)} %concatenate.18.scalars_ref.refs_0_) | copy-start | bytes 148
  88.8 17.0 %copy-start = (f32[4,2,128,128]{3,2,1,0:T(8,128)S(1)}, f32[4,2,128,128]{3,2,1,0:T(8,128)}, u32[]{:S(2)}) copy-start(f32[4,2,128,128]{3,2,1,0:T(8,128)} %get-tuple-element.51.keep_ref) | copy-start | bytes 1572868
  88.9 8.6 %collective-permute-start.18 = (bf16[4,2,128,128]{3,2,1,0:T(8,128)(2,1)}, bf16[4,2,128,128]{3,2,1,0:T(8,128)(2,1)S(1)}, u32[]{:S(2)}, u32[]{:S(2)}) collective-permute-start(bf16[4,2,128,128]{3,2,1,0:T(8,128)(2,1)} %get-tuple-element.46), channel_id=1, source_target_pairs={{0,2},{2,0},{4,6},{6,4},{8,10},{10,8},{12,14},{14,12},{1,3},{3,1},... | collective-permute-start | bytes 786440 | tf_op jit(solution)/shard_map/ppermute | solution.py:374
  97.5 8.4 %collective-permute-start.22 = (bf16[4,2,128,128]{3,2,1,0:T(8,128)(2,1)}, bf16[4,2,128,128]{3,2,1,0:T(8,128)(2,1)S(1)}, u32[]{:S(2)}, u32[]{:S(2)}) collective-permute-start(bf16[4,2,128,128]{3,2,1,0:T(8,128)(2,1)} %get-tuple-element.53), channel_id=1, source_target_pairs={{0,2},{2,0},{4,6},{6,4},{8,10},{10,8},{12,14},{14,12},{1,3},{3,1},... | collective-permute-start | bytes 786440 | tf_op jit(solution)/shard_map/ppermute | solution.py:374
  101.4 5.1 %copy-start.2 = (bf16[256,128]{1,0:T(8,128)(2,1)}, bf16[256,128]{1,0:T(8,128)(2,1)S(1)}, u32[]{:S(2)}) copy-start(bf16[256,128]{1,0:T(8,128)(2,1)S(1)} %get-tuple-element.47.refs_0_) | copy-start | bytes 196612
  101.4 8.8 %collective-permute-start.19 = (bf16[256,128]{1,0:T(8,128)(2,1)S(1)}, bf16[256,128]{1,0:T(8,128)(2,1)S(1)}, u32[]{:S(2)}, u32[]{:S(2)}) collective-permute-start(bf16[256,128]{1,0:T(8,128)(2,1)S(1)} %get-tuple-element.48), channel_id=1, source_target_pairs={{0,4},{2,6},{4,0},{6,2},{8,12},{10,14},{12,8},{14,10},{1,5},{3,7},... | collective-permute-start | bytes 196616 | tf_op jit(solution)/shard_map/ppermute | solution.py:377
  102.0 9.5 %collective-permute-start.20 = (bf16[256,128]{1,0:T(8,128)(2,1)S(1)}, bf16[256,128]{1,0:T(8,128)(2,1)S(1)}, u32[]{:S(2)}, u32[]{:S(2)}) collective-permute-start(bf16[256,128]{1,0:T(8,128)(2,1)S(1)} %get-tuple-element.49), channel_id=1, source_target_pairs={{0,8},{2,10},{4,12},{6,14},{8,0},{10,2},{12,4},{14,6},{1,9},{3,11}... | collective-permute-start | bytes 196616 | tf_op jit(solution)/shard_map/ppermute | solution.py:377
  104.5 7.0 %collective-permute-start.21 = (bf16[256,128]{1,0:T(8,128)(2,1)S(1)}, bf16[256,128]{1,0:T(8,128)(2,1)S(1)}, u32[]{:S(2)}, u32[]{:S(2)}) collective-permute-start(bf16[256,128]{1,0:T(8,128)(2,1)S(1)} %get-tuple-element.50), channel_id=1, source_target_pairs={{0,12},{2,14},{4,8},{6,10},{8,4},{10,6},{12,0},{14,2},{1,13},{3,15... | collective-permute-start | bytes 196616 | tf_op jit(solution)/shard_map/ppermute | solution.py:377
  107.1 6.7 %collective-permute-start.23 = (bf16[256,128]{1,0:T(8,128)(2,1)S(1)}, bf16[256,128]{1,0:T(8,128)(2,1)S(1)}, u32[]{:S(2)}, u32[]{:S(2)}) collective-permute-start(bf16[256,128]{1,0:T(8,128)(2,1)S(1)} %get-tuple-element.55), channel_id=1, source_target_pairs={{0,4},{2,6},{4,0},{6,2},{8,12},{10,14},{12,8},{14,10},{1,5},{3,7},... | collective-permute-start | bytes 196616 | tf_op jit(solution)/shard_map/ppermute | solution.py:377
  107.1 7.3 %collective-permute-start.24 = (bf16[256,128]{1,0:T(8,128)(2,1)S(1)}, bf16[256,128]{1,0:T(8,128)(2,1)S(1)}, u32[]{:S(2)}, u32[]{:S(2)}) collective-permute-start(bf16[256,128]{1,0:T(8,128)(2,1)S(1)} %get-tuple-element.56), channel_id=1, source_target_pairs={{0,8},{2,10},{4,12},{6,14},{8,0},{10,2},{12,4},{14,6},{1,9},{3,11}... | collective-permute-start | bytes 196616 | tf_op jit(solution)/shard_map/ppermute | solution.py:377
  110.2 6.1 %collective-permute-start.25 = (bf16[256,128]{1,0:T(8,128)(2,1)S(1)}, bf16[256,128]{1,0:T(8,128)(2,1)S(1)}, u32[]{:S(2)}, u32[]{:S(2)}) collective-permute-start(bf16[256,128]{1,0:T(8,128)(2,1)S(1)} %get-tuple-element.57), channel_id=1, source_target_pairs={{0,12},{2,14},{4,8},{6,10},{8,4},{10,6},{12,0},{14,2},{1,13},{3,15... | collective-permute-start | bytes 196616 | tf_op jit(solution)/shard_map/ppermute | solution.py:377
  113.8 2.4 %copy-start.24 = (bf16[256,128]{1,0:T(8,128)(2,1)}, bf16[256,128]{1,0:T(8,128)(2,1)S(1)}, u32[]{:S(2)}) copy-start(bf16[256,128]{1,0:T(8,128)(2,1)S(1)} %collective-permute-done.23.refs_1_) | copy-start | bytes 196612
  114.4 1.8 %copy-start.26 = (bf16[256,128]{1,0:T(8,128)(2,1)}, bf16[256,128]{1,0:T(8,128)(2,1)S(1)}, u32[]{:S(2)}) copy-start(bf16[256,128]{1,0:T(8,128)(2,1)S(1)} %collective-permute-done.24.refs_2_) | copy-start | bytes 196612
  (6 other events, 4.6 us)

commit v3 on v0

v3 whole, which is shorter than its diff:
```python
import functools
import math

import jax
import jax.numpy as jnp
from jax import lax
from jax.experimental import pallas as pl
from jax.experimental.pallas import tpu as pltpu
from jax.sharding import PartitionSpec as P

HD = 128
GAIN_ROWS = 16
VMEM_LIMIT = 58 * 2**20
SMALL_VMEM_LIMIT = 8 * 2**20


def rotary_table(position, size_head):
    half_size = size_head // 2
    frequency = jnp.power(
        jnp.float32(500000.0), -2.0 * jnp.arange(half_size, dtype=jnp.float32) / size_head
    )
    angle = jnp.mod(position.astype(jnp.float32)[:, None] * frequency[None, :], 2.0 * math.pi)
    return jnp.cos(angle), jnp.sin(angle)


def rotate(unrotated, position):
    half_size = unrotated.shape[-1] // 2
    cosine, sine = rotary_table(position, unrotated.shape[-1])
    cosine, sine = cosine[:, None, :], sine[:, None, :]
    values = unrotated.astype(jnp.float32)
    first = values[..., :half_size]
    second = values[..., half_size:]
    return jnp.concatenate(
        [first * cosine - second * sine, second * cosine + first * sine], axis=-1
    ).astype(jnp.bfloat16)


def normalize(values, squares_total, gain, feature_count):
    scale = lax.rsqrt(squares_total / feature_count + 1e-05)
    return (values.astype(jnp.float32) * scale[:, None] * gain.astype(jnp.float32)[None, :]).astype(
        jnp.bfloat16
    )


def general_shards(hidden, gain_table, layer_id, w_key, w_value, offsets, owner_map):
    tok_count = lax.axis_size("tok")
    col_count = lax.axis_size("col")
    gain_piece = lax.dynamic_index_in_dim(gain_table, layer_id[0], 0, keepdims=False)
    gain_full = lax.all_gather(gain_piece, "tok", axis=0, tiled=True)
    feature_count = gain_full.shape[0]
    block_rows = hidden.shape[0] * col_count
    tok_rows = lax.all_gather(hidden, "col", axis=0, tiled=True)
    wide = tok_rows.astype(jnp.float32)
    normed = normalize(tok_rows, jnp.sum(wide * wide, axis=1), gain_full, feature_count)
    key_raw, value_new = (
        jnp.dot(
            normed,
            lax.all_gather(weight, "tok", axis=0, tiled=True),
            preferred_element_type=jnp.float32,
        ).astype(jnp.bfloat16)
        for weight in (w_key, w_value)
    )
    heads_here = key_raw.shape[1] // HD
    classes = tok_count // heads_here
    page = block_rows // classes
    group_ids = jnp.arange(tok_count, dtype=jnp.int32)
    inverse = jnp.zeros((tok_count,), jnp.int32).at[owner_map].set(group_ids)

    def arrange_pages(values):
        grouped = (
            values.reshape(classes, page, heads_here, HD)
            .transpose(2, 0, 1, 3)
            .reshape(tok_count, page, HD)
        )
        return jnp.take(grouped, inverse, axis=0).reshape(tok_count * page, HD)

    position = offsets[0] + jnp.arange(block_rows, dtype=jnp.int32)
    key_new = rotate(key_raw.reshape(block_rows, heads_here, HD), position).reshape(block_rows, -1)
    key_out, value_out = (
        lax.all_to_all(arrange_pages(values), "tok", split_axis=0, concat_axis=0, tiled=True)
        for values in (key_new, value_new)
    )
    return (key_out.reshape(1, -1, HD), value_out.reshape(1, -1, HD))


def run_copies(pairs, sems):
    copies = [
        pltpu.make_async_copy(source, target, sems.at[i])
        for i, (source, target) in enumerate(pairs)
    ]
    for copy in copies:
        copy.start()
    return copies


def wait_all(copies):
    for copy in copies:
        copy.wait()


SMEM = pl.BlockSpec(memory_space=pltpu.SMEM)
VMEM = pl.BlockSpec(memory_space=pltpu.VMEM)
HBM = pl.BlockSpec(memory_space=pltpu.HBM)


def here():
    tok = lax.axis_index("tok")
    return lax.axis_index("group"), tok % 2, tok // 2, lax.axis_index("col")


def half_kernel(shard, hidden_ref, half_ref, sems):
    x = here()[1]
    pairs = []
    for i in range(half_ref.shape[1] // shard):
        lanes = pl.ds(pl.multiple_of((2 * i + 1 - x) * shard, shard), shard)
        pairs.append((hidden_ref.at[:, lanes], half_ref.at[:, pl.ds(i * shard, shard)]))
    wait_all(run_copies(pairs, sems))


def away_half(hidden, shard):
    rows, features = hidden.shape
    return pl.pallas_call(
        functools.partial(half_kernel, shard),
        in_specs=[HBM],
        out_specs=VMEM,
        out_shape=jax.ShapeDtypeStruct((rows, features // 2), hidden.dtype),
        scratch_shapes=[pltpu.SemaphoreType.DMA((features // shard // 2,))],
        compiler_params=pltpu.CompilerParams(vmem_limit_bytes=SMALL_VMEM_LIMIT),
    )(hidden)


def pack_kernel(layer_ref, key_ref, value_ref, gain_ref, *refs):
    *packed_refs, table, sems = refs
    shard, columns = key_ref.shape
    half = shard // 2
    width = 2 * columns
    gain_parts = shard // width
    layer = layer_ref[0]
    block = pl.multiple_of(layer // GAIN_ROWS * GAIN_ROWS, GAIN_ROWS)
    pairs = [(gain_ref.at[pl.ds(block, GAIN_ROWS), :], table)]
    for i, packed_ref in enumerate(packed_refs):
        count = PACKED[i][1]
        rows = half // count
        first = pl.multiple_of(here()[0] * half + PACKED[i][0] * rows, rows)
        for k, weight_ref in enumerate((key_ref, value_ref)):
            target = packed_ref.at[pl.ds(0, rows), pl.ds(k * columns, columns)]
            pairs.append((weight_ref.at[pl.ds(first, rows), :], target))
    copies = run_copies(pairs, sems)
    copies[0].wait()
    found = table[...].astype(jnp.float32)
    pick = lax.broadcasted_iota(jnp.int32, found.shape, 0) == layer % GAIN_ROWS
    gain = jnp.sum(jnp.where(pick, found, 0.0), axis=0, keepdims=True)
    for i, packed_ref in enumerate(packed_refs):
        index, count = PACKED[i]
        rows = half // count
        for p in range(gain_parts // count):
            part = index * (gain_parts // count) + p
            packed_ref[rows + p * GAIN_ROWS : rows + (p + 1) * GAIN_ROWS, :] = jnp.broadcast_to(
                gain[:, part * width : (part + 1) * width], (GAIN_ROWS, width)
            ).astype(packed_ref.dtype)
    wait_all(copies[1:])


PACKED = ((0, 2), (1, 2), (0, 1))


def pack_weights(layer_id, w_key, w_value, gain_table):
    shard, columns = w_key.shape
    rows = shard // 2 + shard // (2 * columns) * GAIN_ROWS
    return pl.pallas_call(
        pack_kernel,
        in_specs=[SMEM, HBM, HBM, HBM],
        out_specs=[VMEM] * len(PACKED),
        out_shape=[
            jax.ShapeDtypeStruct((rows // count, 2 * columns), w_key.dtype) for _, count in PACKED
        ],
        scratch_shapes=[
            pltpu.VMEM((GAIN_ROWS, gain_table.shape[1]), gain_table.dtype),
            pltpu.SemaphoreType.DMA((1 + 2 * len(PACKED),)),
        ],
        compiler_params=pltpu.CompilerParams(vmem_limit_bytes=SMALL_VMEM_LIMIT),
    )(layer_id, w_key, w_value, gain_table)


def group_of(owner_ref, owner):
    group = jnp.int32(0)
    for g in range(owner_ref.shape[0]):
        group = jnp.where(owner_ref[g] == owner, g, group)
    return group // 4, group % 4 // 2, group % 2


def multiply_kernel(shard, counts, which, *refs):
    refs = list(refs)
    owner_ref = refs.pop(0)
    sources = [refs.pop(0) for _ in range(4)]
    weight_ref = refs.pop(0)
    line = len(counts)
    mine = [[refs.pop(0) for _ in range(count)] for count in counts]
    theirs = [[]] + [[refs.pop(0) for _ in range(count)] for count in counts[1:]]
    keep, send, weights, gains, raw, total, sems = refs
    y, x, z, c = here()
    half = shard // 2
    columns = weight_ref.shape[1]
    width = 2 * columns
    _, _, page, _ = keep.shape
    device_rows = 2 * page
    pairs, ends = [], []
    for d in range(line):
        first = d * shard
        rows = half // counts[d]
        gain_parts = shard // width // counts[d]
        for i, packed in enumerate(mine[d]):
            for p in range(gain_parts):
                lanes = pl.ds(first + (i * gain_parts + p) * width, width)
                gain_rows = pl.ds(rows + p * GAIN_ROWS, GAIN_ROWS)
                pairs.append((packed.at[gain_rows, :], gains.at[:, lanes]))
        if d == 0:
            pairs.append((weight_ref, weights.at[pl.ds(first, shard), :]))
        picked = pl.ds(which * columns, columns)
        for blocks, side in ((mine[d] if d > 0 else [], y), (theirs[d], 1 - y)):
            for i, packed in enumerate(blocks):
                start = pl.multiple_of(first + side * half + i * rows, rows)
                target = weights.at[pl.ds(start, rows), :]
                pairs.append((packed.at[pl.ds(0, rows), picked], target))
        place_z = jnp.bitwise_xor(z, d)
        for i, source in enumerate(sources):
            block = 2 * place_z + x if i < 2 else place_z
            lanes = pl.ds(pl.multiple_of(block * shard, shard), shard)
            target = raw.at[pl.ds(i * device_rows, device_rows), pl.ds(first, shard)]
            pairs.append((source.at[:, lanes], target))
        ends.append(len(pairs))
    copies = run_copies(pairs, sems)
    for d in range(line):
        wait_all(copies[(ends[d - 1] if d > 0 else 0) : ends[d]])
        block = slice(d * shard, (d + 1) * shard)
        for i in range(2):
            span = slice(i * 2 * device_rows, (i + 1) * 2 * device_rows)
            product = jnp.dot(
                raw[span, block] * gains[0:1, block],
                weights[block, :],
                preferred_element_type=jnp.float32,
            )
            total[span, :] = product if d == 0 else total[span, :] + product
    for owner_z in range(line):
        for owner_x, out in ((x, keep), (1 - x, send)):
            j, core, part = group_of(owner_ref, owner_z * 2 + owner_x)
            lanes = pl.ds(pl.multiple_of(j * HD, HD), HD)
            for side in range(2):
                source = 2 * side + jnp.bitwise_xor(core, c)
                start = pl.multiple_of(source * device_rows + part * page, page)
                out[owner_z, jnp.bitwise_xor(x, side)] = total[pl.ds(start, page), lanes].astype(
                    out.dtype
                )


def multiply(owner_map, sources, weight, which, mine, theirs):
    shard, columns = weight.shape
    line = len(mine)
    device_rows = sources[0].shape[0]
    operands = [
        *sources, weight,
        *[packed for blocks in mine + theirs for packed in blocks],
    ]
    shape = (line, 2, device_rows // 2, HD)
    counts = tuple(len(blocks) for blocks in mine)
    copies = line * (shard // (2 * columns)) + 1 + 2 * sum(counts) + 4 * line
    return pl.pallas_call(
        functools.partial(multiply_kernel, shard, counts, which),
        in_specs=[SMEM] + [HBM] * len(operands),
        out_specs=[VMEM] * 2,
        out_shape=[
            jax.ShapeDtypeStruct(shape, jnp.float32),
            jax.ShapeDtypeStruct(shape, jnp.bfloat16),
        ],
        scratch_shapes=[
            pltpu.VMEM((line * shard, columns), jnp.bfloat16),
            pltpu.VMEM((GAIN_ROWS, line * shard), jnp.bfloat16),
            pltpu.VMEM((4 * device_rows, line * shard), jnp.bfloat16),
            pltpu.VMEM((4 * device_rows, columns), jnp.float32),
            pltpu.SemaphoreType.DMA((copies,)),
        ],
        compiler_params=pltpu.CompilerParams(vmem_limit_bytes=VMEM_LIMIT),
    )(owner_map, *operands)


def finish_kernel(line, turn, owner_ref, keep_ref, came_ref, scale_ref, *refs):
    out_refs = refs[-line:]
    _, x, z, c = here()
    page = keep_ref.shape[2]
    for d, out_ref in enumerate(out_refs):
        owner_z = jnp.bitwise_xor(z, d)
        _, core, part = group_of(owner_ref, owner_z * 2 + x)
        for s in range(2):
            source = 2 * jnp.bitwise_xor(x, s) + jnp.bitwise_xor(core, c)
            scale = scale_ref[source, pl.ds(pl.multiple_of(part * page, page), page), :]
            result = (keep_ref[owner_z, s] + came_ref[owner_z, s].astype(jnp.float32)) * scale
            if turn:
                cos_ref, sin_ref = refs[:2]
                result = result.astype(jnp.bfloat16).astype(jnp.float32)
                page_class = s * 4 + core * 2 + part
                turned = pltpu.roll(result, HD // 2, 1)
                result = result * cos_ref[page_class] + turned * sin_ref[page_class]
            out_ref[s * page : (s + 1) * page, :] = result.astype(jnp.bfloat16)


def finish(owner_map, keep, came, scale, *tables):
    line, _, page, _ = keep.shape
    return pl.pallas_call(
        functools.partial(finish_kernel, line, len(tables) > 0),
        in_specs=[SMEM] + [VMEM] * (3 + len(tables)),
        out_specs=[VMEM] * line,
        out_shape=[jax.ShapeDtypeStruct((2 * page, HD), jnp.bfloat16)] * line,
        compiler_params=pltpu.CompilerParams(vmem_limit_bytes=SMALL_VMEM_LIMIT),
    )(owner_map, keep, came, scale, *tables)


def place_kernel(*refs):
    out_ref = refs[-1]
    z = here()[2]
    rows = refs[0].shape[0]
    for d, block_ref in enumerate(refs[:-1]):
        start = pl.multiple_of(jnp.bitwise_xor(z, d) * rows, rows)
        out_ref[pl.ds(start, rows), :] = block_ref[...]


def place(blocks):
    return pl.pallas_call(
        place_kernel,
        in_specs=[VMEM] * len(blocks),
        out_specs=VMEM,
        out_shape=jax.ShapeDtypeStruct((len(blocks) * blocks[0].shape[0], HD), jnp.bfloat16),
        compiler_params=pltpu.CompilerParams(vmem_limit_bytes=SMALL_VMEM_LIMIT),
    )(*blocks)


def after(value, *others):
    return lax.optimization_barrier((value, *others))[0]


def paired_shards(hidden, gain_table, layer_id, w_key, w_value, offsets, owner_map):
    tok_count = lax.axis_size("tok")
    line = tok_count // 2
    _, x, _, _ = here()
    shard = w_key.shape[0]
    device_rows = hidden.shape[0]
    page = device_rows // 2

    def over_x(values):
        return lax.ppermute(values, "tok", [(t, t ^ 1) for t in range(tok_count)])

    def over_z(values, distance):
        return lax.ppermute(values, "tok", [(t, t ^ (2 * distance)) for t in range(tok_count)])

    def over_y(values):
        return lax.ppermute(values, "group", [(0, 1), (1, 0)])

    def over_c(values):
        return lax.ppermute(values, "col", [(0, 1), (1, 0)])

    other = over_c(hidden)
    pair_offset = over_x(offsets)
    away = away_half(hidden, shard)
    own_away = over_x(after(away, pair_offset))
    *pieces, packed = pack_weights(layer_id, after(w_key, away), w_value, gain_table)
    near_0 = over_z(pieces[0], 1)
    far_0 = over_z(pieces[0], 2)
    near_1 = over_z(after(pieces[1], other), 1)
    far_1 = over_z(after(pieces[1], near_0), 2)
    near_y_0 = over_y(near_0)

    wide = after(hidden, packed).astype(jnp.float32)
    own_squares = jnp.sum(wide * wide, axis=1)
    starts = jnp.where(x == 0, jnp.stack([offsets, pair_offset]), jnp.stack([pair_offset, offsets]))
    position = (starts + jnp.arange(2 * device_rows, dtype=jnp.int32)[None, :]).reshape(-1)
    cosine, sine = rotary_table(position, HD)
    cosine = jnp.concatenate([cosine, cosine], axis=1).reshape(8, page, HD)
    sine = jnp.concatenate([-sine, sine], axis=1).reshape(8, page, HD)

    corner_0 = over_z(after(far_0, near_0, own_squares), 1)
    near_y_1 = over_y(near_1)
    far_y_0 = over_y(after(far_0, near_y_0))
    corner_1 = over_z(after(far_1, near_y_1), 1)
    far_y_1 = over_y(after(far_1, near_y_1))
    corner_y_0 = over_y(after(corner_0, far_y_0, corner_1, cosine, sine))
    corner_y_1 = over_y(after(corner_1, far_y_1))
    other_away = over_c(after(own_away, corner_y_0, far_y_1))

    pair_squares = jnp.stack([own_squares, over_x(own_squares)])
    squares = jnp.stack([pair_squares, over_c(pair_squares)], axis=1).reshape(4, device_rows)
    scale = lax.rsqrt(squares / hidden.shape[1] + 1e-05)
    scale = jnp.broadcast_to(scale[:, :, None], (4, device_rows, HD))

    sources = [hidden, other, own_away, other_away]
    mine = [[packed], [near_0, near_1], [far_0, far_1], [corner_0, corner_1]]
    theirs = [[near_y_0, near_y_1], [far_y_0, far_y_1], [corner_y_0, corner_y_1]]
    key_keep, key_send = multiply(owner_map, sources, w_key, 0, mine, theirs)
    key_came = over_x(key_send)
    value_keep, value_send = multiply(
        owner_map, sources, after(w_value, key_send), 1, mine, theirs
    )
    value_came = over_x(value_send)
    keys = finish(owner_map, key_keep, key_came, scale, cosine, sine)
    values = finish(owner_map, value_keep, after(value_came, keys[0]), scale)
    keys = [keys[0]] + [over_z(keys[d], d) for d in range(1, line)]
    values = [values[0], after(values[1], *keys[1:]), *values[2:]]
    values = [values[0]] + [over_z(values[d], d) for d in range(1, line)]
    return (place(keys)[None], place(values)[None])


def solution(mesh):
    in_specs = (
        P(("group", "tok", "col"), None),
        P(None, "tok"),
        P("group"),
        P("tok", "col"),
        P("tok", "col"),
        P(("group", "tok")),
        P("group"),
    )
    out_specs = (P("col", ("group", "tok"), None), P("col", ("group", "tok"), None))
    paired = mesh.shape["group"] == 2 and mesh.shape["tok"] == 8 and mesh.shape["col"] == 2
    shards = paired_shards if paired else general_shards
    return jax.shard_map(shards, mesh=mesh, in_specs=in_specs, out_specs=out_specs, check_vma=False)
```

time: 224 us -> 107 us (0.48)
  waiting for transfers between devices: 135 us -> 39.4 us
  blocking collectives: 43.9 us -> 0 us
  starting transfers between devices: 3.7 us -> 35.3 us
  Pallas kernels: 0 us -> 16.7 us
  matrix products: 14.4 us -> 0 us
  between operations: 15.2 us -> 2.22 us
  local copies, waits for them, and re-layouts: 3.67 us -> 6.54 us
    all_gather x3 -> x0, waiting for transfers between devices: 125 us -> none  [the longest x1 65.9 us: shards(): lax.all_gather(w_value, 'tok', axis=0, tiled=True)]
    ppermute x0 -> x26, waiting for transfers between devices: none -> 39.4 us  [the longest x12 19.5 us: over_z(): lax.ppermute(values, 'tok', [(t, t ^ 2 * distance) for t in range(tok_cou...]
    ppermute x0 -> x26, starting transfers between devices: none -> 35.3 us  [the longest x12 17.4 us: over_z(): lax.ppermute(values, 'tok', [(t, t ^ 2 * distance) for t in range(tok_cou...]
    all_gather x1 -> x0, blocking collectives: 32.2 us -> none  [shards(): gain_full = lax.all_gather(gain_piece, 'tok', axis=0, tiled=True)]
    pallas_call x0 -> x8, Pallas kernels: none -> 16.7 us  [the longest x2 13.4 us: multiply(): pl.pallas_call(functools.partial(multiply_kernel, shard, counts, which),...]
    dot_general x2 -> x0, matrix products: 14.4 us -> none  [the longest x1 7.42 us: add_block(): jnp.dot(normed, pieces[0], preferred_element_type=jnp.float32)]
    all_to_all x1 -> x0, blocking collectives: 11.7 us -> none  [shards(): lax.all_to_all(arrange_pages(key_new), 'tok', split_axis=0, concat_axis=0...]
    all_to_all x1 -> x0, waiting for transfers between devices: 8.57 us -> none  [shards(): lax.all_to_all(arrange_pages(value_new), 'tok', split_axis=0, concat_axis...]
  transfers between devices with their start and end apart: 4 -> 26, of which waited for: 3 -> 13; matrix products, arithmetic and copies ran while one was open for 7% -> 6% of each run, Pallas kernels for 0% -> 9%
where the time goes in v3:
time: 107 us
  waiting for transfers between devices  39.4 us (37%)
  starting transfers between devices  35.3 us (33%)
  Pallas kernels  16.7 us (16%)
  local copies, waits for them, and re-layouts  6.54 us (6%)
  other arithmetic  6.4 us (6%)
  between operations  2.22 us (2%)
    ppermute x12, waiting for transfers between devices, over_z(): lax.ppermute(values, 'tok', [(t, t ^ 2 * distance) for t in range(tok_cou...  19.5 us
    ppermute x12, starting transfers between devices, over_z(): lax.ppermute(values, 'tok', [(t, t ^ 2 * distance) for t in range(tok_cou...  17.4 us
    ppermute x6, waiting for transfers between devices, over_y(): return lax.ppermute(values, 'group', [(0, 1), (1, 0)])  15.2 us
    pallas_call x2, Pallas kernels, multiply(): pl.pallas_call(functools.partial(multiply_kernel, shard, counts, which),...  13.4 us
    ppermute x5, starting transfers between devices, over_x(): return lax.ppermute(values, 'tok', [(t, t ^ 1) for t in range(tok_count)])  9.63 us
    ppermute x6, starting transfers between devices, over_y(): return lax.ppermute(values, 'group', [(0, 1), (1, 0)])  7.67 us
    unnamed x34, local copies, waits for them, and re-layouts  6.16 us
    ppermute x5, waiting for transfers between devices, over_x(): return lax.ppermute(values, 'tok', [(t, t ^ 1) for t in range(tok_count)])  3.57 us
  transfers between devices with their start and end apart: 26, of which 13 were waited for; matrix products, arithmetic and copies ran while one was open for 6% of the time, Pallas kernels for 9%

profile of v3, /device:TPU:0, one launch (start us, length us, event | category | flops | bytes accessed | tf_op | source)
XLA Modules:
  0.0 106.6 jit_solution(13547418615495807678)
XLA Ops:
  0.6 0.5 collective-permute-start
  1.1 2.6 %collective-permute-start.1 = (s32[1]{0:T(128)}, s32[1]{0:T(128)}, u32[]{:S(2)}, u32[]{:S(2)}) collective-permute-start(s32[1]{0:T(128)} %param.12), channel_id=1, source_target_pairs={{0,2},{2,0},{4,6},{6,4},{8,10},{10,8},{12,14},{14,12},{1,3},{3,1},... | collective-permute-start | bytes 20 | tf_op jit(solution)/shard_map/ppermute | solution.py:349
  3.7 2.2 %copy-done = bf16[256,8192]{1,0:T(8,128)(2,1)S(1)} copy-done((bf16[256,8192]{1,0:T(8,128)(2,1)S(1)}, bf16[256,8192]{1,0:T(8,128)(2,1)}, u32[]{:S(2)}) %copy-start) | copy-done | bytes 4194328
  6.2 1.3 %collective-permute-start.2 = (bf16[256,4096]{1,0:T(8,128)(2,1)S(1)}, bf16[256,4096]{1,0:T(8,128)(2,1)}, u32[]{:S(2)}, u32[]{:S(2)}) collective-permute-start(bf16[256,4096]{1,0:T(8,128)(2,1)S(1)} %shard_map.86), channel_id=1, source_target_pairs={{0,2},{2,0},{4,6},{6,4},{8,10},{10,8},{12,14},{14,12},{1,3},{3,1},... | collective-permute-start | bytes 6291464 | tf_op jit(solution)/shard_map/ppermute | solution.py:349
  8.2 0.2 shard_map.87
  8.4 0.8 copy-done.1
  9.2 1.6 %collective-permute-start.4 = (bf16[272,512]{1,0:T(8,128)(2,1)S(1)}, bf16[272,512]{1,0:T(8,128)(2,1)S(1)}, u32[]{:S(2)}, u32[]{:S(2)}) collective-permute-start(bf16[272,512]{1,0:T(8,128)(2,1)S(1)} %get-tuple-element.33), channel_id=1, source_target_pairs={{0,4},{2,6},{4,0},{6,2},{8,12},{10,14},{12,8},{14,10},{1,5},{3,7},... | collective-permute-start | bytes 835592 | tf_op jit(solution)/shard_map/ppermute | solution.py:352
  10.8 2.6 %collective-permute-start.3 = (bf16[272,512]{1,0:T(8,128)(2,1)S(1)}, bf16[272,512]{1,0:T(8,128)(2,1)}, u32[]{:S(2)}, u32[]{:S(2)}) collective-permute-start(bf16[272,512]{1,0:T(8,128)(2,1)S(1)} %get-tuple-element.33), channel_id=1, source_target_pairs={{0,8},{2,10},{4,12},{6,14},{8,0},{10,2},{12,4},{14,6},{1,9},{3,11}... | collective-permute-start | bytes 835592 | tf_op jit(solution)/shard_map/ppermute | solution.py:352
  14.1 0.5 collective-permute-start.9
  14.6 3.1 %multiply_reduce_fusion = f32[256]{0:T(256)S(1)} fusion(bf16[256,8192]{1,0:T(8,128)(2,1)} %refs_1_.3), kind=kLoop, calls=%fused_computation | loop fusion | flops 6291200 | bytes 4195328 | tf_op jit(solution)/shard_map/reduce_sum | solution.py:372
  17.7 7.7 %collective-permute-done.4.refs_7_ = bf16[272,512]{1,0:T(8,128)(2,1)S(1)} collective-permute-done((bf16[272,512]{1,0:T(8,128)(2,1)S(1)}, bf16[272,512]{1,0:T(8,128)(2,1)S(1)}, u32[]{:S(2)}, u32[]{:S(2)}) %collective-permute-start.4) | collective-permute-done | bytes 278560 | tf_op jit(solution)/shard_map/ppermute | solution.py:352
  25.4 0.3 collective-permute-start.8
  25.7 1.5 %collective-permute-start.6 = (bf16[272,512]{1,0:T(8,128)(2,1)S(1)}, bf16[272,512]{1,0:T(8,128)(2,1)}, u32[]{:S(2)}, u32[]{:S(2)}) collective-permute-start(bf16[272,512]{1,0:T(8,128)(2,1)S(1)} %collective-permute-done.4.refs_7_), channel_id=1, source_target_pairs={{0,16},{16,0},{1,17},{17,1},{2,18},{18,2},{3,19},{19,3},{4,20},{20... | collective-permute-start | bytes 835592 | tf_op jit(solution)/shard_map/ppermute | solution.py:355
  27.2 6.2 %collective-permute-done.9.refs_8_ = bf16[272,512]{1,0:T(8,128)(2,1)S(1)} collective-permute-done((bf16[272,512]{1,0:T(8,128)(2,1)S(1)}, bf16[272,512]{1,0:T(8,128)(2,1)S(1)}, u32[]{:S(2)}, u32[]{:S(2)}) %collective-permute-start.9) | collective-permute-done | bytes 278560 | tf_op jit(solution)/shard_map/ppermute | solution.py:352
  33.4 1.7 %collective-permute-start.10 = (bf16[272,512]{1,0:T(8,128)(2,1)S(1)}, bf16[272,512]{1,0:T(8,128)(2,1)}, u32[]{:S(2)}, u32[]{:S(2)}) collective-permute-start(bf16[272,512]{1,0:T(8,128)(2,1)S(1)} %collective-permute-done.9.refs_8_), channel_id=1, source_target_pairs={{0,16},{16,0},{1,17},{17,1},{2,18},{18,2},{3,19},{19,3},{4,20},{20... | collective-permute-start | bytes 835592 | tf_op jit(solution)/shard_map/ppermute | solution.py:355
  35.1 0.7 broadcast_select_fusion
  36.0 0.4 collective-permute-start.7
  36.4 2.2 %collective-permute-done.8.refs_10_ = bf16[272,512]{1,0:T(8,128)(2,1)} collective-permute-done((bf16[272,512]{1,0:T(8,128)(2,1)S(1)}, bf16[272,512]{1,0:T(8,128)(2,1)}, u32[]{:S(2)}, u32[]{:S(2)}) %collective-permute-start.8) | collective-permute-done | bytes 278560 | tf_op jit(solution)/shard_map/ppermute | solution.py:352
  38.6 3.3 %collective-permute-done.10.refs_14_ = bf16[272,512]{1,0:T(8,128)(2,1)} collective-permute-done((bf16[272,512]{1,0:T(8,128)(2,1)S(1)}, bf16[272,512]{1,0:T(8,128)(2,1)}, u32[]{:S(2)}, u32[]{:S(2)}) %collective-permute-start.10) | collective-permute-done | bytes 278560 | tf_op jit(solution)/shard_map/ppermute | solution.py:355
  42.0 1.7 %collective-permute-start.11 = (bf16[272,512]{1,0:T(8,128)(2,1)}, bf16[272,512]{1,0:T(8,128)(2,1)S(1)}, u32[]{:S(2)}, u32[]{:S(2)}) collective-permute-start(bf16[272,512]{1,0:T(8,128)(2,1)} %collective-permute-done.8.refs_10_), channel_id=1, source_target_pairs={{0,4},{2,6},{4,0},{6,2},{8,12},{10,14},{12,8},{14,10},{1,5},{3,7},... | collective-permute-start | bytes 835592 | tf_op jit(solution)/shard_map/ppermute | solution.py:352
  43.7 2.2 %fusion.5 = (f32[8,128,64]{2,1,0:T(8,128)S(1)}, f32[8,128,64]{2,1,0:T(8,128)S(1)}, f32[8,128,64]{2,1,0:T(8,128)S(1)}) fusion(f32[64]{0:T(128)S(1)} %multiply_power_fusion, f32[8,128]{1,0:T(8,128)S(1)} %add_convert_fusion), kind=kLoop, calls=%fused_computation.10 | loop fusion | flops 524288 | bytes 790784 | tf_op jit(solution)/shard_map/neg | solution.py:377
  45.9 0.3 pad_maximum_fusion
  46.2 1.6 %collective-permute-start.13 = (bf16[272,512]{1,0:T(8,128)(2,1)}, bf16[272,512]{1,0:T(8,128)(2,1)S(1)}, u32[]{:S(2)}, u32[]{:S(2)}) collective-permute-start(bf16[272,512]{1,0:T(8,128)(2,1)} %collective-permute-done.8.refs_10_), channel_id=1, source_target_pairs={{0,16},{16,0},{1,17},{17,1},{2,18},{18,2},{3,19},{19,3},{4,20},{20... | collective-permute-start | bytes 835592 | tf_op jit(solution)/shard_map/ppermute | solution.py:355
  47.8 1.0 collective-permute-done.11.refs_12_
  48.8 1.6 %collective-permute-start.12 = (bf16[272,512]{1,0:T(8,128)(2,1)S(1)}, bf16[272,512]{1,0:T(8,128)(2,1)S(1)}, u32[]{:S(2)}, u32[]{:S(2)}) collective-permute-start(bf16[272,512]{1,0:T(8,128)(2,1)S(1)} %collective-permute-done.5.refs_11_), channel_id=1, source_target_pairs={{0,16},{16,0},{1,17},{17,1},{2,18},{18,2},{3,19},{19,3},{4,20},{20... | collective-permute-start | bytes 835592 | tf_op jit(solution)/shard_map/ppermute | solution.py:355
  50.5 3.6 %collective-permute-done.2.refs_3_ = bf16[256,4096]{1,0:T(8,128)(2,1)} collective-permute-done((bf16[256,4096]{1,0:T(8,128)(2,1)S(1)}, bf16[256,4096]{1,0:T(8,128)(2,1)}, u32[]{:S(2)}, u32[]{:S(2)}) %collective-permute-start.2) | collective-permute-done | bytes 2097184 | tf_op jit(solution)/shard_map/ppermute | solution.py:349
  54.0 0.6 collective-permute-done.13.refs_16_
  54.7 3.0 %collective-permute-done.12.refs_17_ = bf16[272,512]{1,0:T(8,128)(2,1)S(1)} collective-permute-done((bf16[272,512]{1,0:T(8,128)(2,1)S(1)}, bf16[272,512]{1,0:T(8,128)(2,1)S(1)}, u32[]{:S(2)}, u32[]{:S(2)}) %collective-permute-start.12) | collective-permute-done | bytes 278560 | tf_op jit(solution)/shard_map/ppermute | solution.py:355
  57.7 0.9 collective-permute-start.15
  58.5 8.2 %collective-permute-done.15.refs_18_ = bf16[272,512]{1,0:T(8,128)(2,1)S(1)} collective-permute-done((bf16[272,512]{1,0:T(8,128)(2,1)S(1)}, bf16[272,512]{1,0:T(8,128)(2,1)S(1)}, u32[]{:S(2)}, u32[]{:S(2)}) %collective-permute-start.15) | collective-permute-done | bytes 278560 | tf_op jit(solution)/shard_map/ppermute | solution.py:355
  66.8 0.7 copy-done.16
  67.4 1.4 %copy-done.8 = bf16[256,4096]{1,0:T(8,128)(2,1)} copy-done((bf16[256,4096]{1,0:T(8,128)(2,1)}, bf16[256,4096]{1,0:T(8,128)(2,1)S(1)}, u32[]{:S(2)}) %copy-start.8) | copy-done | bytes 2097176
  68.8 6.7 %shard_map.88 = (f32[4,2,128,128]{3,2,1,0:T(8,128)}, bf16[4,2,128,128]{3,2,1,0:T(8,128)(2,1)}) custom-call(s32[8]{0:T(128)} %owner_ref.3, bf16[256,8192]{1,0:T(8,128)(2,1)} %refs_1_.3, bf16[256,8192]{1,0:T(8,128)(2,1)} %collective-permute-done.refs_2_, bf16[256,4096]{1,0:T(8,128)(2,1)} %collective-permute-done.2.refs_3_, bf16[256,4096]{1,0:T(8,128)(2,1)} %copy-done.8, ...), custom_call_target="tpu_custom_call" | custom-call | tf_op jit(solution)/shard_map/pallas_call | solution.py:267
  75.6 3.6 %collective-permute-start.16 = (bf16[4,2,128,128]{3,2,1,0:T(8,128)(2,1)}, bf16[4,2,128,128]{3,2,1,0:T(8,128)(2,1)S(1)}, u32[]{:S(2)}, u32[]{:S(2)}) collective-permute-start(bf16[4,2,128,128]{3,2,1,0:T(8,128)(2,1)} %get-tuple-element.46), channel_id=1, source_target_pairs={{0,2},{2,0},{4,6},{6,4},{8,10},{10,8},{12,14},{14,12},{1,3},{3,1},... | collective-permute-start | bytes 786440 | tf_op jit(solution)/shard_map/ppermute | solution.py:349
  79.3 6.7 %shard_map.91 = (f32[4,2,128,128]{3,2,1,0:T(8,128)}, bf16[4,2,128,128]{3,2,1,0:T(8,128)(2,1)}) custom-call(s32[8]{0:T(128)} %owner_ref.3, bf16[256,8192]{1,0:T(8,128)(2,1)} %refs_1_.3, bf16[256,8192]{1,0:T(8,128)(2,1)} %collective-permute-done.refs_2_, bf16[256,4096]{1,0:T(8,128)(2,1)} %collective-permute-done.2.refs_3_, bf16[256,4096]{1,0:T(8,128)(2,1)} %copy-done.8, ...), custom_call_target="tpu_custom_call" | custom-call | tf_op jit(solution)/shard_map/pallas_call | solution.py:267
  86.0 2.0 %collective-permute-start.22 = (bf16[4,2,128,128]{3,2,1,0:T(8,128)(2,1)}, bf16[4,2,128,128]{3,2,1,0:T(8,128)(2,1)S(1)}, u32[]{:S(2)}, u32[]{:S(2)}) collective-permute-start(bf16[4,2,128,128]{3,2,1,0:T(8,128)(2,1)} %get-tuple-element.53), channel_id=1, source_target_pairs={{0,2},{2,0},{4,6},{6,4},{8,10},{10,8},{12,14},{14,12},{1,3},{3,1},... | collective-permute-start | bytes 786440 | tf_op jit(solution)/shard_map/ppermute | solution.py:349
  88.1 1.1 %collective-permute-done.18 = f32[2,256]{1,0:T(2,128)S(1)} collective-permute-done((f32[2,256]{1,0:T(2,128)S(1)}, f32[2,256]{1,0:T(2,128)S(1)}, u32[]{:S(2)}, u32[]{:S(2)}) %collective-permute-start.18) | collective-permute-done | bytes 2080 | tf_op jit(solution)/shard_map/ppermute | solution.py:358
  89.5 0.8 shard_map.89
  90.4 2.8 %collective-permute-start.20 = (bf16[256,128]{1,0:T(8,128)(2,1)S(1)}, bf16[256,128]{1,0:T(8,128)(2,1)S(1)}, u32[]{:S(2)}, u32[]{:S(2)}) collective-permute-start(bf16[256,128]{1,0:T(8,128)(2,1)S(1)} %get-tuple-element.49), channel_id=1, source_target_pairs={{0,8},{2,10},{4,12},{6,14},{8,0},{10,2},{12,4},{14,6},{1,9},{3,11}... | collective-permute-start | bytes 196616 | tf_op jit(solution)/shard_map/ppermute | solution.py:352
  93.1 1.6 %collective-permute-start.21 = (bf16[256,128]{1,0:T(8,128)(2,1)S(1)}, bf16[256,128]{1,0:T(8,128)(2,1)S(1)}, u32[]{:S(2)}, u32[]{:S(2)}) collective-permute-start(bf16[256,128]{1,0:T(8,128)(2,1)S(1)} %get-tuple-element.50), channel_id=1, source_target_pairs={{0,12},{2,14},{4,8},{6,10},{8,4},{10,6},{12,0},{14,2},{1,13},{3,15... | collective-permute-start | bytes 196616 | tf_op jit(solution)/shard_map/ppermute | solution.py:352
  94.8 1.0 copy-done.4
  95.8 0.6 shard_map.92
  96.5 2.3 %collective-permute-start.25 = (bf16[256,128]{1,0:T(8,128)(2,1)S(1)}, bf16[256,128]{1,0:T(8,128)(2,1)S(1)}, u32[]{:S(2)}, u32[]{:S(2)}) collective-permute-start(bf16[256,128]{1,0:T(8,128)(2,1)S(1)} %get-tuple-element.59), channel_id=1, source_target_pairs={{0,12},{2,14},{4,8},{6,10},{8,4},{10,6},{12,0},{14,2},{1,13},{3,15... | collective-permute-start | bytes 196616 | tf_op jit(solution)/shard_map/ppermute | solution.py:352
  98.8 0.9 collective-permute-done.21.refs_3_
  99.7 4.0 %collective-permute-start.23 = (bf16[256,128]{1,0:T(8,128)(2,1)S(1)}, bf16[256,128]{1,0:T(8,128)(2,1)S(1)}, u32[]{:S(2)}, u32[]{:S(2)}) collective-permute-start(bf16[256,128]{1,0:T(8,128)(2,1)S(1)} %get-tuple-element.57), channel_id=1, source_target_pairs={{0,4},{2,6},{4,0},{6,2},{8,12},{10,14},{12,8},{14,10},{1,5},{3,7},... | collective-permute-start | bytes 196616 | tf_op jit(solution)/shard_map/ppermute | solution.py:352
  103.6 0.7 shard_map.90
  104.5 1.4 %collective-permute-done.23.refs_1_ = bf16[256,128]{1,0:T(8,128)(2,1)S(1)} collective-permute-done((bf16[256,128]{1,0:T(8,128)(2,1)S(1)}, bf16[256,128]{1,0:T(8,128)(2,1)S(1)}, u32[]{:S(2)}, u32[]{:S(2)}) %collective-permute-start.23) | collective-permute-done | bytes 65568 | tf_op jit(solution)/shard_map/ppermute | solution.py:352
  105.9 0.7 shard_map.93
  (62 shorter events, 1.2 us)
Async XLA Ops:
  0.6 13.5 %collective-permute-start = (bf16[256,8192]{1,0:T(8,128)(2,1)}, bf16[256,8192]{1,0:T(8,128)(2,1)}, u32[]{:S(2)}, u32[]{:S(2)}) collective-permute-start(bf16[256,8192]{1,0:T(8,128)(2,1)} %refs_1_.3), channel_id=1, source_target_pairs={{0,1},{1,0},{2,3},{3,2},{4,5},{5,4},{6,7},{7,6},{8,9},{9,8},{10,11... | collective-permute-start | bytes 12582920 | tf_op jit(solution)/shard_map/ppermute | solution.py:358
  1.1 5.0 %collective-permute-start.1 = (s32[1]{0:T(128)}, s32[1]{0:T(128)}, u32[]{:S(2)}, u32[]{:S(2)}) collective-permute-start(s32[1]{0:T(128)} %param.12), channel_id=1, source_target_pairs={{0,2},{2,0},{4,6},{6,4},{8,10},{10,8},{12,14},{14,12},{1,3},{3,1},... | collective-permute-start | bytes 20 | tf_op jit(solution)/shard_map/ppermute | solution.py:349
  3.7 2.2 %copy-start = (bf16[256,8192]{1,0:T(8,128)(2,1)S(1)}, bf16[256,8192]{1,0:T(8,128)(2,1)}, u32[]{:S(2)}) copy-start(bf16[256,8192]{1,0:T(8,128)(2,1)} %refs_1_.3) | copy-start | bytes 12582916
  5.9 2.2 %copy-start.2 = (bf16[1024,256]{1,0:T(8,128)(2,1)S(1)}, bf16[1024,256]{1,0:T(8,128)(2,1)}, u32[]{:S(2)}) copy-start(bf16[1024,256]{1,0:T(8,128)(2,1)} %refs_5_.1) | copy-start | bytes 1572868
  5.9 2.3 %copy-start.3 = (bf16[1024,256]{1,0:T(8,128)(2,1)S(1)}, bf16[1024,256]{1,0:T(8,128)(2,1)}, u32[]{:S(2)}) copy-start(bf16[1024,256]{1,0:T(8,128)(2,1)} %refs_5_.2) | copy-start | bytes 1572868
  5.9 2.3 %copy-start.6 = (bf16[80,1024]{1,0:T(8,128)(2,1)S(1)}, bf16[80,1024]{1,0:T(8,128)(2,1)}, u32[]{:S(2)}) copy-start(bf16[80,1024]{1,0:T(8,128)(2,1)} %gain_ref.1) | copy-start | bytes 491524
  6.2 47.9 %collective-permute-start.2 = (bf16[256,4096]{1,0:T(8,128)(2,1)S(1)}, bf16[256,4096]{1,0:T(8,128)(2,1)}, u32[]{:S(2)}, u32[]{:S(2)}) collective-permute-start(bf16[256,4096]{1,0:T(8,128)(2,1)S(1)} %shard_map.86), channel_id=1, source_target_pairs={{0,2},{2,0},{4,6},{6,4},{8,10},{10,8},{12,14},{14,12},{1,3},{3,1},... | collective-permute-start | bytes 6291464 | tf_op jit(solution)/shard_map/ppermute | solution.py:349
  8.4 0.8 copy-start.1
  9.2 16.2 %collective-permute-start.4 = (bf16[272,512]{1,0:T(8,128)(2,1)S(1)}, bf16[272,512]{1,0:T(8,128)(2,1)S(1)}, u32[]{:S(2)}, u32[]{:S(2)}) collective-permute-start(bf16[272,512]{1,0:T(8,128)(2,1)S(1)} %get-tuple-element.33), channel_id=1, source_target_pairs={{0,4},{2,6},{4,0},{6,2},{8,12},{10,14},{12,8},{14,10},{1,5},{3,7},... | collective-permute-start | bytes 835592 | tf_op jit(solution)/shard_map/ppermute | solution.py:352
  10.8 25.2 %collective-permute-start.3 = (bf16[272,512]{1,0:T(8,128)(2,1)S(1)}, bf16[272,512]{1,0:T(8,128)(2,1)}, u32[]{:S(2)}, u32[]{:S(2)}) collective-permute-start(bf16[272,512]{1,0:T(8,128)(2,1)S(1)} %get-tuple-element.33), channel_id=1, source_target_pairs={{0,8},{2,10},{4,12},{6,14},{8,0},{10,2},{12,4},{14,6},{1,9},{3,11}... | collective-permute-start | bytes 835592 | tf_op jit(solution)/shard_map/ppermute | solution.py:352
  14.1 19.3 %collective-permute-start.9 = (bf16[272,512]{1,0:T(8,128)(2,1)S(1)}, bf16[272,512]{1,0:T(8,128)(2,1)S(1)}, u32[]{:S(2)}, u32[]{:S(2)}) collective-permute-start(bf16[272,512]{1,0:T(8,128)(2,1)S(1)} %get-tuple-element.40), channel_id=1, source_target_pairs={{0,4},{2,6},{4,0},{6,2},{8,12},{10,14},{12,8},{14,10},{1,5},{3,7},... | collective-permute-start | bytes 835592 | tf_op jit(solution)/shard_map/ppermute | solution.py:352
  25.4 41.3 %copy-start.9 = (bf16[272,512]{1,0:T(8,128)(2,1)}, bf16[272,512]{1,0:T(8,128)(2,1)S(1)}, u32[]{:S(2)}) copy-start(bf16[272,512]{1,0:T(8,128)(2,1)S(1)} %collective-permute-done.4.refs_7_) | copy-start | bytes 835588
  25.4 13.2 %collective-permute-start.8 = (bf16[272,512]{1,0:T(8,128)(2,1)S(1)}, bf16[272,512]{1,0:T(8,128)(2,1)}, u32[]{:S(2)}, u32[]{:S(2)}) collective-permute-start(bf16[272,512]{1,0:T(8,128)(2,1)S(1)} %get-tuple-element.40), channel_id=1, source_target_pairs={{0,8},{2,10},{4,12},{6,14},{8,0},{10,2},{12,4},{14,6},{1,9},{3,11}... | collective-permute-start | bytes 835592 | tf_op jit(solution)/shard_map/ppermute | solution.py:352
  25.7 10.3 %collective-permute-start.6 = (bf16[272,512]{1,0:T(8,128)(2,1)S(1)}, bf16[272,512]{1,0:T(8,128)(2,1)}, u32[]{:S(2)}, u32[]{:S(2)}) collective-permute-start(bf16[272,512]{1,0:T(8,128)(2,1)S(1)} %collective-permute-done.4.refs_7_), channel_id=1, source_target_pairs={{0,16},{16,0},{1,17},{17,1},{2,18},{18,2},{3,19},{19,3},{4,20},{20... | collective-permute-start | bytes 835592 | tf_op jit(solution)/shard_map/ppermute | solution.py:355
  33.4 12.5 %copy-start.10 = (bf16[272,512]{1,0:T(8,128)(2,1)}, bf16[272,512]{1,0:T(8,128)(2,1)S(1)}, u32[]{:S(2)}) copy-start(bf16[272,512]{1,0:T(8,128)(2,1)S(1)} %collective-permute-done.9.refs_8_) | copy-start | bytes 835588
  33.4 8.6 %collective-permute-start.10 = (bf16[272,512]{1,0:T(8,128)(2,1)S(1)}, bf16[272,512]{1,0:T(8,128)(2,1)}, u32[]{:S(2)}, u32[]{:S(2)}) collective-permute-start(bf16[272,512]{1,0:T(8,128)(2,1)S(1)} %collective-permute-done.9.refs_8_), channel_id=1, source_target_pairs={{0,16},{16,0},{1,17},{17,1},{2,18},{18,2},{3,19},{19,3},{4,20},{20... | collective-permute-start | bytes 835592 | tf_op jit(solution)/shard_map/ppermute | solution.py:355
  36.0 11.8 %collective-permute-start.5 = (bf16[272,512]{1,0:T(8,128)(2,1)}, bf16[272,512]{1,0:T(8,128)(2,1)S(1)}, u32[]{:S(2)}, u32[]{:S(2)}) collective-permute-start(bf16[272,512]{1,0:T(8,128)(2,1)} %collective-permute-done.3.refs_9_), channel_id=1, source_target_pairs={{0,4},{2,6},{4,0},{6,2},{8,12},{10,14},{12,8},{14,10},{1,5},{3,7},... | collective-permute-start | bytes 835592 | tf_op jit(solution)/shard_map/ppermute | solution.py:352
  36.0 11.8 %collective-permute-start.7 = (bf16[272,512]{1,0:T(8,128)(2,1)}, bf16[272,512]{1,0:T(8,128)(2,1)S(1)}, u32[]{:S(2)}, u32[]{:S(2)}) collective-permute-start(bf16[272,512]{1,0:T(8,128)(2,1)} %collective-permute-done.3.refs_9_), channel_id=1, source_target_pairs={{0,16},{16,0},{1,17},{17,1},{2,18},{18,2},{3,19},{19,3},{4,20},{20... | collective-permute-start | bytes 835592 | tf_op jit(solution)/shard_map/ppermute | solution.py:355
  42.0 6.9 %collective-permute-start.11 = (bf16[272,512]{1,0:T(8,128)(2,1)}, bf16[272,512]{1,0:T(8,128)(2,1)S(1)}, u32[]{:S(2)}, u32[]{:S(2)}) collective-permute-start(bf16[272,512]{1,0:T(8,128)(2,1)} %collective-permute-done.8.refs_10_), channel_id=1, source_target_pairs={{0,4},{2,6},{4,0},{6,2},{8,12},{10,14},{12,8},{14,10},{1,5},{3,7},... | collective-permute-start | bytes 835592 | tf_op jit(solution)/shard_map/ppermute | solution.py:352
  46.2 8.5 %collective-permute-start.13 = (bf16[272,512]{1,0:T(8,128)(2,1)}, bf16[272,512]{1,0:T(8,128)(2,1)S(1)}, u32[]{:S(2)}, u32[]{:S(2)}) collective-permute-start(bf16[272,512]{1,0:T(8,128)(2,1)} %collective-permute-done.8.refs_10_), channel_id=1, source_target_pairs={{0,16},{16,0},{1,17},{17,1},{2,18},{18,2},{3,19},{19,3},{4,20},{20... | collective-permute-start | bytes 835592 | tf_op jit(solution)/shard_map/ppermute | solution.py:355
  47.8 19.0 %copy-start.11 = (bf16[272,512]{1,0:T(8,128)(2,1)}, bf16[272,512]{1,0:T(8,128)(2,1)S(1)}, u32[]{:S(2)}) copy-start(bf16[272,512]{1,0:T(8,128)(2,1)S(1)} %collective-permute-done.5.refs_11_) | copy-start | bytes 835588
  47.8 19.0 %copy-start.12 = (bf16[272,512]{1,0:T(8,128)(2,1)}, bf16[272,512]{1,0:T(8,128)(2,1)S(1)}, u32[]{:S(2)}) copy-start(bf16[272,512]{1,0:T(8,128)(2,1)S(1)} %collective-permute-done.7.refs_15_) | copy-start | bytes 835588
  48.8 9.7 %copy-start.13 = (bf16[272,512]{1,0:T(8,128)(2,1)}, bf16[272,512]{1,0:T(8,128)(2,1)S(1)}, u32[]{:S(2)}) copy-start(bf16[272,512]{1,0:T(8,128)(2,1)S(1)} %collective-permute-done.11.refs_12_) | copy-start | bytes 835588
  48.8 8.8 %collective-permute-start.12 = (bf16[272,512]{1,0:T(8,128)(2,1)S(1)}, bf16[272,512]{1,0:T(8,128)(2,1)S(1)}, u32[]{:S(2)}, u32[]{:S(2)}) collective-permute-start(bf16[272,512]{1,0:T(8,128)(2,1)S(1)} %collective-permute-done.5.refs_11_), channel_id=1, source_target_pairs={{0,16},{16,0},{1,17},{17,1},{2,18},{18,2},{3,19},{19,3},{4,20},{20... | collective-permute-start | bytes 835592 | tf_op jit(solution)/shard_map/ppermute | solution.py:355
  54.7 12.1 %copy-start.14 = (bf16[272,512]{1,0:T(8,128)(2,1)}, bf16[272,512]{1,0:T(8,128)(2,1)S(1)}, u32[]{:S(2)}) copy-start(bf16[272,512]{1,0:T(8,128)(2,1)S(1)} %collective-permute-done.13.refs_16_) | copy-start | bytes 835588
  57.7 9.1 %copy-start.15 = (bf16[272,512]{1,0:T(8,128)(2,1)}, bf16[272,512]{1,0:T(8,128)(2,1)S(1)}, u32[]{:S(2)}) copy-start(bf16[272,512]{1,0:T(8,128)(2,1)S(1)} %collective-permute-done.12.refs_17_) | copy-start | bytes 835588
  57.7 9.1 %collective-permute-start.14 = (bf16[256,4096]{1,0:T(8,128)(2,1)}, bf16[256,4096]{1,0:T(8,128)(2,1)S(1)}, u32[]{:S(2)}, u32[]{:S(2)}) collective-permute-start(bf16[256,4096]{1,0:T(8,128)(2,1)} %collective-permute-done.2.refs_3_), channel_id=1, source_target_pairs={{0,1},{1,0},{2,3},{3,2},{4,5},{5,4},{6,7},{7,6},{8,9},{9,8},{10,11... | collective-permute-start | bytes 6291464 | tf_op jit(solution)/shard_map/ppermute | solution.py:358
  57.7 9.1 %collective-permute-start.15 = (bf16[272,512]{1,0:T(8,128)(2,1)S(1)}, bf16[272,512]{1,0:T(8,128)(2,1)S(1)}, u32[]{:S(2)}, u32[]{:S(2)}) collective-permute-start(bf16[272,512]{1,0:T(8,128)(2,1)S(1)} %collective-permute-done.11.refs_12_), channel_id=1, source_target_pairs={{0,16},{16,0},{1,17},{17,1},{2,18},{18,2},{3,19},{19,3},{4,20},{20... | collective-permute-start | bytes 835592 | tf_op jit(solution)/shard_map/ppermute | solution.py:355
  66.7 0.7 copy-start.16
  67.4 1.4 %copy-start.8 = (bf16[256,4096]{1,0:T(8,128)(2,1)}, bf16[256,4096]{1,0:T(8,128)(2,1)S(1)}, u32[]{:S(2)}) copy-start(bf16[256,4096]{1,0:T(8,128)(2,1)S(1)} %collective-permute-done.14.refs_4_) | copy-start | bytes 6291460
  75.6 14.0 %copy-start.5 = (f32[4,2,128,128]{3,2,1,0:T(8,128)S(1)}, f32[4,2,128,128]{3,2,1,0:T(8,128)}, u32[]{:S(2)}) copy-start(f32[4,2,128,128]{3,2,1,0:T(8,128)} %get-tuple-element.45.keep_ref) | copy-start | bytes 1572868
  75.6 14.0 %copy-start.7 = (s32[8]{0:T(128)S(1)}, s32[8]{0:T(128)}, u32[]{:S(2)}) copy-start(s32[8]{0:T(128)} %owner_ref.3) | copy-start | bytes 100
  75.6 13.7 %collective-permute-start.16 = (bf16[4,2,128,128]{3,2,1,0:T(8,128)(2,1)}, bf16[4,2,128,128]{3,2,1,0:T(8,128)(2,1)S(1)}, u32[]{:S(2)}, u32[]{:S(2)}) collective-permute-start(bf16[4,2,128,128]{3,2,1,0:T(8,128)(2,1)} %get-tuple-element.46), channel_id=1, source_target_pairs={{0,2},{2,0},{4,6},{6,4},{8,10},{10,8},{12,14},{14,12},{1,3},{3,1},... | collective-permute-start | bytes 786440 | tf_op jit(solution)/shard_map/ppermute | solution.py:349
  79.2 8.8 %collective-permute-start.17 = (f32[256]{0:T(256)S(1)}, f32[256]{0:T(256)S(1)}, u32[]{:S(2)}, u32[]{:S(2)}) collective-permute-start(f32[256]{0:T(256)S(1)} %multiply_reduce_fusion), channel_id=1, source_target_pairs={{0,2},{2,0},{4,6},{6,4},{8,10},{10,8},{12,14},{14,12},{1,3},{3,1},... | collective-permute-start | bytes 3080 | tf_op jit(solution)/shard_map/ppermute | solution.py:349
  86.0 8.7 %collective-permute-start.22 = (bf16[4,2,128,128]{3,2,1,0:T(8,128)(2,1)}, bf16[4,2,128,128]{3,2,1,0:T(8,128)(2,1)S(1)}, u32[]{:S(2)}, u32[]{:S(2)}) collective-permute-start(bf16[4,2,128,128]{3,2,1,0:T(8,128)(2,1)} %get-tuple-element.53), channel_id=1, source_target_pairs={{0,2},{2,0},{4,6},{6,4},{8,10},{10,8},{12,14},{14,12},{1,3},{3,1},... | collective-permute-start | bytes 786440 | tf_op jit(solution)/shard_map/ppermute | solution.py:349
  88.0 1.2 %collective-permute-start.18 = (f32[2,256]{1,0:T(2,128)S(1)}, f32[2,256]{1,0:T(2,128)S(1)}, u32[]{:S(2)}, u32[]{:S(2)}) collective-permute-start(f32[2,256]{1,0:T(2,128)S(1)} %get-tuple-element.64), channel_id=1, source_target_pairs={{0,1},{1,0},{2,3},{3,2},{4,5},{5,4},{6,7},{7,6},{8,9},{9,8},{10,11... | collective-permute-start | bytes 6152 | tf_op jit(solution)/shard_map/ppermute | solution.py:358
  90.3 8.5 %collective-permute-start.19 = (bf16[256,128]{1,0:T(8,128)(2,1)S(1)}, bf16[256,128]{1,0:T(8,128)(2,1)S(1)}, u32[]{:S(2)}, u32[]{:S(2)}) collective-permute-start(bf16[256,128]{1,0:T(8,128)(2,1)S(1)} %get-tuple-element.48), channel_id=1, source_target_pairs={{0,4},{2,6},{4,0},{6,2},{8,12},{10,14},{12,8},{14,10},{1,5},{3,7},... | collective-permute-start | bytes 196616 | tf_op jit(solution)/shard_map/ppermute | solution.py:352
  90.4 8.4 %collective-permute-start.20 = (bf16[256,128]{1,0:T(8,128)(2,1)S(1)}, bf16[256,128]{1,0:T(8,128)(2,1)S(1)}, u32[]{:S(2)}, u32[]{:S(2)}) collective-permute-start(bf16[256,128]{1,0:T(8,128)(2,1)S(1)} %get-tuple-element.49), channel_id=1, source_target_pairs={{0,8},{2,10},{4,12},{6,14},{8,0},{10,2},{12,4},{14,6},{1,9},{3,11}... | collective-permute-start | bytes 196616 | tf_op jit(solution)/shard_map/ppermute | solution.py:352
  93.1 6.5 %collective-permute-start.21 = (bf16[256,128]{1,0:T(8,128)(2,1)S(1)}, bf16[256,128]{1,0:T(8,128)(2,1)S(1)}, u32[]{:S(2)}, u32[]{:S(2)}) collective-permute-start(bf16[256,128]{1,0:T(8,128)(2,1)S(1)} %get-tuple-element.50), channel_id=1, source_target_pairs={{0,12},{2,14},{4,8},{6,10},{8,4},{10,6},{12,0},{14,2},{1,13},{3,15... | collective-permute-start | bytes 196616 | tf_op jit(solution)/shard_map/ppermute | solution.py:352
  94.7 1.0 copy-start.4
  96.4 8.1 %collective-permute-start.24 = (bf16[256,128]{1,0:T(8,128)(2,1)S(1)}, bf16[256,128]{1,0:T(8,128)(2,1)S(1)}, u32[]{:S(2)}, u32[]{:S(2)}) collective-permute-start(bf16[256,128]{1,0:T(8,128)(2,1)S(1)} %get-tuple-element.58), channel_id=1, source_target_pairs={{0,8},{2,10},{4,12},{6,14},{8,0},{10,2},{12,4},{14,6},{1,9},{3,11}... | collective-permute-start | bytes 196616 | tf_op jit(solution)/shard_map/ppermute | solution.py:352
  96.5 8.0 %collective-permute-start.25 = (bf16[256,128]{1,0:T(8,128)(2,1)S(1)}, bf16[256,128]{1,0:T(8,128)(2,1)S(1)}, u32[]{:S(2)}, u32[]{:S(2)}) collective-permute-start(bf16[256,128]{1,0:T(8,128)(2,1)S(1)} %get-tuple-element.59), channel_id=1, source_target_pairs={{0,12},{2,14},{4,8},{6,10},{8,4},{10,6},{12,0},{14,2},{1,13},{3,15... | collective-permute-start | bytes 196616 | tf_op jit(solution)/shard_map/ppermute | solution.py:352
  99.7 6.2 %collective-permute-start.23 = (bf16[256,128]{1,0:T(8,128)(2,1)S(1)}, bf16[256,128]{1,0:T(8,128)(2,1)S(1)}, u32[]{:S(2)}, u32[]{:S(2)}) collective-permute-start(bf16[256,128]{1,0:T(8,128)(2,1)S(1)} %get-tuple-element.57), channel_id=1, source_target_pairs={{0,4},{2,6},{4,0},{6,2},{8,12},{10,14},{12,8},{14,10},{1,5},{3,7},... | collective-permute-start | bytes 196616 | tf_op jit(solution)/shard_map/ppermute | solution.py:352

commit v4 on v3

--- a/solution.py
+++ b/solution.py
@@ -10,7 +10,7 @@
 
 HD = 128
 GAIN_ROWS = 16
-VMEM_LIMIT = 58 * 2**20
+VMEM_LIMIT = 61 * 2**20
 SMALL_VMEM_LIMIT = 8 * 2**20
 
 
@@ -358,9 +358,8 @@
         return lax.ppermute(values, "col", [(0, 1), (1, 0)])
 
     other = over_c(hidden)
-    pair_offset = over_x(offsets)
     away = away_half(hidden, shard)
-    own_away = over_x(after(away, pair_offset))
+    own_away = over_x(away)
     *pieces, packed = pack_weights(layer_id, after(w_key, away), w_value, gain_table)
     near_0 = over_z(pieces[0], 1)
     far_0 = over_z(pieces[0], 2)
@@ -370,30 +369,35 @@
 
     wide = after(hidden, packed).astype(jnp.float32)
     own_squares = jnp.sum(wide * wide, axis=1)
-    starts = jnp.where(x == 0, jnp.stack([offsets, pair_offset]), jnp.stack([pair_offset, offsets]))
-    position = (starts + jnp.arange(2 * device_rows, dtype=jnp.int32)[None, :]).reshape(-1)
-    cosine, sine = rotary_table(position, HD)
-    cosine = jnp.concatenate([cosine, cosine], axis=1).reshape(8, page, HD)
-    sine = jnp.concatenate([-sine, sine], axis=1).reshape(8, page, HD)
-
     corner_0 = over_z(after(far_0, near_0, own_squares), 1)
     near_y_1 = over_y(near_1)
     far_y_0 = over_y(after(far_0, near_y_0))
     corner_1 = over_z(after(far_1, near_y_1), 1)
     far_y_1 = over_y(after(far_1, near_y_1))
-    corner_y_0 = over_y(after(corner_0, far_y_0, corner_1, cosine, sine))
+    corner_y_0 = over_y(after(corner_0, far_y_0, corner_1))
     corner_y_1 = over_y(after(corner_1, far_y_1))
-    other_away = over_c(after(own_away, corner_y_0, far_y_1))
-
-    pair_squares = jnp.stack([own_squares, over_x(own_squares)])
-    squares = jnp.stack([pair_squares, over_c(pair_squares)], axis=1).reshape(4, device_rows)
+    start = jnp.broadcast_to(offsets[0].astype(jnp.float32), (device_rows,))
+    own_facts = jnp.stack([own_squares, start])
+    came_facts = over_x(after(own_facts, own_away))
+    pair_facts = jnp.stack([own_facts, came_facts])
+    other_away = over_c(after(own_away, corner_y_0, far_y_1, came_facts))
+
+    starts = jnp.where(x == 0, pair_facts[:, 1, 0], pair_facts[::-1, 1, 0]).astype(jnp.int32)
+    position = (starts[:, None] + jnp.arange(2 * device_rows, dtype=jnp.int32)).reshape(-1)
+    cosine, sine = rotary_table(position, HD)
+    cosine = jnp.concatenate([cosine, cosine], axis=1).reshape(8, page, HD)
+    sine = jnp.concatenate([-sine, sine], axis=1).reshape(8, page, HD)
+    pair_squares = pair_facts[:, 0]
+    squares = jnp.stack([pair_squares, over_c(after(pair_squares, corner_y_1))], axis=1).reshape(4, device_rows)
     scale = lax.rsqrt(squares / hidden.shape[1] + 1e-05)
     scale = jnp.broadcast_to(scale[:, :, None], (4, device_rows, HD))
 
     sources = [hidden, other, own_away, other_away]
     mine = [[packed], [near_0, near_1], [far_0, far_1], [corner_0, corner_1]]
     theirs = [[near_y_0, near_y_1], [far_y_0, far_y_1], [corner_y_0, corner_y_1]]
-    key_keep, key_send = multiply(owner_map, sources, w_key, 0, mine, theirs)
+    key_keep, key_send = multiply(
+        owner_map, sources, after(w_key, scale, cosine, sine), 0, mine, theirs
+    )
     key_came = over_x(key_send)
     value_keep, value_send = multiply(
         owner_map, sources, after(w_value, key_send), 1, mine, theirs

time: 107 us -> 103 us (0.963)
  waiting for transfers between devices: 39.4 us -> 44.2 us
  starting transfers between devices: 35.3 us -> 31.7 us
  other arithmetic: 6.4 us -> 3.65 us
  local copies, waits for them, and re-layouts: 6.54 us -> 4.51 us
    ppermute x12, waiting for transfers between devices: 19.5 us -> 30.1 us  [over_z(): lax.ppermute(values, 'tok', [(t, t ^ 2 * distance) for t in range(tok_cou...]
    ppermute x6, waiting for transfers between devices: 15.2 us -> 8.64 us  [over_y(): return lax.ppermute(values, 'group', [(0, 1), (1, 0)])]
    ppermute x5 -> x4, starting transfers between devices: 9.63 us -> 5.48 us  [over_x(): return lax.ppermute(values, 'tok', [(t, t ^ 1) for t in range(tok_count)])]
    reduce_sum x1, other arithmetic: 3.1 us -> 0.92 us  [paired_shards(): own_squares = jnp.sum(wide * wide, axis=1)]
    unnamed x34 -> x45, local copies, waits for them, and re-layouts: 6.16 us -> 4.12 us
    ppermute x6, starting transfers between devices: 7.67 us -> 9.07 us  [over_y(): return lax.ppermute(values, 'group', [(0, 1), (1, 0)])]
    ppermute x5 -> x4, waiting for transfers between devices: 3.57 us -> 4.71 us  [over_x(): return lax.ppermute(values, 'tok', [(t, t ^ 1) for t in range(tok_count)])]
  transfers between devices with their start and end apart: 26 -> 25, of which waited for: 13 -> 13; matrix products, arithmetic and copies ran while one was open for 6% -> 4% of each run, Pallas kernels for 9% -> 9%
where the time goes in v4:
time: 103 us
  waiting for transfers between devices  44.2 us (43%)
  starting transfers between devices  31.7 us (31%)
  Pallas kernels  16.8 us (16%)
  local copies, waits for them, and re-layouts  4.51 us (4%)
  other arithmetic  3.65 us (4%)
  between operations  2.24 us (2%)
    ppermute x12, waiting for transfers between devices, over_z(): lax.ppermute(values, 'tok', [(t, t ^ 2 * distance) for t in range(tok_cou...  30.1 us
    ppermute x12, starting transfers between devices, over_z(): lax.ppermute(values, 'tok', [(t, t ^ 2 * distance) for t in range(tok_cou...  16.6 us
    pallas_call x2, Pallas kernels, multiply(): pl.pallas_call(functools.partial(multiply_kernel, shard, counts, which),...  13.5 us
    ppermute x6, starting transfers between devices, over_y(): return lax.ppermute(values, 'group', [(0, 1), (1, 0)])  9.07 us
    ppermute x6, waiting for transfers between devices, over_y(): return lax.ppermute(values, 'group', [(0, 1), (1, 0)])  8.64 us
    ppermute x4, starting transfers between devices, over_x(): return lax.ppermute(values, 'tok', [(t, t ^ 1) for t in range(tok_count)])  5.48 us
    ppermute x4, waiting for transfers between devices, over_x(): return lax.ppermute(values, 'tok', [(t, t ^ 1) for t in range(tok_count)])  4.71 us
    unnamed x45, local copies, waits for them, and re-layouts  4.12 us
  transfers between devices with their start and end apart: 25, of which 13 were waited for; matrix products, arithmetic and copies ran while one was open for 4% of the time, Pallas kernels for 9%

profile of v4, /device:TPU:0, one launch (start us, length us, event | category | flops | bytes accessed | tf_op | source)
XLA Modules:
  0.0 103.1 jit_solution(7714569909546332489)
XLA Ops:
  0.6 0.5 collective-permute-start
  1.1 2.2 %copy-done = bf16[256,8192]{1,0:T(8,128)(2,1)S(1)} copy-done((bf16[256,8192]{1,0:T(8,128)(2,1)S(1)}, bf16[256,8192]{1,0:T(8,128)(2,1)}, u32[]{:S(2)}) %copy-start) | copy-done | bytes 4194328
  3.6 2.6 %collective-permute-start.1 = (bf16[256,4096]{1,0:T(8,128)(2,1)S(1)}, bf16[256,4096]{1,0:T(8,128)(2,1)}, u32[]{:S(2)}, u32[]{:S(2)}) collective-permute-start(bf16[256,4096]{1,0:T(8,128)(2,1)S(1)} %shard_map.86), channel_id=1, source_target_pairs={{0,2},{2,0},{4,6},{6,4},{8,10},{10,8},{12,14},{14,12},{1,3},{3,1},... | collective-permute-start | bytes 6291464 | tf_op jit(solution)/shard_map/ppermute | solution.py:349
  7.1 0.8 copy-done.2
  7.9 1.6 %collective-permute-start.3 = (bf16[272,512]{1,0:T(8,128)(2,1)S(1)}, bf16[272,512]{1,0:T(8,128)(2,1)S(1)}, u32[]{:S(2)}, u32[]{:S(2)}) collective-permute-start(bf16[272,512]{1,0:T(8,128)(2,1)S(1)} %get-tuple-element.34), channel_id=1, source_target_pairs={{0,4},{2,6},{4,0},{6,2},{8,12},{10,14},{12,8},{14,10},{1,5},{3,7},... | collective-permute-start | bytes 835592 | tf_op jit(solution)/shard_map/ppermute | solution.py:352
  9.5 1.6 %collective-permute-start.8 = (bf16[272,512]{1,0:T(8,128)(2,1)S(1)}, bf16[272,512]{1,0:T(8,128)(2,1)S(1)}, u32[]{:S(2)}, u32[]{:S(2)}) collective-permute-start(bf16[272,512]{1,0:T(8,128)(2,1)S(1)} %get-tuple-element.41), channel_id=1, source_target_pairs={{0,4},{2,6},{4,0},{6,2},{8,12},{10,14},{12,8},{14,10},{1,5},{3,7},... | collective-permute-start | bytes 835592 | tf_op jit(solution)/shard_map/ppermute | solution.py:352
  11.1 2.6 %collective-permute-start.2 = (bf16[272,512]{1,0:T(8,128)(2,1)S(1)}, bf16[272,512]{1,0:T(8,128)(2,1)S(1)}, u32[]{:S(2)}, u32[]{:S(2)}) collective-permute-start(bf16[272,512]{1,0:T(8,128)(2,1)S(1)} %get-tuple-element.34), channel_id=1, source_target_pairs={{0,8},{2,10},{4,12},{6,14},{8,0},{10,2},{12,4},{14,6},{1,9},{3,11}... | collective-permute-start | bytes 835592 | tf_op jit(solution)/shard_map/ppermute | solution.py:352
  13.7 9.7 %collective-permute-done.3.refs_7_ = bf16[272,512]{1,0:T(8,128)(2,1)S(1)} collective-permute-done((bf16[272,512]{1,0:T(8,128)(2,1)S(1)}, bf16[272,512]{1,0:T(8,128)(2,1)S(1)}, u32[]{:S(2)}, u32[]{:S(2)}) %collective-permute-start.3) | collective-permute-done | bytes 278560 | tf_op jit(solution)/shard_map/ppermute | solution.py:352
  23.4 1.7 %collective-permute-start.7 = (bf16[272,512]{1,0:T(8,128)(2,1)S(1)}, bf16[272,512]{1,0:T(8,128)(2,1)S(1)}, u32[]{:S(2)}, u32[]{:S(2)}) collective-permute-start(bf16[272,512]{1,0:T(8,128)(2,1)S(1)} %get-tuple-element.41), channel_id=1, source_target_pairs={{0,8},{2,10},{4,12},{6,14},{8,0},{10,2},{12,4},{14,6},{1,9},{3,11}... | collective-permute-start | bytes 835592 | tf_op jit(solution)/shard_map/ppermute | solution.py:352
  25.1 1.5 %collective-permute-start.5 = (bf16[272,512]{1,0:T(8,128)(2,1)S(1)}, bf16[272,512]{1,0:T(8,128)(2,1)S(1)}, u32[]{:S(2)}, u32[]{:S(2)}) collective-permute-start(bf16[272,512]{1,0:T(8,128)(2,1)S(1)} %collective-permute-done.3.refs_7_), channel_id=1, source_target_pairs={{0,16},{16,0},{1,17},{17,1},{2,18},{18,2},{3,19},{19,3},{4,20},{20... | collective-permute-start | bytes 835592 | tf_op jit(solution)/shard_map/ppermute | solution.py:355
  26.6 2.2 %collective-permute-done.8.refs_8_ = bf16[272,512]{1,0:T(8,128)(2,1)S(1)} collective-permute-done((bf16[272,512]{1,0:T(8,128)(2,1)S(1)}, bf16[272,512]{1,0:T(8,128)(2,1)S(1)}, u32[]{:S(2)}, u32[]{:S(2)}) %collective-permute-start.8) | collective-permute-done | bytes 278560 | tf_op jit(solution)/shard_map/ppermute | solution.py:352
  28.7 1.6 %collective-permute-start.9 = (bf16[272,512]{1,0:T(8,128)(2,1)S(1)}, bf16[272,512]{1,0:T(8,128)(2,1)S(1)}, u32[]{:S(2)}, u32[]{:S(2)}) collective-permute-start(bf16[272,512]{1,0:T(8,128)(2,1)S(1)} %collective-permute-done.8.refs_8_), channel_id=1, source_target_pairs={{0,16},{16,0},{1,17},{17,1},{2,18},{18,2},{3,19},{19,3},{4,20},{20... | collective-permute-start | bytes 835592 | tf_op jit(solution)/shard_map/ppermute | solution.py:355
  30.3 0.9 multiply_reduce_fusion
  31.2 0.8 collective-permute-start.4
  32.0 1.4 %collective-permute-done.5.refs_13_ = bf16[272,512]{1,0:T(8,128)(2,1)S(1)} collective-permute-done((bf16[272,512]{1,0:T(8,128)(2,1)S(1)}, bf16[272,512]{1,0:T(8,128)(2,1)S(1)}, u32[]{:S(2)}, u32[]{:S(2)}) %collective-permute-start.5) | collective-permute-done | bytes 278560 | tf_op jit(solution)/shard_map/ppermute | solution.py:355
  33.4 1.4 %collective-permute-start.6 = (bf16[272,512]{1,0:T(8,128)(2,1)S(1)}, bf16[272,512]{1,0:T(8,128)(2,1)S(1)}, u32[]{:S(2)}, u32[]{:S(2)}) collective-permute-start(bf16[272,512]{1,0:T(8,128)(2,1)S(1)} %collective-permute-done.2.refs_9_), channel_id=1, source_target_pairs={{0,16},{16,0},{1,17},{17,1},{2,18},{18,2},{3,19},{19,3},{4,20},{20... | collective-permute-start | bytes 835592 | tf_op jit(solution)/shard_map/ppermute | solution.py:355
  34.8 8.0 %collective-permute-done.7.refs_10_ = bf16[272,512]{1,0:T(8,128)(2,1)S(1)} collective-permute-done((bf16[272,512]{1,0:T(8,128)(2,1)S(1)}, bf16[272,512]{1,0:T(8,128)(2,1)S(1)}, u32[]{:S(2)}, u32[]{:S(2)}) %collective-permute-start.7) | collective-permute-done | bytes 278560 | tf_op jit(solution)/shard_map/ppermute | solution.py:352
  42.8 0.3 collective-permute-start.10
  43.1 1.5 %collective-permute-start.12 = (bf16[272,512]{1,0:T(8,128)(2,1)S(1)}, bf16[272,512]{1,0:T(8,128)(2,1)S(1)}, u32[]{:S(2)}, u32[]{:S(2)}) collective-permute-start(bf16[272,512]{1,0:T(8,128)(2,1)S(1)} %collective-permute-done.7.refs_10_), channel_id=1, source_target_pairs={{0,16},{16,0},{1,17},{17,1},{2,18},{18,2},{3,19},{19,3},{4,20},{20... | collective-permute-start | bytes 835592 | tf_op jit(solution)/shard_map/ppermute | solution.py:355
  44.6 0.4 collective-permute-done.4.refs_11_
  45.0 6.3 %collective-permute-done.10.refs_12_ = bf16[272,512]{1,0:T(8,128)(2,1)S(1)} collective-permute-done((bf16[272,512]{1,0:T(8,128)(2,1)S(1)}, bf16[272,512]{1,0:T(8,128)(2,1)S(1)}, u32[]{:S(2)}, u32[]{:S(2)}) %collective-permute-start.10) | collective-permute-done | bytes 278560 | tf_op jit(solution)/shard_map/ppermute | solution.py:352
  51.3 1.5 %collective-permute-start.11 = (bf16[272,512]{1,0:T(8,128)(2,1)S(1)}, bf16[272,512]{1,0:T(8,128)(2,1)S(1)}, u32[]{:S(2)}, u32[]{:S(2)}) collective-permute-start(bf16[272,512]{1,0:T(8,128)(2,1)S(1)} %collective-permute-done.4.refs_11_), channel_id=1, source_target_pairs={{0,16},{16,0},{1,17},{17,1},{2,18},{18,2},{3,19},{19,3},{4,20},{20... | collective-permute-start | bytes 835592 | tf_op jit(solution)/shard_map/ppermute | solution.py:355
  53.5 0.8 collective-permute-start.13
  54.3 2.9 %collective-permute-done.13 = f32[2,256]{1,0:T(2,128)S(1)} collective-permute-done((f32[2,256]{1,0:T(2,128)S(1)}, f32[2,256]{1,0:T(2,128)S(1)}, u32[]{:S(2)}, u32[]{:S(2)}) %collective-permute-start.13) | collective-permute-done | bytes 2080 | tf_op jit(solution)/shard_map/ppermute | solution.py:349
  57.2 1.9 %collective-permute-done.11.refs_17_ = bf16[272,512]{1,0:T(8,128)(2,1)S(1)} collective-permute-done((bf16[272,512]{1,0:T(8,128)(2,1)S(1)}, bf16[272,512]{1,0:T(8,128)(2,1)S(1)}, u32[]{:S(2)}, u32[]{:S(2)}) %collective-permute-start.11) | collective-permute-done | bytes 278560 | tf_op jit(solution)/shard_map/ppermute | solution.py:355
  59.6 1.5 %collective-permute-start.15 = (bf16[272,512]{1,0:T(8,128)(2,1)S(1)}, bf16[272,512]{1,0:T(8,128)(2,1)S(1)}, u32[]{:S(2)}, u32[]{:S(2)}) collective-permute-start(bf16[272,512]{1,0:T(8,128)(2,1)S(1)} %collective-permute-done.10.refs_12_), channel_id=1, source_target_pairs={{0,16},{16,0},{1,17},{17,1},{2,18},{18,2},{3,19},{19,3},{4,20},{20... | collective-permute-start | bytes 835592 | tf_op jit(solution)/shard_map/ppermute | solution.py:355
  61.1 2.2 %fusion.5 = (f32[8,128,64]{2,1,0:T(8,128)S(1)}, f32[8,128,64]{2,1,0:T(8,128)S(1)}, f32[8,128,64]{2,1,0:T(8,128)S(1)}) fusion(f32[64]{0:T(128)S(1)} %multiply_power_fusion, f32[8,128]{1,0:T(8,128)S(1)} %add_convert_fusion), kind=kLoop, calls=%fused_computation.10 | loop fusion | flops 524288 | bytes 790784 | tf_op jit(solution)/shard_map/neg | solution.py:389
  63.3 5.3 %collective-permute-done.15.refs_18_ = bf16[272,512]{1,0:T(8,128)(2,1)S(1)} collective-permute-done((bf16[272,512]{1,0:T(8,128)(2,1)S(1)}, bf16[272,512]{1,0:T(8,128)(2,1)S(1)}, u32[]{:S(2)}, u32[]{:S(2)}) %collective-permute-start.15) | collective-permute-done | bytes 278560 | tf_op jit(solution)/shard_map/ppermute | solution.py:355
  68.6 0.3 pad_maximum_fusion
  69.0 0.8 collective-permute-done.16
  70.1 6.7 %shard_map.88 = (f32[4,2,128,128]{3,2,1,0:T(8,128)}, bf16[4,2,128,128]{3,2,1,0:T(8,128)(2,1)}) custom-call(s32[8]{0:T(128)} %owner_ref.3, bf16[256,8192]{1,0:T(8,128)(2,1)} %refs_1_.3, bf16[256,8192]{1,0:T(8,128)(2,1)} %copy-done.9, bf16[256,4096]{1,0:T(8,128)(2,1)} %collective-permute-done.1.refs_3_, bf16[256,4096]{1,0:T(8,128)(2,1)} %collective-permute-done.14.refs_4_, ...), custom_call_target="tpu_custom_call" | custom-call | tf_op jit(solution)/shard_map/pallas_call | solution.py:267
  76.8 0.8 collective-permute-start.17
  77.7 6.7 %shard_map.91 = (f32[4,2,128,128]{3,2,1,0:T(8,128)}, bf16[4,2,128,128]{3,2,1,0:T(8,128)(2,1)}) custom-call(s32[8]{0:T(128)} %owner_ref.3, bf16[256,8192]{1,0:T(8,128)(2,1)} %refs_1_.3, bf16[256,8192]{1,0:T(8,128)(2,1)} %copy-done.9, bf16[256,4096]{1,0:T(8,128)(2,1)} %collective-permute-done.1.refs_3_, bf16[256,4096]{1,0:T(8,128)(2,1)} %collective-permute-done.14.refs_4_, ...), custom_call_target="tpu_custom_call" | custom-call | tf_op jit(solution)/shard_map/pallas_call | solution.py:267
  84.4 1.3 %collective-permute-start.21 = (bf16[4,2,128,128]{3,2,1,0:T(8,128)(2,1)}, bf16[4,2,128,128]{3,2,1,0:T(8,128)(2,1)S(1)}, u32[]{:S(2)}, u32[]{:S(2)}) collective-permute-start(bf16[4,2,128,128]{3,2,1,0:T(8,128)(2,1)} %get-tuple-element.57), channel_id=1, source_target_pairs={{0,2},{2,0},{4,6},{6,4},{8,10},{10,8},{12,14},{14,12},{1,3},{3,1},... | collective-permute-start | bytes 786440 | tf_op jit(solution)/shard_map/ppermute | solution.py:349
  85.7 0.8 shard_map.89
  86.5 0.4 collective-permute-start.18
  86.9 3.3 %collective-permute-start.19 = (bf16[256,128]{1,0:T(8,128)(2,1)S(1)}, bf16[256,128]{1,0:T(8,128)(2,1)S(1)}, u32[]{:S(2)}, u32[]{:S(2)}) collective-permute-start(bf16[256,128]{1,0:T(8,128)(2,1)S(1)} %get-tuple-element.53), channel_id=1, source_target_pairs={{0,8},{2,10},{4,12},{6,14},{8,0},{10,2},{12,4},{14,6},{1,9},{3,11}... | collective-permute-start | bytes 196616 | tf_op jit(solution)/shard_map/ppermute | solution.py:352
  90.1 0.8 collective-permute-start.20
  90.9 1.8 %collective-permute-done.21.came_ref = bf16[4,2,128,128]{3,2,1,0:T(8,128)(2,1)S(1)} collective-permute-done((bf16[4,2,128,128]{3,2,1,0:T(8,128)(2,1)}, bf16[4,2,128,128]{3,2,1,0:T(8,128)(2,1)S(1)}, u32[]{:S(2)}, u32[]{:S(2)}) %collective-permute-start.21) | collective-permute-done | bytes 262176 | tf_op jit(solution)/shard_map/ppermute | solution.py:349
  92.8 1.0 %copy-done.5 = f32[4,2,128,128]{3,2,1,0:T(8,128)S(1)} copy-done((f32[4,2,128,128]{3,2,1,0:T(8,128)S(1)}, f32[4,2,128,128]{3,2,1,0:T(8,128)}, u32[]{:S(2)}) %copy-start.5) | copy-done | bytes 524312
  93.8 0.6 shard_map.92
  94.4 0.8 collective-permute-start.23
  95.2 2.0 %collective-permute-start.24 = (bf16[256,128]{1,0:T(8,128)(2,1)S(1)}, bf16[256,128]{1,0:T(8,128)(2,1)S(1)}, u32[]{:S(2)}, u32[]{:S(2)}) collective-permute-start(bf16[256,128]{1,0:T(8,128)(2,1)S(1)} %get-tuple-element.63), channel_id=1, source_target_pairs={{0,12},{2,14},{4,8},{6,10},{8,4},{10,6},{12,0},{14,2},{1,13},{3,15... | collective-permute-start | bytes 196616 | tf_op jit(solution)/shard_map/ppermute | solution.py:352
  97.3 0.8 collective-permute-start.22
  98.1 0.7 shard_map.90
  98.8 3.1 %collective-permute-done.23.refs_2_ = bf16[256,128]{1,0:T(8,128)(2,1)S(1)} collective-permute-done((bf16[256,128]{1,0:T(8,128)(2,1)S(1)}, bf16[256,128]{1,0:T(8,128)(2,1)S(1)}, u32[]{:S(2)}, u32[]{:S(2)}) %collective-permute-start.23) | collective-permute-done | bytes 65568 | tf_op jit(solution)/shard_map/ppermute | solution.py:352
  101.9 0.4 collective-permute-done.22.refs_1_
  102.4 0.7 shard_map.93
  (72 shorter events, 1.2 us)
Async XLA Ops:
  0.6 8.9 %collective-permute-start = (bf16[256,8192]{1,0:T(8,128)(2,1)}, bf16[256,8192]{1,0:T(8,128)(2,1)S(1)}, u32[]{:S(2)}, u32[]{:S(2)}) collective-permute-start(bf16[256,8192]{1,0:T(8,128)(2,1)} %refs_1_.3), channel_id=1, source_target_pairs={{0,1},{1,0},{2,3},{3,2},{4,5},{5,4},{6,7},{7,6},{8,9},{9,8},{10,11... | collective-permute-start | bytes 12582920 | tf_op jit(solution)/shard_map/ppermute | solution.py:358
  1.1 2.2 %copy-start = (bf16[256,8192]{1,0:T(8,128)(2,1)S(1)}, bf16[256,8192]{1,0:T(8,128)(2,1)}, u32[]{:S(2)}) copy-start(bf16[256,8192]{1,0:T(8,128)(2,1)} %refs_1_.3) | copy-start | bytes 12582916
  3.3 3.5 %copy-start.3 = (bf16[1024,256]{1,0:T(8,128)(2,1)S(1)}, bf16[1024,256]{1,0:T(8,128)(2,1)}, u32[]{:S(2)}) copy-start(bf16[1024,256]{1,0:T(8,128)(2,1)} %refs_5_) | copy-start | bytes 1572868
  3.3 3.5 %copy-start.4 = (bf16[1024,256]{1,0:T(8,128)(2,1)S(1)}, bf16[1024,256]{1,0:T(8,128)(2,1)}, u32[]{:S(2)}) copy-start(bf16[1024,256]{1,0:T(8,128)(2,1)} %refs_5_.1) | copy-start | bytes 1572868
  3.3 3.5 %copy-start.7 = (bf16[80,1024]{1,0:T(8,128)(2,1)S(1)}, bf16[80,1024]{1,0:T(8,128)(2,1)}, u32[]{:S(2)}) copy-start(bf16[80,1024]{1,0:T(8,128)(2,1)} %gain_ref.1) | copy-start | bytes 491524
  3.3 27.0 %copy-start.1 = (bf16[256,8192]{1,0:T(8,128)(2,1)S(1)}, bf16[256,8192]{1,0:T(8,128)(2,1)}, u32[]{:S(2)}) copy-start(bf16[256,8192]{1,0:T(8,128)(2,1)} %refs_1_.3) | copy-start | bytes 12582916
  3.6 49.9 %collective-permute-start.1 = (bf16[256,4096]{1,0:T(8,128)(2,1)S(1)}, bf16[256,4096]{1,0:T(8,128)(2,1)}, u32[]{:S(2)}, u32[]{:S(2)}) collective-permute-start(bf16[256,4096]{1,0:T(8,128)(2,1)S(1)} %shard_map.86), channel_id=1, source_target_pairs={{0,2},{2,0},{4,6},{6,4},{8,10},{10,8},{12,14},{14,12},{1,3},{3,1},... | collective-permute-start | bytes 6291464 | tf_op jit(solution)/shard_map/ppermute | solution.py:349
  7.1 0.8 copy-start.2
  7.9 15.5 %collective-permute-start.3 = (bf16[272,512]{1,0:T(8,128)(2,1)S(1)}, bf16[272,512]{1,0:T(8,128)(2,1)S(1)}, u32[]{:S(2)}, u32[]{:S(2)}) collective-permute-start(bf16[272,512]{1,0:T(8,128)(2,1)S(1)} %get-tuple-element.34), channel_id=1, source_target_pairs={{0,4},{2,6},{4,0},{6,2},{8,12},{10,14},{12,8},{14,10},{1,5},{3,7},... | collective-permute-start | bytes 835592 | tf_op jit(solution)/shard_map/ppermute | solution.py:352
  9.5 19.2 %copy-start.9 = (bf16[256,8192]{1,0:T(8,128)(2,1)}, bf16[256,8192]{1,0:T(8,128)(2,1)S(1)}, u32[]{:S(2)}) copy-start(bf16[256,8192]{1,0:T(8,128)(2,1)S(1)} %collective-permute-done.refs_2_) | copy-start | bytes 12582916
  9.5 19.2 %collective-permute-start.8 = (bf16[272,512]{1,0:T(8,128)(2,1)S(1)}, bf16[272,512]{1,0:T(8,128)(2,1)S(1)}, u32[]{:S(2)}, u32[]{:S(2)}) collective-permute-start(bf16[272,512]{1,0:T(8,128)(2,1)S(1)} %get-tuple-element.41), channel_id=1, source_target_pairs={{0,4},{2,6},{4,0},{6,2},{8,12},{10,14},{12,8},{14,10},{1,5},{3,7},... | collective-permute-start | bytes 835592 | tf_op jit(solution)/shard_map/ppermute | solution.py:352
  11.1 20.1 %collective-permute-start.2 = (bf16[272,512]{1,0:T(8,128)(2,1)S(1)}, bf16[272,512]{1,0:T(8,128)(2,1)S(1)}, u32[]{:S(2)}, u32[]{:S(2)}) collective-permute-start(bf16[272,512]{1,0:T(8,128)(2,1)S(1)} %get-tuple-element.34), channel_id=1, source_target_pairs={{0,8},{2,10},{4,12},{6,14},{8,0},{10,2},{12,4},{14,6},{1,9},{3,11}... | collective-permute-start | bytes 835592 | tf_op jit(solution)/shard_map/ppermute | solution.py:352
  23.4 45.6 %copy-start.10 = (bf16[272,512]{1,0:T(8,128)(2,1)}, bf16[272,512]{1,0:T(8,128)(2,1)S(1)}, u32[]{:S(2)}) copy-start(bf16[272,512]{1,0:T(8,128)(2,1)S(1)} %collective-permute-done.3.refs_7_) | copy-start | bytes 835588
  23.4 19.4 %collective-permute-start.7 = (bf16[272,512]{1,0:T(8,128)(2,1)S(1)}, bf16[272,512]{1,0:T(8,128)(2,1)S(1)}, u32[]{:S(2)}, u32[]{:S(2)}) collective-permute-start(bf16[272,512]{1,0:T(8,128)(2,1)S(1)} %get-tuple-element.41), channel_id=1, source_target_pairs={{0,8},{2,10},{4,12},{6,14},{8,0},{10,2},{12,4},{14,6},{1,9},{3,11}... | collective-permute-start | bytes 835592 | tf_op jit(solution)/shard_map/ppermute | solution.py:352
  25.1 8.4 %collective-permute-start.5 = (bf16[272,512]{1,0:T(8,128)(2,1)S(1)}, bf16[272,512]{1,0:T(8,128)(2,1)S(1)}, u32[]{:S(2)}, u32[]{:S(2)}) collective-permute-start(bf16[272,512]{1,0:T(8,128)(2,1)S(1)} %collective-permute-done.3.refs_7_), channel_id=1, source_target_pairs={{0,16},{16,0},{1,17},{17,1},{2,18},{18,2},{3,19},{19,3},{4,20},{20... | collective-permute-start | bytes 835592 | tf_op jit(solution)/shard_map/ppermute | solution.py:355
  28.7 40.3 %copy-start.11 = (bf16[272,512]{1,0:T(8,128)(2,1)}, bf16[272,512]{1,0:T(8,128)(2,1)S(1)}, u32[]{:S(2)}) copy-start(bf16[272,512]{1,0:T(8,128)(2,1)S(1)} %collective-permute-done.8.refs_8_) | copy-start | bytes 835588
  28.7 14.0 %collective-permute-start.9 = (bf16[272,512]{1,0:T(8,128)(2,1)S(1)}, bf16[272,512]{1,0:T(8,128)(2,1)S(1)}, u32[]{:S(2)}, u32[]{:S(2)}) collective-permute-start(bf16[272,512]{1,0:T(8,128)(2,1)S(1)} %collective-permute-done.8.refs_8_), channel_id=1, source_target_pairs={{0,16},{16,0},{1,17},{17,1},{2,18},{18,2},{3,19},{19,3},{4,20},{20... | collective-permute-start | bytes 835592 | tf_op jit(solution)/shard_map/ppermute | solution.py:355
  31.2 38.8 %copy-start.12 = (bf16[272,512]{1,0:T(8,128)(2,1)}, bf16[272,512]{1,0:T(8,128)(2,1)S(1)}, u32[]{:S(2)}) copy-start(bf16[272,512]{1,0:T(8,128)(2,1)S(1)} %collective-permute-done.2.refs_9_) | copy-start | bytes 835588
  31.2 13.8 %collective-permute-start.4 = (bf16[272,512]{1,0:T(8,128)(2,1)S(1)}, bf16[272,512]{1,0:T(8,128)(2,1)S(1)}, u32[]{:S(2)}, u32[]{:S(2)}) collective-permute-start(bf16[272,512]{1,0:T(8,128)(2,1)S(1)} %collective-permute-done.2.refs_9_), channel_id=1, source_target_pairs={{0,4},{2,6},{4,0},{6,2},{8,12},{10,14},{12,8},{14,10},{1,5},{3,7},... | collective-permute-start | bytes 835592 | tf_op jit(solution)/shard_map/ppermute | solution.py:352
  33.4 23.8 %copy-start.14 = (bf16[272,512]{1,0:T(8,128)(2,1)}, bf16[272,512]{1,0:T(8,128)(2,1)S(1)}, u32[]{:S(2)}) copy-start(bf16[272,512]{1,0:T(8,128)(2,1)S(1)} %collective-permute-done.5.refs_13_) | copy-start | bytes 835588
  33.4 11.6 %collective-permute-start.6 = (bf16[272,512]{1,0:T(8,128)(2,1)S(1)}, bf16[272,512]{1,0:T(8,128)(2,1)S(1)}, u32[]{:S(2)}, u32[]{:S(2)}) collective-permute-start(bf16[272,512]{1,0:T(8,128)(2,1)S(1)} %collective-permute-done.2.refs_9_), channel_id=1, source_target_pairs={{0,16},{16,0},{1,17},{17,1},{2,18},{18,2},{3,19},{19,3},{4,20},{20... | collective-permute-start | bytes 835592 | tf_op jit(solution)/shard_map/ppermute | solution.py:355
  42.8 27.3 %copy-start.13 = (bf16[272,512]{1,0:T(8,128)(2,1)}, bf16[272,512]{1,0:T(8,128)(2,1)S(1)}, u32[]{:S(2)}) copy-start(bf16[272,512]{1,0:T(8,128)(2,1)S(1)} %collective-permute-done.7.refs_10_) | copy-start | bytes 835588
  42.8 16.4 %copy-start.15 = (bf16[272,512]{1,0:T(8,128)(2,1)}, bf16[272,512]{1,0:T(8,128)(2,1)S(1)}, u32[]{:S(2)}) copy-start(bf16[272,512]{1,0:T(8,128)(2,1)S(1)} %collective-permute-done.9.refs_14_) | copy-start | bytes 835588
  42.8 8.6 %collective-permute-start.10 = (bf16[272,512]{1,0:T(8,128)(2,1)S(1)}, bf16[272,512]{1,0:T(8,128)(2,1)S(1)}, u32[]{:S(2)}, u32[]{:S(2)}) collective-permute-start(bf16[272,512]{1,0:T(8,128)(2,1)S(1)} %collective-permute-done.7.refs_10_), channel_id=1, source_target_pairs={{0,4},{2,6},{4,0},{6,2},{8,12},{10,14},{12,8},{14,10},{1,5},{3,7},... | collective-permute-start | bytes 835592 | tf_op jit(solution)/shard_map/ppermute | solution.py:352
  43.1 14.1 %collective-permute-start.12 = (bf16[272,512]{1,0:T(8,128)(2,1)S(1)}, bf16[272,512]{1,0:T(8,128)(2,1)S(1)}, u32[]{:S(2)}, u32[]{:S(2)}) collective-permute-start(bf16[272,512]{1,0:T(8,128)(2,1)S(1)} %collective-permute-done.7.refs_10_), channel_id=1, source_target_pairs={{0,16},{16,0},{1,17},{17,1},{2,18},{18,2},{3,19},{19,3},{4,20},{20... | collective-permute-start | bytes 835592 | tf_op jit(solution)/shard_map/ppermute | solution.py:355
  45.0 14.1 %copy-start.16 = (bf16[272,512]{1,0:T(8,128)(2,1)}, bf16[272,512]{1,0:T(8,128)(2,1)S(1)}, u32[]{:S(2)}) copy-start(bf16[272,512]{1,0:T(8,128)(2,1)S(1)} %collective-permute-done.4.refs_11_) | copy-start | bytes 835588
  45.0 6.3 %copy-start.17 = (bf16[272,512]{1,0:T(8,128)(2,1)}, bf16[272,512]{1,0:T(8,128)(2,1)S(1)}, u32[]{:S(2)}) copy-start(bf16[272,512]{1,0:T(8,128)(2,1)S(1)} %collective-permute-done.6.refs_15_) | copy-start | bytes 835588
  51.3 18.5 %copy-start.18 = (bf16[272,512]{1,0:T(8,128)(2,1)}, bf16[272,512]{1,0:T(8,128)(2,1)S(1)}, u32[]{:S(2)}) copy-start(bf16[272,512]{1,0:T(8,128)(2,1)S(1)} %collective-permute-done.10.refs_12_) | copy-start | bytes 835588
  51.3 7.8 %collective-permute-start.11 = (bf16[272,512]{1,0:T(8,128)(2,1)S(1)}, bf16[272,512]{1,0:T(8,128)(2,1)S(1)}, u32[]{:S(2)}, u32[]{:S(2)}) collective-permute-start(bf16[272,512]{1,0:T(8,128)(2,1)S(1)} %collective-permute-done.4.refs_11_), channel_id=1, source_target_pairs={{0,16},{16,0},{1,17},{17,1},{2,18},{18,2},{3,19},{19,3},{4,20},{20... | collective-permute-start | bytes 835592 | tf_op jit(solution)/shard_map/ppermute | solution.py:355
  53.5 3.7 %collective-permute-start.13 = (f32[2,256]{1,0:T(2,128)S(1)}, f32[2,256]{1,0:T(2,128)S(1)}, u32[]{:S(2)}, u32[]{:S(2)}) collective-permute-start(f32[2,256]{1,0:T(2,128)S(1)} %get-tuple-element.44), channel_id=1, source_target_pairs={{0,2},{2,0},{4,6},{6,4},{8,10},{10,8},{12,14},{14,12},{1,3},{3,1},... | collective-permute-start | bytes 6152 | tf_op jit(solution)/shard_map/ppermute | solution.py:349
  57.2 1.9 %copy-start.19 = (bf16[272,512]{1,0:T(8,128)(2,1)}, bf16[272,512]{1,0:T(8,128)(2,1)S(1)}, u32[]{:S(2)}) copy-start(bf16[272,512]{1,0:T(8,128)(2,1)S(1)} %collective-permute-done.12.refs_16_) | copy-start | bytes 835588
  59.1 10.7 %copy-start.20 = (bf16[272,512]{1,0:T(8,128)(2,1)}, bf16[272,512]{1,0:T(8,128)(2,1)S(1)}, u32[]{:S(2)}) copy-start(bf16[272,512]{1,0:T(8,128)(2,1)S(1)} %collective-permute-done.11.refs_17_) | copy-start | bytes 835588
  59.1 10.9 %collective-permute-start.14 = (bf16[256,4096]{1,0:T(8,128)(2,1)}, bf16[256,4096]{1,0:T(8,128)(2,1)}, u32[]{:S(2)}, u32[]{:S(2)}) collective-permute-start(bf16[256,4096]{1,0:T(8,128)(2,1)} %collective-permute-done.1.refs_3_), channel_id=1, source_target_pairs={{0,1},{1,0},{2,3},{3,2},{4,5},{5,4},{6,7},{7,6},{8,9},{9,8},{10,11... | collective-permute-start | bytes 6291464 | tf_op jit(solution)/shard_map/ppermute | solution.py:358
  59.6 9.0 %collective-permute-start.15 = (bf16[272,512]{1,0:T(8,128)(2,1)S(1)}, bf16[272,512]{1,0:T(8,128)(2,1)S(1)}, u32[]{:S(2)}, u32[]{:S(2)}) collective-permute-start(bf16[272,512]{1,0:T(8,128)(2,1)S(1)} %collective-permute-done.10.refs_12_), channel_id=1, source_target_pairs={{0,16},{16,0},{1,17},{17,1},{2,18},{18,2},{3,19},{19,3},{4,20},{20... | collective-permute-start | bytes 835592 | tf_op jit(solution)/shard_map/ppermute | solution.py:355
  68.6 1.2 %copy-start.21 = (bf16[272,512]{1,0:T(8,128)(2,1)}, bf16[272,512]{1,0:T(8,128)(2,1)S(1)}, u32[]{:S(2)}) copy-start(bf16[272,512]{1,0:T(8,128)(2,1)S(1)} %collective-permute-done.15.refs_18_) | copy-start | bytes 835588
  68.6 1.2 %collective-permute-start.16 = (f32[2,256]{1,0:T(2,128)S(1)}, f32[2,256]{1,0:T(2,128)S(1)}, u32[]{:S(2)}, u32[]{:S(2)}) collective-permute-start(f32[2,256]{1,0:T(2,128)S(1)} %bitcast.15), channel_id=1, source_target_pairs={{0,1},{1,0},{2,3},{3,2},{4,5},{5,4},{6,7},{7,6},{8,9},{9,8},{10,11... | collective-permute-start | bytes 6152 | tf_op jit(solution)/shard_map/ppermute | solution.py:358
  76.8 8.9 %copy-start.6 = (f32[4,2,128,128]{3,2,1,0:T(8,128)S(1)}, f32[4,2,128,128]{3,2,1,0:T(8,128)}, u32[]{:S(2)}) copy-start(f32[4,2,128,128]{3,2,1,0:T(8,128)} %get-tuple-element.49.keep_ref) | copy-start | bytes 1572868
  76.8 8.9 %copy-start.8 = (s32[8]{0:T(128)S(1)}, s32[8]{0:T(128)}, u32[]{:S(2)}) copy-start(s32[8]{0:T(128)} %owner_ref.3) | copy-start | bytes 100
  76.8 8.9 %collective-permute-start.17 = (bf16[4,2,128,128]{3,2,1,0:T(8,128)(2,1)}, bf16[4,2,128,128]{3,2,1,0:T(8,128)(2,1)S(1)}, u32[]{:S(2)}, u32[]{:S(2)}) collective-permute-start(bf16[4,2,128,128]{3,2,1,0:T(8,128)(2,1)} %get-tuple-element.50), channel_id=1, source_target_pairs={{0,2},{2,0},{4,6},{6,4},{8,10},{10,8},{12,14},{14,12},{1,3},{3,1},... | collective-permute-start | bytes 786440 | tf_op jit(solution)/shard_map/ppermute | solution.py:349
  84.4 8.4 %collective-permute-start.21 = (bf16[4,2,128,128]{3,2,1,0:T(8,128)(2,1)}, bf16[4,2,128,128]{3,2,1,0:T(8,128)(2,1)S(1)}, u32[]{:S(2)}, u32[]{:S(2)}) collective-permute-start(bf16[4,2,128,128]{3,2,1,0:T(8,128)(2,1)} %get-tuple-element.57), channel_id=1, source_target_pairs={{0,2},{2,0},{4,6},{6,4},{8,10},{10,8},{12,14},{14,12},{1,3},{3,1},... | collective-permute-start | bytes 786440 | tf_op jit(solution)/shard_map/ppermute | solution.py:349
  86.5 10.8 %collective-permute-start.18 = (bf16[256,128]{1,0:T(8,128)(2,1)S(1)}, bf16[256,128]{1,0:T(8,128)(2,1)S(1)}, u32[]{:S(2)}, u32[]{:S(2)}) collective-permute-start(bf16[256,128]{1,0:T(8,128)(2,1)S(1)} %get-tuple-element.52), channel_id=1, source_target_pairs={{0,4},{2,6},{4,0},{6,2},{8,12},{10,14},{12,8},{14,10},{1,5},{3,7},... | collective-permute-start | bytes 196616 | tf_op jit(solution)/shard_map/ppermute | solution.py:352
  86.9 10.4 %collective-permute-start.19 = (bf16[256,128]{1,0:T(8,128)(2,1)S(1)}, bf16[256,128]{1,0:T(8,128)(2,1)S(1)}, u32[]{:S(2)}, u32[]{:S(2)}) collective-permute-start(bf16[256,128]{1,0:T(8,128)(2,1)S(1)} %get-tuple-element.53), channel_id=1, source_target_pairs={{0,8},{2,10},{4,12},{6,14},{8,0},{10,2},{12,4},{14,6},{1,9},{3,11}... | collective-permute-start | bytes 196616 | tf_op jit(solution)/shard_map/ppermute | solution.py:352
  90.1 7.1 %collective-permute-start.20 = (bf16[256,128]{1,0:T(8,128)(2,1)S(1)}, bf16[256,128]{1,0:T(8,128)(2,1)S(1)}, u32[]{:S(2)}, u32[]{:S(2)}) collective-permute-start(bf16[256,128]{1,0:T(8,128)(2,1)S(1)} %get-tuple-element.54), channel_id=1, source_target_pairs={{0,12},{2,14},{4,8},{6,10},{8,4},{10,6},{12,0},{14,2},{1,13},{3,15... | collective-permute-start | bytes 196616 | tf_op jit(solution)/shard_map/ppermute | solution.py:352
  92.8 1.0 %copy-start.5 = (f32[4,2,128,128]{3,2,1,0:T(8,128)S(1)}, f32[4,2,128,128]{3,2,1,0:T(8,128)}, u32[]{:S(2)}) copy-start(f32[4,2,128,128]{3,2,1,0:T(8,128)} %get-tuple-element.56.keep_ref) | copy-start | bytes 1572868
  94.4 7.5 %collective-permute-start.23 = (bf16[256,128]{1,0:T(8,128)(2,1)S(1)}, bf16[256,128]{1,0:T(8,128)(2,1)S(1)}, u32[]{:S(2)}, u32[]{:S(2)}) collective-permute-start(bf16[256,128]{1,0:T(8,128)(2,1)S(1)} %get-tuple-element.62), channel_id=1, source_target_pairs={{0,8},{2,10},{4,12},{6,14},{8,0},{10,2},{12,4},{14,6},{1,9},{3,11}... | collective-permute-start | bytes 196616 | tf_op jit(solution)/shard_map/ppermute | solution.py:352
  95.2 6.7 %collective-permute-start.24 = (bf16[256,128]{1,0:T(8,128)(2,1)S(1)}, bf16[256,128]{1,0:T(8,128)(2,1)S(1)}, u32[]{:S(2)}, u32[]{:S(2)}) collective-permute-start(bf16[256,128]{1,0:T(8,128)(2,1)S(1)} %get-tuple-element.63), channel_id=1, source_target_pairs={{0,12},{2,14},{4,8},{6,10},{8,4},{10,6},{12,0},{14,2},{1,13},{3,15... | collective-permute-start | bytes 196616 | tf_op jit(solution)/shard_map/ppermute | solution.py:352
  97.3 5.1 %collective-permute-start.22 = (bf16[256,128]{1,0:T(8,128)(2,1)S(1)}, bf16[256,128]{1,0:T(8,128)(2,1)S(1)}, u32[]{:S(2)}, u32[]{:S(2)}) collective-permute-start(bf16[256,128]{1,0:T(8,128)(2,1)S(1)} %get-tuple-element.61), channel_id=1, source_target_pairs={{0,4},{2,6},{4,0},{6,2},{8,12},{10,14},{12,8},{14,10},{1,5},{3,7},... | collective-permute-start | bytes 196616 | tf_op jit(solution)/shard_map/ppermute | solution.py:352

commit v5 on v4

--- a/solution.py
+++ b/solution.py
@@ -388,7 +388,7 @@
     cosine = jnp.concatenate([cosine, cosine], axis=1).reshape(8, page, HD)
     sine = jnp.concatenate([-sine, sine], axis=1).reshape(8, page, HD)
     pair_squares = pair_facts[:, 0]
-    squares = jnp.stack([pair_squares, over_c(after(pair_squares, corner_y_1))], axis=1).reshape(4, device_rows)
+    squares = jnp.stack([pair_squares, over_c(pair_squares)], axis=1).reshape(4, device_rows)
     scale = lax.rsqrt(squares / hidden.shape[1] + 1e-05)
     scale = jnp.broadcast_to(scale[:, :, None], (4, device_rows, HD))
 

time: 103 us -> 102 us (level)
  waiting for transfers between devices: 44.2 us -> 42.1 us
    unnamed x45 -> x43, local copies, waits for them, and re-layouts: 4.12 us -> 4.12 us
  transfers between devices with their start and end apart: 25 -> 25, of which waited for: 13 -> 14; matrix products, arithmetic and copies ran while one was open for 4% -> 4% of each run, Pallas kernels for 9% -> 9%
where the time goes in v5:
time: 102 us; the launch traced here: 101 us
  waiting for transfers between devices  42.1 us (41%)
  starting transfers between devices  31.9 us (31%)
  Pallas kernels  16.8 us (16%)
  local copies, waits for them, and re-layouts  4.5 us (4%)
  other arithmetic  3.65 us (4%)
  between operations  2.25 us (2%)
    ppermute x12, waiting for transfers between devices, over_z(): lax.ppermute(values, 'tok', [(t, t ^ 2 * distance) for t in range(tok_cou...  30.7 us
    ppermute x12, starting transfers between devices, over_z(): lax.ppermute(values, 'tok', [(t, t ^ 2 * distance) for t in range(tok_cou...  16.3 us
    pallas_call x2, Pallas kernels, multiply(): pl.pallas_call(functools.partial(multiply_kernel, shard, counts, which),...  13.5 us
    ppermute x6, starting transfers between devices, over_y(): return lax.ppermute(values, 'group', [(0, 1), (1, 0)])  9.07 us
    ppermute x6, waiting for transfers between devices, over_y(): return lax.ppermute(values, 'group', [(0, 1), (1, 0)])  7.67 us
    ppermute x4, starting transfers between devices, over_x(): return lax.ppermute(values, 'tok', [(t, t ^ 1) for t in range(tok_count)])  5.48 us
    unnamed x43, local copies, waits for them, and re-layouts  4.12 us
    ppermute x4, waiting for transfers between devices, over_x(): return lax.ppermute(values, 'tok', [(t, t ^ 1) for t in range(tok_count)])  3.72 us
  transfers between devices with their start and end apart: 25, of which 14 were waited for; matrix products, arithmetic and copies ran while one was open for 4% of the time, Pallas kernels for 9%

profile of v5, /device:TPU:0, one launch (start us, length us, event | category | flops | bytes accessed | tf_op | source)
XLA Modules:
  0.0 101.2 jit_solution(14269883315939682114)
XLA Ops:
  0.6 0.5 collective-permute-start
  1.1 2.2 %copy-done = bf16[256,8192]{1,0:T(8,128)(2,1)S(1)} copy-done((bf16[256,8192]{1,0:T(8,128)(2,1)S(1)}, bf16[256,8192]{1,0:T(8,128)(2,1)}, u32[]{:S(2)}) %copy-start) | copy-done | bytes 4194328
  3.6 2.6 %collective-permute-start.1 = (bf16[256,4096]{1,0:T(8,128)(2,1)S(1)}, bf16[256,4096]{1,0:T(8,128)(2,1)}, u32[]{:S(2)}, u32[]{:S(2)}) collective-permute-start(bf16[256,4096]{1,0:T(8,128)(2,1)S(1)} %shard_map.86), channel_id=1, source_target_pairs={{0,2},{2,0},{4,6},{6,4},{8,10},{10,8},{12,14},{14,12},{1,3},{3,1},... | collective-permute-start | bytes 6291464 | tf_op jit(solution)/shard_map/ppermute | solution.py:349
  7.1 0.8 copy-done.2
  7.9 1.6 %collective-permute-start.3 = (bf16[272,512]{1,0:T(8,128)(2,1)S(1)}, bf16[272,512]{1,0:T(8,128)(2,1)S(1)}, u32[]{:S(2)}, u32[]{:S(2)}) collective-permute-start(bf16[272,512]{1,0:T(8,128)(2,1)S(1)} %get-tuple-element.33), channel_id=1, source_target_pairs={{0,4},{2,6},{4,0},{6,2},{8,12},{10,14},{12,8},{14,10},{1,5},{3,7},... | collective-permute-start | bytes 835592 | tf_op jit(solution)/shard_map/ppermute | solution.py:352
  9.5 1.6 %collective-permute-start.8 = (bf16[272,512]{1,0:T(8,128)(2,1)S(1)}, bf16[272,512]{1,0:T(8,128)(2,1)S(1)}, u32[]{:S(2)}, u32[]{:S(2)}) collective-permute-start(bf16[272,512]{1,0:T(8,128)(2,1)S(1)} %get-tuple-element.40), channel_id=1, source_target_pairs={{0,4},{2,6},{4,0},{6,2},{8,12},{10,14},{12,8},{14,10},{1,5},{3,7},... | collective-permute-start | bytes 835592 | tf_op jit(solution)/shard_map/ppermute | solution.py:352
  11.1 2.6 %collective-permute-start.2 = (bf16[272,512]{1,0:T(8,128)(2,1)S(1)}, bf16[272,512]{1,0:T(8,128)(2,1)S(1)}, u32[]{:S(2)}, u32[]{:S(2)}) collective-permute-start(bf16[272,512]{1,0:T(8,128)(2,1)S(1)} %get-tuple-element.33), channel_id=1, source_target_pairs={{0,8},{2,10},{4,12},{6,14},{8,0},{10,2},{12,4},{14,6},{1,9},{3,11}... | collective-permute-start | bytes 835592 | tf_op jit(solution)/shard_map/ppermute | solution.py:352
  13.7 9.7 %collective-permute-done.3.refs_7_ = bf16[272,512]{1,0:T(8,128)(2,1)S(1)} collective-permute-done((bf16[272,512]{1,0:T(8,128)(2,1)S(1)}, bf16[272,512]{1,0:T(8,128)(2,1)S(1)}, u32[]{:S(2)}, u32[]{:S(2)}) %collective-permute-start.3) | collective-permute-done | bytes 278560 | tf_op jit(solution)/shard_map/ppermute | solution.py:352
  23.4 1.7 %collective-permute-start.7 = (bf16[272,512]{1,0:T(8,128)(2,1)S(1)}, bf16[272,512]{1,0:T(8,128)(2,1)S(1)}, u32[]{:S(2)}, u32[]{:S(2)}) collective-permute-start(bf16[272,512]{1,0:T(8,128)(2,1)S(1)} %get-tuple-element.40), channel_id=1, source_target_pairs={{0,8},{2,10},{4,12},{6,14},{8,0},{10,2},{12,4},{14,6},{1,9},{3,11}... | collective-permute-start | bytes 835592 | tf_op jit(solution)/shard_map/ppermute | solution.py:352
  25.1 1.5 %collective-permute-start.5 = (bf16[272,512]{1,0:T(8,128)(2,1)S(1)}, bf16[272,512]{1,0:T(8,128)(2,1)S(1)}, u32[]{:S(2)}, u32[]{:S(2)}) collective-permute-start(bf16[272,512]{1,0:T(8,128)(2,1)S(1)} %collective-permute-done.3.refs_7_), channel_id=1, source_target_pairs={{0,16},{16,0},{1,17},{17,1},{2,18},{18,2},{3,19},{19,3},{4,20},{20... | collective-permute-start | bytes 835592 | tf_op jit(solution)/shard_map/ppermute | solution.py:355
  26.6 2.2 %collective-permute-done.8.refs_8_ = bf16[272,512]{1,0:T(8,128)(2,1)S(1)} collective-permute-done((bf16[272,512]{1,0:T(8,128)(2,1)S(1)}, bf16[272,512]{1,0:T(8,128)(2,1)S(1)}, u32[]{:S(2)}, u32[]{:S(2)}) %collective-permute-start.8) | collective-permute-done | bytes 278560 | tf_op jit(solution)/shard_map/ppermute | solution.py:352
  28.7 1.6 %collective-permute-start.9 = (bf16[272,512]{1,0:T(8,128)(2,1)S(1)}, bf16[272,512]{1,0:T(8,128)(2,1)S(1)}, u32[]{:S(2)}, u32[]{:S(2)}) collective-permute-start(bf16[272,512]{1,0:T(8,128)(2,1)S(1)} %collective-permute-done.8.refs_8_), channel_id=1, source_target_pairs={{0,16},{16,0},{1,17},{17,1},{2,18},{18,2},{3,19},{19,3},{4,20},{20... | collective-permute-start | bytes 835592 | tf_op jit(solution)/shard_map/ppermute | solution.py:355
  30.3 0.9 multiply_reduce_fusion
  31.2 0.8 collective-permute-start.4
  32.0 1.4 %collective-permute-done.5.refs_13_ = bf16[272,512]{1,0:T(8,128)(2,1)S(1)} collective-permute-done((bf16[272,512]{1,0:T(8,128)(2,1)S(1)}, bf16[272,512]{1,0:T(8,128)(2,1)S(1)}, u32[]{:S(2)}, u32[]{:S(2)}) %collective-permute-start.5) | collective-permute-done | bytes 278560 | tf_op jit(solution)/shard_map/ppermute | solution.py:355
  33.4 1.4 %collective-permute-start.6 = (bf16[272,512]{1,0:T(8,128)(2,1)S(1)}, bf16[272,512]{1,0:T(8,128)(2,1)S(1)}, u32[]{:S(2)}, u32[]{:S(2)}) collective-permute-start(bf16[272,512]{1,0:T(8,128)(2,1)S(1)} %collective-permute-done.2.refs_9_), channel_id=1, source_target_pairs={{0,16},{16,0},{1,17},{17,1},{2,18},{18,2},{3,19},{19,3},{4,20},{20... | collective-permute-start | bytes 835592 | tf_op jit(solution)/shard_map/ppermute | solution.py:355
  34.8 8.0 %collective-permute-done.7.refs_10_ = bf16[272,512]{1,0:T(8,128)(2,1)S(1)} collective-permute-done((bf16[272,512]{1,0:T(8,128)(2,1)S(1)}, bf16[272,512]{1,0:T(8,128)(2,1)S(1)}, u32[]{:S(2)}, u32[]{:S(2)}) %collective-permute-start.7) | collective-permute-done | bytes 278560 | tf_op jit(solution)/shard_map/ppermute | solution.py:352
  42.8 0.3 collective-permute-start.10
  43.1 1.5 %collective-permute-start.12 = (bf16[272,512]{1,0:T(8,128)(2,1)S(1)}, bf16[272,512]{1,0:T(8,128)(2,1)S(1)}, u32[]{:S(2)}, u32[]{:S(2)}) collective-permute-start(bf16[272,512]{1,0:T(8,128)(2,1)S(1)} %collective-permute-done.7.refs_10_), channel_id=1, source_target_pairs={{0,16},{16,0},{1,17},{17,1},{2,18},{18,2},{3,19},{19,3},{4,20},{20... | collective-permute-start | bytes 835592 | tf_op jit(solution)/shard_map/ppermute | solution.py:355
  44.6 0.4 collective-permute-done.4.refs_11_
  45.0 6.3 %collective-permute-done.10.refs_12_ = bf16[272,512]{1,0:T(8,128)(2,1)S(1)} collective-permute-done((bf16[272,512]{1,0:T(8,128)(2,1)S(1)}, bf16[272,512]{1,0:T(8,128)(2,1)S(1)}, u32[]{:S(2)}, u32[]{:S(2)}) %collective-permute-start.10) | collective-permute-done | bytes 278560 | tf_op jit(solution)/shard_map/ppermute | solution.py:352
  51.3 1.5 %collective-permute-start.11 = (bf16[272,512]{1,0:T(8,128)(2,1)S(1)}, bf16[272,512]{1,0:T(8,128)(2,1)S(1)}, u32[]{:S(2)}, u32[]{:S(2)}) collective-permute-start(bf16[272,512]{1,0:T(8,128)(2,1)S(1)} %collective-permute-done.4.refs_11_), channel_id=1, source_target_pairs={{0,16},{16,0},{1,17},{17,1},{2,18},{18,2},{3,19},{19,3},{4,20},{20... | collective-permute-start | bytes 835592 | tf_op jit(solution)/shard_map/ppermute | solution.py:355
  53.5 0.8 collective-permute-start.13
  54.3 2.9 %collective-permute-done.13 = f32[2,256]{1,0:T(2,128)S(1)} collective-permute-done((f32[2,256]{1,0:T(2,128)S(1)}, f32[2,256]{1,0:T(2,128)S(1)}, u32[]{:S(2)}, u32[]{:S(2)}) %collective-permute-start.13) | collective-permute-done | bytes 2080 | tf_op jit(solution)/shard_map/ppermute | solution.py:349
  57.2 1.9 %collective-permute-done.11.refs_17_ = bf16[272,512]{1,0:T(8,128)(2,1)S(1)} collective-permute-done((bf16[272,512]{1,0:T(8,128)(2,1)S(1)}, bf16[272,512]{1,0:T(8,128)(2,1)S(1)}, u32[]{:S(2)}, u32[]{:S(2)}) %collective-permute-start.11) | collective-permute-done | bytes 278560 | tf_op jit(solution)/shard_map/ppermute | solution.py:355
  59.2 0.5 collective-permute-start.15
  60.1 1.5 %collective-permute-start.16 = (bf16[272,512]{1,0:T(8,128)(2,1)S(1)}, bf16[272,512]{1,0:T(8,128)(2,1)}, u32[]{:S(2)}, u32[]{:S(2)}) collective-permute-start(bf16[272,512]{1,0:T(8,128)(2,1)S(1)} %collective-permute-done.10.refs_12_), channel_id=1, source_target_pairs={{0,16},{16,0},{1,17},{17,1},{2,18},{18,2},{3,19},{19,3},{4,20},{20... | collective-permute-start | bytes 835592 | tf_op jit(solution)/shard_map/ppermute | solution.py:355
  61.7 2.2 %fusion.5 = (f32[8,128,64]{2,1,0:T(8,128)S(1)}, f32[8,128,64]{2,1,0:T(8,128)S(1)}, f32[8,128,64]{2,1,0:T(8,128)S(1)}) fusion(f32[64]{0:T(128)S(1)} %multiply_power_fusion, f32[8,128]{1,0:T(8,128)S(1)} %add_convert_fusion), kind=kLoop, calls=%fused_computation.10 | loop fusion | flops 524288 | bytes 790784 | tf_op jit(solution)/shard_map/neg | solution.py:389
  63.8 0.3 pad_maximum_fusion
  64.5 4.4 %collective-permute-done.16.refs_18_ = bf16[272,512]{1,0:T(8,128)(2,1)} collective-permute-done((bf16[272,512]{1,0:T(8,128)(2,1)S(1)}, bf16[272,512]{1,0:T(8,128)(2,1)}, u32[]{:S(2)}, u32[]{:S(2)}) %collective-permute-start.16) | collective-permute-done | bytes 278560 | tf_op jit(solution)/shard_map/ppermute | solution.py:355
  68.9 6.7 %shard_map.88 = (f32[4,2,128,128]{3,2,1,0:T(8,128)}, bf16[4,2,128,128]{3,2,1,0:T(8,128)(2,1)}) custom-call(s32[8]{0:T(128)} %owner_ref.3, bf16[256,8192]{1,0:T(8,128)(2,1)} %refs_1_.3, bf16[256,8192]{1,0:T(8,128)(2,1)} %copy-done.9, bf16[256,4096]{1,0:T(8,128)(2,1)} %collective-permute-done.1.refs_3_, bf16[256,4096]{1,0:T(8,128)(2,1)} %collective-permute-done.14.refs_4_, ...), custom_call_target="tpu_custom_call" | custom-call | tf_op jit(solution)/shard_map/pallas_call | solution.py:267
  75.6 0.8 collective-permute-start.17
  76.4 6.7 %shard_map.91 = (f32[4,2,128,128]{3,2,1,0:T(8,128)}, bf16[4,2,128,128]{3,2,1,0:T(8,128)(2,1)}) custom-call(s32[8]{0:T(128)} %owner_ref.3, bf16[256,8192]{1,0:T(8,128)(2,1)} %refs_1_.3, bf16[256,8192]{1,0:T(8,128)(2,1)} %copy-done.9, bf16[256,4096]{1,0:T(8,128)(2,1)} %collective-permute-done.1.refs_3_, bf16[256,4096]{1,0:T(8,128)(2,1)} %collective-permute-done.14.refs_4_, ...), custom_call_target="tpu_custom_call" | custom-call | tf_op jit(solution)/shard_map/pallas_call | solution.py:267
  83.2 1.3 %collective-permute-start.21 = (bf16[4,2,128,128]{3,2,1,0:T(8,128)(2,1)}, bf16[4,2,128,128]{3,2,1,0:T(8,128)(2,1)S(1)}, u32[]{:S(2)}, u32[]{:S(2)}) collective-permute-start(bf16[4,2,128,128]{3,2,1,0:T(8,128)(2,1)} %get-tuple-element.55), channel_id=1, source_target_pairs={{0,2},{2,0},{4,6},{6,4},{8,10},{10,8},{12,14},{14,12},{1,3},{3,1},... | collective-permute-start | bytes 786440 | tf_op jit(solution)/shard_map/ppermute | solution.py:349
  84.5 0.8 shard_map.89
  85.3 0.4 collective-permute-start.18
  85.6 3.3 %collective-permute-start.19 = (bf16[256,128]{1,0:T(8,128)(2,1)S(1)}, bf16[256,128]{1,0:T(8,128)(2,1)S(1)}, u32[]{:S(2)}, u32[]{:S(2)}) collective-permute-start(bf16[256,128]{1,0:T(8,128)(2,1)S(1)} %get-tuple-element.51), channel_id=1, source_target_pairs={{0,8},{2,10},{4,12},{6,14},{8,0},{10,2},{12,4},{14,6},{1,9},{3,11}... | collective-permute-start | bytes 196616 | tf_op jit(solution)/shard_map/ppermute | solution.py:352
  88.9 0.8 collective-permute-start.20
  89.7 0.8 collective-permute-done.21.came_ref
  90.6 1.0 %copy-done.5 = f32[4,2,128,128]{3,2,1,0:T(8,128)S(1)} copy-done((f32[4,2,128,128]{3,2,1,0:T(8,128)S(1)}, f32[4,2,128,128]{3,2,1,0:T(8,128)}, u32[]{:S(2)}) %copy-start.5) | copy-done | bytes 524312
  91.6 0.6 shard_map.92
  92.2 1.9 %collective-permute-start.23 = (bf16[256,128]{1,0:T(8,128)(2,1)S(1)}, bf16[256,128]{1,0:T(8,128)(2,1)S(1)}, u32[]{:S(2)}, u32[]{:S(2)}) collective-permute-start(bf16[256,128]{1,0:T(8,128)(2,1)S(1)} %get-tuple-element.60), channel_id=1, source_target_pairs={{0,8},{2,10},{4,12},{6,14},{8,0},{10,2},{12,4},{14,6},{1,9},{3,11}... | collective-permute-start | bytes 196616 | tf_op jit(solution)/shard_map/ppermute | solution.py:352
  94.1 1.1 %collective-permute-start.24 = (bf16[256,128]{1,0:T(8,128)(2,1)S(1)}, bf16[256,128]{1,0:T(8,128)(2,1)S(1)}, u32[]{:S(2)}, u32[]{:S(2)}) collective-permute-start(bf16[256,128]{1,0:T(8,128)(2,1)S(1)} %get-tuple-element.61), channel_id=1, source_target_pairs={{0,12},{2,14},{4,8},{6,10},{8,4},{10,6},{12,0},{14,2},{1,13},{3,15... | collective-permute-start | bytes 196616 | tf_op jit(solution)/shard_map/ppermute | solution.py:352
  95.5 0.4 collective-permute-start.22
  95.9 0.7 shard_map.90
  96.6 2.2 %collective-permute-done.23.refs_2_ = bf16[256,128]{1,0:T(8,128)(2,1)S(1)} collective-permute-done((bf16[256,128]{1,0:T(8,128)(2,1)S(1)}, bf16[256,128]{1,0:T(8,128)(2,1)S(1)}, u32[]{:S(2)}, u32[]{:S(2)}) %collective-permute-start.23) | collective-permute-done | bytes 65568 | tf_op jit(solution)/shard_map/ppermute | solution.py:352
  98.8 1.5 %collective-permute-done.24.refs_3_ = bf16[256,128]{1,0:T(8,128)(2,1)S(1)} collective-permute-done((bf16[256,128]{1,0:T(8,128)(2,1)S(1)}, bf16[256,128]{1,0:T(8,128)(2,1)S(1)}, u32[]{:S(2)}, u32[]{:S(2)}) %collective-permute-start.24) | collective-permute-done | bytes 65568 | tf_op jit(solution)/shard_map/ppermute | solution.py:352
  100.5 0.7 shard_map.93
  (70 shorter events, 1.7 us)
Async XLA Ops:
  0.6 8.9 %collective-permute-start = (bf16[256,8192]{1,0:T(8,128)(2,1)}, bf16[256,8192]{1,0:T(8,128)(2,1)S(1)}, u32[]{:S(2)}, u32[]{:S(2)}) collective-permute-start(bf16[256,8192]{1,0:T(8,128)(2,1)} %refs_1_.3), channel_id=1, source_target_pairs={{0,1},{1,0},{2,3},{3,2},{4,5},{5,4},{6,7},{7,6},{8,9},{9,8},{10,11... | collective-permute-start | bytes 12582920 | tf_op jit(solution)/shard_map/ppermute | solution.py:358
  1.1 2.2 %copy-start = (bf16[256,8192]{1,0:T(8,128)(2,1)S(1)}, bf16[256,8192]{1,0:T(8,128)(2,1)}, u32[]{:S(2)}) copy-start(bf16[256,8192]{1,0:T(8,128)(2,1)} %refs_1_.3) | copy-start | bytes 12582916
  3.3 3.5 %copy-start.3 = (bf16[1024,256]{1,0:T(8,128)(2,1)S(1)}, bf16[1024,256]{1,0:T(8,128)(2,1)}, u32[]{:S(2)}) copy-start(bf16[1024,256]{1,0:T(8,128)(2,1)} %refs_5_) | copy-start | bytes 1572868
  3.3 3.5 %copy-start.4 = (bf16[1024,256]{1,0:T(8,128)(2,1)S(1)}, bf16[1024,256]{1,0:T(8,128)(2,1)}, u32[]{:S(2)}) copy-start(bf16[1024,256]{1,0:T(8,128)(2,1)} %refs_5_.1) | copy-start | bytes 1572868
  3.3 3.5 %copy-start.7 = (bf16[80,1024]{1,0:T(8,128)(2,1)S(1)}, bf16[80,1024]{1,0:T(8,128)(2,1)}, u32[]{:S(2)}) copy-start(bf16[80,1024]{1,0:T(8,128)(2,1)} %gain_ref.1) | copy-start | bytes 491524
  3.3 27.0 %copy-start.1 = (bf16[256,8192]{1,0:T(8,128)(2,1)S(1)}, bf16[256,8192]{1,0:T(8,128)(2,1)}, u32[]{:S(2)}) copy-start(bf16[256,8192]{1,0:T(8,128)(2,1)} %refs_1_.3) | copy-start | bytes 12582916
  3.6 49.9 %collective-permute-start.1 = (bf16[256,4096]{1,0:T(8,128)(2,1)S(1)}, bf16[256,4096]{1,0:T(8,128)(2,1)}, u32[]{:S(2)}, u32[]{:S(2)}) collective-permute-start(bf16[256,4096]{1,0:T(8,128)(2,1)S(1)} %shard_map.86), channel_id=1, source_target_pairs={{0,2},{2,0},{4,6},{6,4},{8,10},{10,8},{12,14},{14,12},{1,3},{3,1},... | collective-permute-start | bytes 6291464 | tf_op jit(solution)/shard_map/ppermute | solution.py:349
  7.1 0.8 copy-start.2
  7.9 15.5 %collective-permute-start.3 = (bf16[272,512]{1,0:T(8,128)(2,1)S(1)}, bf16[272,512]{1,0:T(8,128)(2,1)S(1)}, u32[]{:S(2)}, u32[]{:S(2)}) collective-permute-start(bf16[272,512]{1,0:T(8,128)(2,1)S(1)} %get-tuple-element.33), channel_id=1, source_target_pairs={{0,4},{2,6},{4,0},{6,2},{8,12},{10,14},{12,8},{14,10},{1,5},{3,7},... | collective-permute-start | bytes 835592 | tf_op jit(solution)/shard_map/ppermute | solution.py:352
  9.5 19.2 %copy-start.9 = (bf16[256,8192]{1,0:T(8,128)(2,1)}, bf16[256,8192]{1,0:T(8,128)(2,1)S(1)}, u32[]{:S(2)}) copy-start(bf16[256,8192]{1,0:T(8,128)(2,1)S(1)} %collective-permute-done.refs_2_) | copy-start | bytes 12582916
  9.5 19.2 %collective-permute-start.8 = (bf16[272,512]{1,0:T(8,128)(2,1)S(1)}, bf16[272,512]{1,0:T(8,128)(2,1)S(1)}, u32[]{:S(2)}, u32[]{:S(2)}) collective-permute-start(bf16[272,512]{1,0:T(8,128)(2,1)S(1)} %get-tuple-element.40), channel_id=1, source_target_pairs={{0,4},{2,6},{4,0},{6,2},{8,12},{10,14},{12,8},{14,10},{1,5},{3,7},... | collective-permute-start | bytes 835592 | tf_op jit(solution)/shard_map/ppermute | solution.py:352
  11.1 20.1 %collective-permute-start.2 = (bf16[272,512]{1,0:T(8,128)(2,1)S(1)}, bf16[272,512]{1,0:T(8,128)(2,1)S(1)}, u32[]{:S(2)}, u32[]{:S(2)}) collective-permute-start(bf16[272,512]{1,0:T(8,128)(2,1)S(1)} %get-tuple-element.33), channel_id=1, source_target_pairs={{0,8},{2,10},{4,12},{6,14},{8,0},{10,2},{12,4},{14,6},{1,9},{3,11}... | collective-permute-start | bytes 835592 | tf_op jit(solution)/shard_map/ppermute | solution.py:352
  23.4 40.8 %copy-start.10 = (bf16[272,512]{1,0:T(8,128)(2,1)}, bf16[272,512]{1,0:T(8,128)(2,1)S(1)}, u32[]{:S(2)}) copy-start(bf16[272,512]{1,0:T(8,128)(2,1)S(1)} %collective-permute-done.3.refs_7_) | copy-start | bytes 835588
  23.4 19.4 %collective-permute-start.7 = (bf16[272,512]{1,0:T(8,128)(2,1)S(1)}, bf16[272,512]{1,0:T(8,128)(2,1)S(1)}, u32[]{:S(2)}, u32[]{:S(2)}) collective-permute-start(bf16[272,512]{1,0:T(8,128)(2,1)S(1)} %get-tuple-element.40), channel_id=1, source_target_pairs={{0,8},{2,10},{4,12},{6,14},{8,0},{10,2},{12,4},{14,6},{1,9},{3,11}... | collective-permute-start | bytes 835592 | tf_op jit(solution)/shard_map/ppermute | solution.py:352
  25.1 8.4 %collective-permute-start.5 = (bf16[272,512]{1,0:T(8,128)(2,1)S(1)}, bf16[272,512]{1,0:T(8,128)(2,1)S(1)}, u32[]{:S(2)}, u32[]{:S(2)}) collective-permute-start(bf16[272,512]{1,0:T(8,128)(2,1)S(1)} %collective-permute-done.3.refs_7_), channel_id=1, source_target_pairs={{0,16},{16,0},{1,17},{17,1},{2,18},{18,2},{3,19},{19,3},{4,20},{20... | collective-permute-start | bytes 835592 | tf_op jit(solution)/shard_map/ppermute | solution.py:355
  28.7 35.5 %copy-start.11 = (bf16[272,512]{1,0:T(8,128)(2,1)}, bf16[272,512]{1,0:T(8,128)(2,1)S(1)}, u32[]{:S(2)}) copy-start(bf16[272,512]{1,0:T(8,128)(2,1)S(1)} %collective-permute-done.8.refs_8_) | copy-start | bytes 835588
  28.7 14.0 %collective-permute-start.9 = (bf16[272,512]{1,0:T(8,128)(2,1)S(1)}, bf16[272,512]{1,0:T(8,128)(2,1)S(1)}, u32[]{:S(2)}, u32[]{:S(2)}) collective-permute-start(bf16[272,512]{1,0:T(8,128)(2,1)S(1)} %collective-permute-done.8.refs_8_), channel_id=1, source_target_pairs={{0,16},{16,0},{1,17},{17,1},{2,18},{18,2},{3,19},{19,3},{4,20},{20... | collective-permute-start | bytes 835592 | tf_op jit(solution)/shard_map/ppermute | solution.py:355
  31.2 37.6 %copy-start.12 = (bf16[272,512]{1,0:T(8,128)(2,1)}, bf16[272,512]{1,0:T(8,128)(2,1)S(1)}, u32[]{:S(2)}) copy-start(bf16[272,512]{1,0:T(8,128)(2,1)S(1)} %collective-permute-done.2.refs_9_) | copy-start | bytes 835588
  31.2 13.8 %collective-permute-start.4 = (bf16[272,512]{1,0:T(8,128)(2,1)S(1)}, bf16[272,512]{1,0:T(8,128)(2,1)S(1)}, u32[]{:S(2)}, u32[]{:S(2)}) collective-permute-start(bf16[272,512]{1,0:T(8,128)(2,1)S(1)} %collective-permute-done.2.refs_9_), channel_id=1, source_target_pairs={{0,4},{2,6},{4,0},{6,2},{8,12},{10,14},{12,8},{14,10},{1,5},{3,7},... | collective-permute-start | bytes 835592 | tf_op jit(solution)/shard_map/ppermute | solution.py:352
  33.4 23.8 %copy-start.14 = (bf16[272,512]{1,0:T(8,128)(2,1)}, bf16[272,512]{1,0:T(8,128)(2,1)S(1)}, u32[]{:S(2)}) copy-start(bf16[272,512]{1,0:T(8,128)(2,1)S(1)} %collective-permute-done.5.refs_13_) | copy-start | bytes 835588
  33.4 11.6 %collective-permute-start.6 = (bf16[272,512]{1,0:T(8,128)(2,1)S(1)}, bf16[272,512]{1,0:T(8,128)(2,1)S(1)}, u32[]{:S(2)}, u32[]{:S(2)}) collective-permute-start(bf16[272,512]{1,0:T(8,128)(2,1)S(1)} %collective-permute-done.2.refs_9_), channel_id=1, source_target_pairs={{0,16},{16,0},{1,17},{17,1},{2,18},{18,2},{3,19},{19,3},{4,20},{20... | collective-permute-start | bytes 835592 | tf_op jit(solution)/shard_map/ppermute | solution.py:355
  42.8 26.1 %copy-start.13 = (bf16[272,512]{1,0:T(8,128)(2,1)}, bf16[272,512]{1,0:T(8,128)(2,1)S(1)}, u32[]{:S(2)}) copy-start(bf16[272,512]{1,0:T(8,128)(2,1)S(1)} %collective-permute-done.7.refs_10_) | copy-start | bytes 835588
  42.8 16.4 %copy-start.15 = (bf16[272,512]{1,0:T(8,128)(2,1)}, bf16[272,512]{1,0:T(8,128)(2,1)S(1)}, u32[]{:S(2)}) copy-start(bf16[272,512]{1,0:T(8,128)(2,1)S(1)} %collective-permute-done.9.refs_14_) | copy-start | bytes 835588
  42.8 8.6 %collective-permute-start.10 = (bf16[272,512]{1,0:T(8,128)(2,1)S(1)}, bf16[272,512]{1,0:T(8,128)(2,1)S(1)}, u32[]{:S(2)}, u32[]{:S(2)}) collective-permute-start(bf16[272,512]{1,0:T(8,128)(2,1)S(1)} %collective-permute-done.7.refs_10_), channel_id=1, source_target_pairs={{0,4},{2,6},{4,0},{6,2},{8,12},{10,14},{12,8},{14,10},{1,5},{3,7},... | collective-permute-start | bytes 835592 | tf_op jit(solution)/shard_map/ppermute | solution.py:352
  43.1 14.1 %collective-permute-start.12 = (bf16[272,512]{1,0:T(8,128)(2,1)S(1)}, bf16[272,512]{1,0:T(8,128)(2,1)S(1)}, u32[]{:S(2)}, u32[]{:S(2)}) collective-permute-start(bf16[272,512]{1,0:T(8,128)(2,1)S(1)} %collective-permute-done.7.refs_10_), channel_id=1, source_target_pairs={{0,16},{16,0},{1,17},{17,1},{2,18},{18,2},{3,19},{19,3},{4,20},{20... | collective-permute-start | bytes 835592 | tf_op jit(solution)/shard_map/ppermute | solution.py:355
  45.0 14.1 %copy-start.16 = (bf16[272,512]{1,0:T(8,128)(2,1)}, bf16[272,512]{1,0:T(8,128)(2,1)S(1)}, u32[]{:S(2)}) copy-start(bf16[272,512]{1,0:T(8,128)(2,1)S(1)} %collective-permute-done.4.refs_11_) | copy-start | bytes 835588
  45.0 6.3 %copy-start.17 = (bf16[272,512]{1,0:T(8,128)(2,1)}, bf16[272,512]{1,0:T(8,128)(2,1)S(1)}, u32[]{:S(2)}) copy-start(bf16[272,512]{1,0:T(8,128)(2,1)S(1)} %collective-permute-done.6.refs_15_) | copy-start | bytes 835588
  51.3 12.9 %copy-start.18 = (bf16[272,512]{1,0:T(8,128)(2,1)}, bf16[272,512]{1,0:T(8,128)(2,1)S(1)}, u32[]{:S(2)}) copy-start(bf16[272,512]{1,0:T(8,128)(2,1)S(1)} %collective-permute-done.10.refs_12_) | copy-start | bytes 835588
  51.3 7.8 %collective-permute-start.11 = (bf16[272,512]{1,0:T(8,128)(2,1)S(1)}, bf16[272,512]{1,0:T(8,128)(2,1)S(1)}, u32[]{:S(2)}, u32[]{:S(2)}) collective-permute-start(bf16[272,512]{1,0:T(8,128)(2,1)S(1)} %collective-permute-done.4.refs_11_), channel_id=1, source_target_pairs={{0,16},{16,0},{1,17},{17,1},{2,18},{18,2},{3,19},{19,3},{4,20},{20... | collective-permute-start | bytes 835592 | tf_op jit(solution)/shard_map/ppermute | solution.py:355
  53.5 3.7 %collective-permute-start.13 = (f32[2,256]{1,0:T(2,128)S(1)}, f32[2,256]{1,0:T(2,128)S(1)}, u32[]{:S(2)}, u32[]{:S(2)}) collective-permute-start(f32[2,256]{1,0:T(2,128)S(1)} %get-tuple-element.43), channel_id=1, source_target_pairs={{0,2},{2,0},{4,6},{6,4},{8,10},{10,8},{12,14},{14,12},{1,3},{3,1},... | collective-permute-start | bytes 6152 | tf_op jit(solution)/shard_map/ppermute | solution.py:349
  57.2 1.9 %copy-start.19 = (bf16[272,512]{1,0:T(8,128)(2,1)}, bf16[272,512]{1,0:T(8,128)(2,1)S(1)}, u32[]{:S(2)}) copy-start(bf16[272,512]{1,0:T(8,128)(2,1)S(1)} %collective-permute-done.12.refs_16_) | copy-start | bytes 835588
  59.1 5.1 %copy-start.20 = (bf16[272,512]{1,0:T(8,128)(2,1)}, bf16[272,512]{1,0:T(8,128)(2,1)S(1)}, u32[]{:S(2)}) copy-start(bf16[272,512]{1,0:T(8,128)(2,1)S(1)} %collective-permute-done.11.refs_17_) | copy-start | bytes 835588
  59.1 9.7 %collective-permute-start.14 = (bf16[256,4096]{1,0:T(8,128)(2,1)}, bf16[256,4096]{1,0:T(8,128)(2,1)}, u32[]{:S(2)}, u32[]{:S(2)}) collective-permute-start(bf16[256,4096]{1,0:T(8,128)(2,1)} %collective-permute-done.1.refs_3_), channel_id=1, source_target_pairs={{0,1},{1,0},{2,3},{3,2},{4,5},{5,4},{6,7},{7,6},{8,9},{9,8},{10,11... | collective-permute-start | bytes 6291464 | tf_op jit(solution)/shard_map/ppermute | solution.py:358
  59.2 5.0 %collective-permute-start.15 = (f32[2,256]{1,0:T(2,128)S(1)}, f32[2,256]{1,0:T(2,128)S(1)}, u32[]{:S(2)}, u32[]{:S(2)}) collective-permute-start(f32[2,256]{1,0:T(2,128)S(1)} %bitcast.15), channel_id=1, source_target_pairs={{0,1},{1,0},{2,3},{3,2},{4,5},{5,4},{6,7},{7,6},{8,9},{9,8},{10,11... | collective-permute-start | bytes 6152 | tf_op jit(solution)/shard_map/ppermute | solution.py:358
  60.1 8.7 %collective-permute-start.16 = (bf16[272,512]{1,0:T(8,128)(2,1)S(1)}, bf16[272,512]{1,0:T(8,128)(2,1)}, u32[]{:S(2)}, u32[]{:S(2)}) collective-permute-start(bf16[272,512]{1,0:T(8,128)(2,1)S(1)} %collective-permute-done.10.refs_12_), channel_id=1, source_target_pairs={{0,16},{16,0},{1,17},{17,1},{2,18},{18,2},{3,19},{19,3},{4,20},{20... | collective-permute-start | bytes 835592 | tf_op jit(solution)/shard_map/ppermute | solution.py:355
  75.6 8.9 %copy-start.6 = (f32[4,2,128,128]{3,2,1,0:T(8,128)S(1)}, f32[4,2,128,128]{3,2,1,0:T(8,128)}, u32[]{:S(2)}) copy-start(f32[4,2,128,128]{3,2,1,0:T(8,128)} %get-tuple-element.47.keep_ref) | copy-start | bytes 1572868
  75.6 8.9 %copy-start.8 = (s32[8]{0:T(128)S(1)}, s32[8]{0:T(128)}, u32[]{:S(2)}) copy-start(s32[8]{0:T(128)} %owner_ref.3) | copy-start | bytes 100
  75.6 8.9 %collective-permute-start.17 = (bf16[4,2,128,128]{3,2,1,0:T(8,128)(2,1)}, bf16[4,2,128,128]{3,2,1,0:T(8,128)(2,1)S(1)}, u32[]{:S(2)}, u32[]{:S(2)}) collective-permute-start(bf16[4,2,128,128]{3,2,1,0:T(8,128)(2,1)} %get-tuple-element.48), channel_id=1, source_target_pairs={{0,2},{2,0},{4,6},{6,4},{8,10},{10,8},{12,14},{14,12},{1,3},{3,1},... | collective-permute-start | bytes 786440 | tf_op jit(solution)/shard_map/ppermute | solution.py:349
  83.2 7.4 %collective-permute-start.21 = (bf16[4,2,128,128]{3,2,1,0:T(8,128)(2,1)}, bf16[4,2,128,128]{3,2,1,0:T(8,128)(2,1)S(1)}, u32[]{:S(2)}, u32[]{:S(2)}) collective-permute-start(bf16[4,2,128,128]{3,2,1,0:T(8,128)(2,1)} %get-tuple-element.55), channel_id=1, source_target_pairs={{0,2},{2,0},{4,6},{6,4},{8,10},{10,8},{12,14},{14,12},{1,3},{3,1},... | collective-permute-start | bytes 786440 | tf_op jit(solution)/shard_map/ppermute | solution.py:349
  85.3 9.9 %collective-permute-start.18 = (bf16[256,128]{1,0:T(8,128)(2,1)S(1)}, bf16[256,128]{1,0:T(8,128)(2,1)S(1)}, u32[]{:S(2)}, u32[]{:S(2)}) collective-permute-start(bf16[256,128]{1,0:T(8,128)(2,1)S(1)} %get-tuple-element.50), channel_id=1, source_target_pairs={{0,4},{2,6},{4,0},{6,2},{8,12},{10,14},{12,8},{14,10},{1,5},{3,7},... | collective-permute-start | bytes 196616 | tf_op jit(solution)/shard_map/ppermute | solution.py:352
  85.6 9.6 %collective-permute-start.19 = (bf16[256,128]{1,0:T(8,128)(2,1)S(1)}, bf16[256,128]{1,0:T(8,128)(2,1)S(1)}, u32[]{:S(2)}, u32[]{:S(2)}) collective-permute-start(bf16[256,128]{1,0:T(8,128)(2,1)S(1)} %get-tuple-element.51), channel_id=1, source_target_pairs={{0,8},{2,10},{4,12},{6,14},{8,0},{10,2},{12,4},{14,6},{1,9},{3,11}... | collective-permute-start | bytes 196616 | tf_op jit(solution)/shard_map/ppermute | solution.py:352
  88.9 6.6 %collective-permute-start.20 = (bf16[256,128]{1,0:T(8,128)(2,1)S(1)}, bf16[256,128]{1,0:T(8,128)(2,1)S(1)}, u32[]{:S(2)}, u32[]{:S(2)}) collective-permute-start(bf16[256,128]{1,0:T(8,128)(2,1)S(1)} %get-tuple-element.52), channel_id=1, source_target_pairs={{0,12},{2,14},{4,8},{6,10},{8,4},{10,6},{12,0},{14,2},{1,13},{3,15... | collective-permute-start | bytes 196616 | tf_op jit(solution)/shard_map/ppermute | solution.py:352
  90.6 1.0 %copy-start.5 = (f32[4,2,128,128]{3,2,1,0:T(8,128)S(1)}, f32[4,2,128,128]{3,2,1,0:T(8,128)}, u32[]{:S(2)}) copy-start(f32[4,2,128,128]{3,2,1,0:T(8,128)} %get-tuple-element.54.keep_ref) | copy-start | bytes 1572868
  92.2 6.6 %collective-permute-start.23 = (bf16[256,128]{1,0:T(8,128)(2,1)S(1)}, bf16[256,128]{1,0:T(8,128)(2,1)S(1)}, u32[]{:S(2)}, u32[]{:S(2)}) collective-permute-start(bf16[256,128]{1,0:T(8,128)(2,1)S(1)} %get-tuple-element.60), channel_id=1, source_target_pairs={{0,8},{2,10},{4,12},{6,14},{8,0},{10,2},{12,4},{14,6},{1,9},{3,11}... | collective-permute-start | bytes 196616 | tf_op jit(solution)/shard_map/ppermute | solution.py:352
  94.1 6.2 %collective-permute-start.24 = (bf16[256,128]{1,0:T(8,128)(2,1)S(1)}, bf16[256,128]{1,0:T(8,128)(2,1)S(1)}, u32[]{:S(2)}, u32[]{:S(2)}) collective-permute-start(bf16[256,128]{1,0:T(8,128)(2,1)S(1)} %get-tuple-element.61), channel_id=1, source_target_pairs={{0,12},{2,14},{4,8},{6,10},{8,4},{10,6},{12,0},{14,2},{1,13},{3,15... | collective-permute-start | bytes 196616 | tf_op jit(solution)/shard_map/ppermute | solution.py:352
  95.5 5.0 %collective-permute-start.22 = (bf16[256,128]{1,0:T(8,128)(2,1)S(1)}, bf16[256,128]{1,0:T(8,128)(2,1)S(1)}, u32[]{:S(2)}, u32[]{:S(2)}) collective-permute-start(bf16[256,128]{1,0:T(8,128)(2,1)S(1)} %get-tuple-element.59), channel_id=1, source_target_pairs={{0,4},{2,6},{4,0},{6,2},{8,12},{10,14},{12,8},{14,10},{1,5},{3,7},... | collective-permute-start | bytes 196616 | tf_op jit(solution)/shard_map/ppermute | solution.py:352

commit v6 on v5

--- a/solution.py
+++ b/solution.py
@@ -189,9 +189,87 @@
     return group // 4, group % 4 // 2, group % 2
 
 
+def shard_pairs(d, mine, theirs, y, columns, picked, weights, gains):
+    width = 2 * columns
+    half = (mine[0].shape[0] - GAIN_ROWS * (2 // len(mine))) * len(mine)
+    shard = 2 * half
+    first = d * shard
+    rows = half // len(mine)
+    gain_parts = shard // width // len(mine)
+    pairs = []
+    for i, packed in enumerate(mine):
+        for p in range(gain_parts):
+            lanes = pl.ds(first + (i * gain_parts + p) * width, width)
+            gain_rows = pl.ds(rows + p * GAIN_ROWS, GAIN_ROWS)
+            pairs.append((packed.at[gain_rows, :], gains.at[:, lanes]))
+    for blocks, side in ((mine if d > 0 else [], y), (theirs, 1 - y)):
+        for i, packed in enumerate(blocks):
+            start = pl.multiple_of(first + side * half + i * rows, rows)
+            target = weights.at[pl.ds(start, rows), :]
+            pairs.append((packed.at[pl.ds(0, rows), picked], target))
+    return pairs
+
+
+def early_kernel(shard, counts, *refs):
+    refs = list(refs)
+    sources = [refs.pop(0) for _ in range(2)]
+    key_ref, value_ref = refs.pop(0), refs.pop(0)
+    mine = [[refs.pop(0) for _ in range(count)] for count in counts]
+    theirs = [[]] + [[refs.pop(0) for _ in range(count)] for count in counts[1:]]
+    total, weights, gains, raw, sems = refs
+    y, x, z, _ = here()
+    columns = key_ref.shape[1]
+    device_rows = sources[0].shape[0]
+    pairs, ends = [], [0]
+    for d in range(len(counts)):
+        if d == 0:
+            for k, weight_ref in enumerate((key_ref, value_ref)):
+                target = weights.at[pl.ds(0, shard), pl.ds(k * columns, columns)]
+                pairs.append((weight_ref, target))
+        picked = pl.ds(0, 2 * columns)
+        pairs += shard_pairs(d, mine[d], theirs[d], y, columns, picked, weights, gains)
+        lanes = pl.ds(pl.multiple_of((2 * jnp.bitwise_xor(z, d) + x) * shard, shard), shard)
+        for i, source in enumerate(sources):
+            target = raw.at[pl.ds(i * device_rows, device_rows), pl.ds(d * shard, shard)]
+            pairs.append((source.at[:, lanes], target))
+        ends.append(len(pairs))
+    copies = run_copies(pairs, sems)
+    for d in range(len(counts)):
+        wait_all(copies[ends[d] : ends[d + 1]])
+        block = slice(d * shard, (d + 1) * shard)
+        product = jnp.dot(
+            raw[:, block] * gains[0:1, block], weights[block, :], preferred_element_type=jnp.float32
+        )
+        total[...] = product if d == 0 else total[...] + product
+
+
+def early(sources, w_key, w_value, mine, theirs):
+    shard, columns = w_key.shape
+    counts = tuple(len(blocks) for blocks in mine)
+    features = shard * len(mine)
+    rows = 2 * sources[0].shape[0]
+    operands = [
+        *sources, w_key, w_value, *[packed for blocks in mine + theirs for packed in blocks],
+    ]
+    copies = len(mine) * (shard // (2 * columns) + 2) + 2 + 2 * sum(counts)
+    return pl.pallas_call(
+        functools.partial(early_kernel, shard, counts),
+        in_specs=[HBM] * len(operands),
+        out_specs=VMEM,
+        out_shape=jax.ShapeDtypeStruct((rows, 2 * columns), jnp.float32),
+        scratch_shapes=[
+            pltpu.VMEM((features, 2 * columns), jnp.bfloat16),
+            pltpu.VMEM((GAIN_ROWS, features), jnp.bfloat16),
+            pltpu.VMEM((rows, features), jnp.bfloat16),
+            pltpu.SemaphoreType.DMA((copies,)),
+        ],
+        compiler_params=pltpu.CompilerParams(vmem_limit_bytes=VMEM_LIMIT),
+    )(*operands)
+
+
 def multiply_kernel(shard, counts, which, *refs):
     refs = list(refs)
-    owner_ref = refs.pop(0)
+    owner_ref, before_ref = refs.pop(0), refs.pop(0)
     sources = [refs.pop(0) for _ in range(4)]
     weight_ref = refs.pop(0)
     line = len(counts)
@@ -199,31 +277,20 @@
     theirs = [[]] + [[refs.pop(0) for _ in range(count)] for count in counts[1:]]
     keep, send, weights, gains, raw, total, sems = refs
     y, x, z, c = here()
-    half = shard // 2
     columns = weight_ref.shape[1]
-    width = 2 * columns
     _, _, page, _ = keep.shape
     device_rows = 2 * page
-    pairs, ends = [], []
+    picked = pl.ds(which * columns, columns)
+    pairs, ends = [(before_ref.at[:, picked], total.at[pl.ds(0, 2 * device_rows), :])], []
     for d in range(line):
         first = d * shard
-        rows = half // counts[d]
-        gain_parts = shard // width // counts[d]
-        for i, packed in enumerate(mine[d]):
-            for p in range(gain_parts):
-                lanes = pl.ds(first + (i * gain_parts + p) * width, width)
-                gain_rows = pl.ds(rows + p * GAIN_ROWS, GAIN_ROWS)
-                pairs.append((packed.at[gain_rows, :], gains.at[:, lanes]))
         if d == 0:
             pairs.append((weight_ref, weights.at[pl.ds(first, shard), :]))
-        picked = pl.ds(which * columns, columns)
-        for blocks, side in ((mine[d] if d > 0 else [], y), (theirs[d], 1 - y)):
-            for i, packed in enumerate(blocks):
-                start = pl.multiple_of(first + side * half + i * rows, rows)
-                target = weights.at[pl.ds(start, rows), :]
-                pairs.append((packed.at[pl.ds(0, rows), picked], target))
+        pairs += shard_pairs(d, mine[d], theirs[d], y, columns, picked, weights, gains)
         place_z = jnp.bitwise_xor(z, d)
         for i, source in enumerate(sources):
+            if i < 2 and d < line - 1:
+                continue
             block = 2 * place_z + x if i < 2 else place_z
             lanes = pl.ds(pl.multiple_of(block * shard, shard), shard)
             target = raw.at[pl.ds(i * device_rows, device_rows), pl.ds(first, shard)]
@@ -233,7 +300,7 @@
     for d in range(line):
         wait_all(copies[(ends[d - 1] if d > 0 else 0) : ends[d]])
         block = slice(d * shard, (d + 1) * shard)
-        for i in range(2):
+        for i in range(0 if d == line - 1 else 1, 2):
             span = slice(i * 2 * device_rows, (i + 1) * 2 * device_rows)
             product = jnp.dot(
                 raw[span, block] * gains[0:1, block],
@@ -253,17 +320,18 @@
                 )
 
 
-def multiply(owner_map, sources, weight, which, mine, theirs):
+def multiply(owner_map, before, sources, weight, which, mine, theirs):
     shard, columns = weight.shape
     line = len(mine)
     device_rows = sources[0].shape[0]
     operands = [
+        before,
         *sources, weight,
         *[packed for blocks in mine + theirs for packed in blocks],
     ]
     shape = (line, 2, device_rows // 2, HD)
     counts = tuple(len(blocks) for blocks in mine)
-    copies = line * (shard // (2 * columns)) + 1 + 2 * sum(counts) + 4 * line
+    copies = 1 + line * (shard // (2 * columns)) + 1 + 2 * sum(counts) + 4 * line
     return pl.pallas_call(
         functools.partial(multiply_kernel, shard, counts, which),
         in_specs=[SMEM] + [HBM] * len(operands),
@@ -395,12 +463,13 @@
     sources = [hidden, other, own_away, other_away]
     mine = [[packed], [near_0, near_1], [far_0, far_1], [corner_0, corner_1]]
     theirs = [[near_y_0, near_y_1], [far_y_0, far_y_1], [corner_y_0, corner_y_1]]
+    before = early([hidden, other], w_key, w_value, mine[:-1], theirs[:-1])
     key_keep, key_send = multiply(
-        owner_map, sources, after(w_key, scale, cosine, sine), 0, mine, theirs
+        owner_map, before, sources, after(w_key, scale, cosine, sine), 0, mine, theirs
     )
     key_came = over_x(key_send)
     value_keep, value_send = multiply(
-        owner_map, sources, after(w_value, key_send), 1, mine, theirs
+        owner_map, before, sources, after(w_value, key_send), 1, mine, theirs
     )
     value_came = over_x(value_send)
     keys = finish(owner_map, key_keep, key_came, scale, cosine, sine)

time: 102 us -> 101 us (level)
  waiting for transfers between devices: 42.1 us -> 37.9 us
  Pallas kernels: 16.8 us -> 20 us
    pallas_call x0 -> x1, Pallas kernels: none -> 4.75 us  [early(): pl.pallas_call(functools.partial(early_kernel, shard, counts), in_specs=[...]
    ppermute x6, waiting for transfers between devices: 7.67 us -> 3.47 us  [over_y(): return lax.ppermute(values, 'group', [(0, 1), (1, 0)])]
    pallas_call x2, Pallas kernels: 13.5 us -> 11.9 us  [multiply(): pl.pallas_call(functools.partial(multiply_kernel, shard, counts, which),...]
    unnamed x43 -> x41, local copies, waits for them, and re-layouts: 4.12 us -> 4.79 us
  transfers between devices with their start and end apart: 25 -> 25, of which waited for: 14 -> 14; matrix products, arithmetic and copies ran while one was open for 4% -> 4% of each run, Pallas kernels for 9% -> 13%
where the time goes in v6:
time: 101 us
  waiting for transfers between devices  37.9 us (38%)
  starting transfers between devices  31.8 us (31%)
  Pallas kernels  20 us (20%)
  local copies, waits for them, and re-layouts  5.18 us (5%)
  other arithmetic  3.65 us (4%)
  between operations  2.25 us (2%)
    ppermute x12, waiting for transfers between devices, over_z(): lax.ppermute(values, 'tok', [(t, t ^ 2 * distance) for t in range(tok_cou...  30 us
    ppermute x12, starting transfers between devices, over_z(): lax.ppermute(values, 'tok', [(t, t ^ 2 * distance) for t in range(tok_cou...  16.6 us
    pallas_call x2, Pallas kernels, multiply(): pl.pallas_call(functools.partial(multiply_kernel, shard, counts, which),...  11.9 us
    ppermute x6, starting transfers between devices, over_y(): return lax.ppermute(values, 'group', [(0, 1), (1, 0)])  9.07 us
    ppermute x4, starting transfers between devices, over_x(): return lax.ppermute(values, 'tok', [(t, t ^ 1) for t in range(tok_count)])  5.48 us
    unnamed x41, local copies, waits for them, and re-layouts  4.79 us
    pallas_call x1, Pallas kernels, early(): pl.pallas_call(functools.partial(early_kernel, shard, counts), in_specs=[...  4.75 us
    ppermute x4, waiting for transfers between devices, over_x(): return lax.ppermute(values, 'tok', [(t, t ^ 1) for t in range(tok_count)])  4.43 us
  transfers between devices with their start and end apart: 25, of which 14 were waited for; matrix products, arithmetic and copies ran while one was open for 4% of the time, Pallas kernels for 13%

profile of v6, /device:TPU:0, one launch (start us, length us, event | category | flops | bytes accessed | tf_op | source)
XLA Modules:
  0.0 100.7 jit_solution(13633307114989285449)
XLA Ops:
  0.6 0.5 collective-permute-start
  1.1 2.2 %copy-done = bf16[256,8192]{1,0:T(8,128)(2,1)S(1)} copy-done((bf16[256,8192]{1,0:T(8,128)(2,1)S(1)}, bf16[256,8192]{1,0:T(8,128)(2,1)}, u32[]{:S(2)}) %copy-start) | copy-done | bytes 4194328
  3.6 2.6 %collective-permute-start.9 = (bf16[256,4096]{1,0:T(8,128)(2,1)S(1)}, bf16[256,4096]{1,0:T(8,128)(2,1)}, u32[]{:S(2)}, u32[]{:S(2)}) collective-permute-start(bf16[256,4096]{1,0:T(8,128)(2,1)S(1)} %shard_map.86), channel_id=1, source_target_pairs={{0,2},{2,0},{4,6},{6,4},{8,10},{10,8},{12,14},{14,12},{1,3},{3,1},... | collective-permute-start | bytes 6291464 | tf_op jit(solution)/shard_map/ppermute | solution.py:417
  7.1 0.8 copy-done.2
  7.9 1.6 %collective-permute-start.1 = (bf16[272,512]{1,0:T(8,128)(2,1)S(1)}, bf16[272,512]{1,0:T(8,128)(2,1)S(1)}, u32[]{:S(2)}, u32[]{:S(2)}) collective-permute-start(bf16[272,512]{1,0:T(8,128)(2,1)S(1)} %get-tuple-element.34), channel_id=1, source_target_pairs={{0,4},{2,6},{4,0},{6,2},{8,12},{10,14},{12,8},{14,10},{1,5},{3,7},... | collective-permute-start | bytes 835592 | tf_op jit(solution)/shard_map/ppermute | solution.py:420
  9.5 1.6 %collective-permute-start.2 = (bf16[272,512]{1,0:T(8,128)(2,1)S(1)}, bf16[272,512]{1,0:T(8,128)(2,1)S(1)}, u32[]{:S(2)}, u32[]{:S(2)}) collective-permute-start(bf16[272,512]{1,0:T(8,128)(2,1)S(1)} %get-tuple-element.37), channel_id=1, source_target_pairs={{0,4},{2,6},{4,0},{6,2},{8,12},{10,14},{12,8},{14,10},{1,5},{3,7},... | collective-permute-start | bytes 835592 | tf_op jit(solution)/shard_map/ppermute | solution.py:420
  11.1 2.6 %collective-permute-start.3 = (bf16[272,512]{1,0:T(8,128)(2,1)S(1)}, bf16[272,512]{1,0:T(8,128)(2,1)S(1)}, u32[]{:S(2)}, u32[]{:S(2)}) collective-permute-start(bf16[272,512]{1,0:T(8,128)(2,1)S(1)} %get-tuple-element.34), channel_id=1, source_target_pairs={{0,8},{2,10},{4,12},{6,14},{8,0},{10,2},{12,4},{14,6},{1,9},{3,11}... | collective-permute-start | bytes 835592 | tf_op jit(solution)/shard_map/ppermute | solution.py:420
  13.7 9.7 %collective-permute-done.1.refs_5_.refs_8_ = bf16[272,512]{1,0:T(8,128)(2,1)S(1)} collective-permute-done((bf16[272,512]{1,0:T(8,128)(2,1)S(1)}, bf16[272,512]{1,0:T(8,128)(2,1)S(1)}, u32[]{:S(2)}, u32[]{:S(2)}) %collective-permute-start.1) | collective-permute-done | bytes 278560 | tf_op jit(solution)/shard_map/ppermute | solution.py:420
  23.4 1.7 %collective-permute-start.4 = (bf16[272,512]{1,0:T(8,128)(2,1)S(1)}, bf16[272,512]{1,0:T(8,128)(2,1)S(1)}, u32[]{:S(2)}, u32[]{:S(2)}) collective-permute-start(bf16[272,512]{1,0:T(8,128)(2,1)S(1)} %get-tuple-element.37), channel_id=1, source_target_pairs={{0,8},{2,10},{4,12},{6,14},{8,0},{10,2},{12,4},{14,6},{1,9},{3,11}... | collective-permute-start | bytes 835592 | tf_op jit(solution)/shard_map/ppermute | solution.py:420
  25.1 1.5 %collective-permute-start.5 = (bf16[272,512]{1,0:T(8,128)(2,1)S(1)}, bf16[272,512]{1,0:T(8,128)(2,1)S(1)}, u32[]{:S(2)}, u32[]{:S(2)}) collective-permute-start(bf16[272,512]{1,0:T(8,128)(2,1)S(1)} %collective-permute-done.1.refs_5_.refs_8_), channel_id=1, source_target_pairs={{0,16},{16,0},{1,17},{17,1},{2,18},{18,2},{3,19},{19,3},{4,20},{20... | collective-permute-start | bytes 835592 | tf_op jit(solution)/shard_map/ppermute | solution.py:423
  26.6 2.2 %collective-permute-done.2.refs_6_.refs_9_ = bf16[272,512]{1,0:T(8,128)(2,1)S(1)} collective-permute-done((bf16[272,512]{1,0:T(8,128)(2,1)S(1)}, bf16[272,512]{1,0:T(8,128)(2,1)S(1)}, u32[]{:S(2)}, u32[]{:S(2)}) %collective-permute-start.2) | collective-permute-done | bytes 278560 | tf_op jit(solution)/shard_map/ppermute | solution.py:420
  28.7 1.6 %collective-permute-start.6 = (bf16[272,512]{1,0:T(8,128)(2,1)S(1)}, bf16[272,512]{1,0:T(8,128)(2,1)S(1)}, u32[]{:S(2)}, u32[]{:S(2)}) collective-permute-start(bf16[272,512]{1,0:T(8,128)(2,1)S(1)} %collective-permute-done.2.refs_6_.refs_9_), channel_id=1, source_target_pairs={{0,16},{16,0},{1,17},{17,1},{2,18},{18,2},{3,19},{19,3},{4,20},{20... | collective-permute-start | bytes 835592 | tf_op jit(solution)/shard_map/ppermute | solution.py:423
  30.3 0.9 multiply_reduce_fusion
  31.2 0.8 collective-permute-start.10
  32.0 1.4 %collective-permute-done.5.refs_9_.refs_14_ = bf16[272,512]{1,0:T(8,128)(2,1)S(1)} collective-permute-done((bf16[272,512]{1,0:T(8,128)(2,1)S(1)}, bf16[272,512]{1,0:T(8,128)(2,1)S(1)}, u32[]{:S(2)}, u32[]{:S(2)}) %collective-permute-start.5) | collective-permute-done | bytes 278560 | tf_op jit(solution)/shard_map/ppermute | solution.py:423
  33.4 1.4 %collective-permute-start.7 = (bf16[272,512]{1,0:T(8,128)(2,1)S(1)}, bf16[272,512]{1,0:T(8,128)(2,1)S(1)}, u32[]{:S(2)}, u32[]{:S(2)}) collective-permute-start(bf16[272,512]{1,0:T(8,128)(2,1)S(1)} %collective-permute-done.3.refs_7_.refs_10_), channel_id=1, source_target_pairs={{0,16},{16,0},{1,17},{17,1},{2,18},{18,2},{3,19},{19,3},{4,20},{20... | collective-permute-start | bytes 835592 | tf_op jit(solution)/shard_map/ppermute | solution.py:423
  34.8 8.0 %collective-permute-done.4.refs_8_.refs_11_ = bf16[272,512]{1,0:T(8,128)(2,1)S(1)} collective-permute-done((bf16[272,512]{1,0:T(8,128)(2,1)S(1)}, bf16[272,512]{1,0:T(8,128)(2,1)S(1)}, u32[]{:S(2)}, u32[]{:S(2)}) %collective-permute-start.4) | collective-permute-done | bytes 278560 | tf_op jit(solution)/shard_map/ppermute | solution.py:420
  43.1 1.5 %collective-permute-start.8 = (bf16[272,512]{1,0:T(8,128)(2,1)S(1)}, bf16[272,512]{1,0:T(8,128)(2,1)S(1)}, u32[]{:S(2)}, u32[]{:S(2)}) collective-permute-start(bf16[272,512]{1,0:T(8,128)(2,1)S(1)} %collective-permute-done.4.refs_8_.refs_11_), channel_id=1, source_target_pairs={{0,16},{16,0},{1,17},{17,1},{2,18},{18,2},{3,19},{19,3},{4,20},{20... | collective-permute-start | bytes 835592 | tf_op jit(solution)/shard_map/ppermute | solution.py:423
  44.6 0.4 collective-permute-done.10.refs_12_
  45.0 6.4 %collective-permute-done.11.refs_13_ = bf16[272,512]{1,0:T(8,128)(2,1)} collective-permute-done((bf16[272,512]{1,0:T(8,128)(2,1)S(1)}, bf16[272,512]{1,0:T(8,128)(2,1)}, u32[]{:S(2)}, u32[]{:S(2)}) %collective-permute-start.11) | collective-permute-done | bytes 278560 | tf_op jit(solution)/shard_map/ppermute | solution.py:420
  51.5 1.5 %collective-permute-start.12 = (bf16[272,512]{1,0:T(8,128)(2,1)S(1)}, bf16[272,512]{1,0:T(8,128)(2,1)S(1)}, u32[]{:S(2)}, u32[]{:S(2)}) collective-permute-start(bf16[272,512]{1,0:T(8,128)(2,1)S(1)} %collective-permute-done.10.refs_12_), channel_id=1, source_target_pairs={{0,16},{16,0},{1,17},{17,1},{2,18},{18,2},{3,19},{19,3},{4,20},{20... | collective-permute-start | bytes 835592 | tf_op jit(solution)/shard_map/ppermute | solution.py:423
  53.7 0.8 collective-permute-start.13
  54.4 2.9 %collective-permute-done.13 = f32[2,256]{1,0:T(2,128)S(1)} collective-permute-done((f32[2,256]{1,0:T(2,128)S(1)}, f32[2,256]{1,0:T(2,128)S(1)}, u32[]{:S(2)}, u32[]{:S(2)}) %collective-permute-start.13) | collective-permute-done | bytes 2080 | tf_op jit(solution)/shard_map/ppermute | solution.py:417
  57.3 1.8 %collective-permute-done.12.refs_18_ = bf16[272,512]{1,0:T(8,128)(2,1)S(1)} collective-permute-done((bf16[272,512]{1,0:T(8,128)(2,1)S(1)}, bf16[272,512]{1,0:T(8,128)(2,1)S(1)}, u32[]{:S(2)}, u32[]{:S(2)}) %collective-permute-start.12) | collective-permute-done | bytes 278560 | tf_op jit(solution)/shard_map/ppermute | solution.py:423
  59.2 0.7 copy-done.19
  60.3 1.5 %collective-permute-start.16 = (bf16[272,512]{1,0:T(8,128)(2,1)}, bf16[272,512]{1,0:T(8,128)(2,1)}, u32[]{:S(2)}, u32[]{:S(2)}) collective-permute-start(bf16[272,512]{1,0:T(8,128)(2,1)} %collective-permute-done.11.refs_13_), channel_id=1, source_target_pairs={{0,16},{16,0},{1,17},{17,1},{2,18},{18,2},{3,19},{19,3},{4,20},{20... | collective-permute-start | bytes 835592 | tf_op jit(solution)/shard_map/ppermute | solution.py:423
  61.9 2.2 %fusion.5 = (f32[8,128,64]{2,1,0:T(8,128)S(1)}, f32[8,128,64]{2,1,0:T(8,128)S(1)}, f32[8,128,64]{2,1,0:T(8,128)S(1)}) fusion(f32[64]{0:T(128)S(1)} %multiply_power_fusion, f32[8,128]{1,0:T(8,128)S(1)} %add_convert_fusion), kind=kLoop, calls=%fused_computation.10 | loop fusion | flops 524288 | bytes 790784 | tf_op jit(solution)/shard_map/neg | solution.py:457
  64.0 0.3 pad_maximum_fusion
  64.7 4.8 %shard_map.88.refs_1_ = f32[512,512]{1,0:T(8,128)} custom-call(bf16[256,8192]{1,0:T(8,128)(2,1)} %refs_2_.5, bf16[256,8192]{1,0:T(8,128)(2,1)} %copy-done.9, bf16[1024,256]{1,0:T(8,128)(2,1)} %refs_6_, bf16[1024,256]{1,0:T(8,128)(2,1)} %refs_6_.1, bf16[544,512]{1,0:T(8,128)(2,1)} %copy-done.2, bf16[272,512]{1,0:T(8,128)(2,1)} %copy-done.10, ...), custom_call_target="tpu_custom_call" | custom-call | tf_op jit(solution)/shard_map/pallas_call | solution.py:255
  69.7 6.0 %shard_map.89 = (f32[4,2,128,128]{3,2,1,0:T(8,128)}, bf16[4,2,128,128]{3,2,1,0:T(8,128)(2,1)}) custom-call(s32[8]{0:T(128)} %owner_ref.3, f32[512,512]{1,0:T(8,128)} %shard_map.88.refs_1_, bf16[256,8192]{1,0:T(8,128)(2,1)} %refs_2_.5, bf16[256,8192]{1,0:T(8,128)(2,1)} %copy-done.9, bf16[256,4096]{1,0:T(8,128)(2,1)} %collective-permute-done.9.refs_4_, ...), custom_call_target="tpu_custom_call" | custom-call | tf_op jit(solution)/shard_map/pallas_call | solution.py:335
  75.7 0.8 collective-permute-start.17
  76.5 6.0 %shard_map.92 = (f32[4,2,128,128]{3,2,1,0:T(8,128)}, bf16[4,2,128,128]{3,2,1,0:T(8,128)(2,1)}) custom-call(s32[8]{0:T(128)} %owner_ref.3, f32[512,512]{1,0:T(8,128)} %shard_map.88.refs_1_, bf16[256,8192]{1,0:T(8,128)(2,1)} %refs_2_.5, bf16[256,8192]{1,0:T(8,128)(2,1)} %copy-done.9, bf16[256,4096]{1,0:T(8,128)(2,1)} %collective-permute-done.9.refs_4_, ...), custom_call_target="tpu_custom_call" | custom-call | tf_op jit(solution)/shard_map/pallas_call | solution.py:335
  82.5 1.3 %collective-permute-start.21 = (bf16[4,2,128,128]{3,2,1,0:T(8,128)(2,1)}, bf16[4,2,128,128]{3,2,1,0:T(8,128)(2,1)S(1)}, u32[]{:S(2)}, u32[]{:S(2)}) collective-permute-start(bf16[4,2,128,128]{3,2,1,0:T(8,128)(2,1)} %get-tuple-element.55), channel_id=1, source_target_pairs={{0,2},{2,0},{4,6},{6,4},{8,10},{10,8},{12,14},{14,12},{1,3},{3,1},... | collective-permute-start | bytes 786440 | tf_op jit(solution)/shard_map/ppermute | solution.py:417
  84.2 0.7 shard_map.90
  84.9 0.4 collective-permute-start.18
  85.3 3.0 %collective-permute-start.19 = (bf16[256,128]{1,0:T(8,128)(2,1)S(1)}, bf16[256,128]{1,0:T(8,128)(2,1)S(1)}, u32[]{:S(2)}, u32[]{:S(2)}) collective-permute-start(bf16[256,128]{1,0:T(8,128)(2,1)S(1)} %get-tuple-element.51), channel_id=1, source_target_pairs={{0,8},{2,10},{4,12},{6,14},{8,0},{10,2},{12,4},{14,6},{1,9},{3,11}... | collective-permute-start | bytes 196616 | tf_op jit(solution)/shard_map/ppermute | solution.py:420
  88.3 1.1 %collective-permute-start.20 = (bf16[256,128]{1,0:T(8,128)(2,1)S(1)}, bf16[256,128]{1,0:T(8,128)(2,1)S(1)}, u32[]{:S(2)}, u32[]{:S(2)}) collective-permute-start(bf16[256,128]{1,0:T(8,128)(2,1)S(1)} %get-tuple-element.52), channel_id=1, source_target_pairs={{0,12},{2,14},{4,8},{6,10},{8,4},{10,6},{12,0},{14,2},{1,13},{3,15... | collective-permute-start | bytes 196616 | tf_op jit(solution)/shard_map/ppermute | solution.py:420
  89.4 1.2 %collective-permute-done.21.came_ref = bf16[4,2,128,128]{3,2,1,0:T(8,128)(2,1)S(1)} collective-permute-done((bf16[4,2,128,128]{3,2,1,0:T(8,128)(2,1)}, bf16[4,2,128,128]{3,2,1,0:T(8,128)(2,1)S(1)}, u32[]{:S(2)}, u32[]{:S(2)}) %collective-permute-start.21) | collective-permute-done | bytes 262176 | tf_op jit(solution)/shard_map/ppermute | solution.py:417
  90.6 1.0 %copy-done.5 = f32[4,2,128,128]{3,2,1,0:T(8,128)S(1)} copy-done((f32[4,2,128,128]{3,2,1,0:T(8,128)S(1)}, f32[4,2,128,128]{3,2,1,0:T(8,128)}, u32[]{:S(2)}) %copy-start.5) | copy-done | bytes 524312
  91.7 0.6 shard_map.93
  92.3 0.9 collective-permute-start.23
  93.2 1.8 %collective-permute-start.24 = (bf16[256,128]{1,0:T(8,128)(2,1)S(1)}, bf16[256,128]{1,0:T(8,128)(2,1)S(1)}, u32[]{:S(2)}, u32[]{:S(2)}) collective-permute-start(bf16[256,128]{1,0:T(8,128)(2,1)S(1)} %get-tuple-element.61), channel_id=1, source_target_pairs={{0,12},{2,14},{4,8},{6,10},{8,4},{10,6},{12,0},{14,2},{1,13},{3,15... | collective-permute-start | bytes 196616 | tf_op jit(solution)/shard_map/ppermute | solution.py:420
  95.0 1.0 collective-permute-start.22
  95.9 0.7 shard_map.91
  96.7 1.9 %collective-permute-done.23.refs_2_ = bf16[256,128]{1,0:T(8,128)(2,1)S(1)} collective-permute-done((bf16[256,128]{1,0:T(8,128)(2,1)S(1)}, bf16[256,128]{1,0:T(8,128)(2,1)S(1)}, u32[]{:S(2)}, u32[]{:S(2)}) %collective-permute-start.23) | collective-permute-done | bytes 65568 | tf_op jit(solution)/shard_map/ppermute | solution.py:420
  98.6 0.8 collective-permute-done.24.refs_3_
  99.4 0.6 collective-permute-done.22.refs_1_
  100.0 0.7 shard_map.94
  (69 shorter events, 2.2 us)
Async XLA Ops:
  0.6 8.9 %collective-permute-start = (bf16[256,8192]{1,0:T(8,128)(2,1)}, bf16[256,8192]{1,0:T(8,128)(2,1)S(1)}, u32[]{:S(2)}, u32[]{:S(2)}) collective-permute-start(bf16[256,8192]{1,0:T(8,128)(2,1)} %refs_2_.5), channel_id=1, source_target_pairs={{0,1},{1,0},{2,3},{3,2},{4,5},{5,4},{6,7},{7,6},{8,9},{9,8},{10,11... | collective-permute-start | bytes 12582920 | tf_op jit(solution)/shard_map/ppermute | solution.py:426
  1.1 2.2 %copy-start = (bf16[256,8192]{1,0:T(8,128)(2,1)S(1)}, bf16[256,8192]{1,0:T(8,128)(2,1)}, u32[]{:S(2)}) copy-start(bf16[256,8192]{1,0:T(8,128)(2,1)} %refs_2_.5) | copy-start | bytes 12582916
  3.3 3.5 %copy-start.3 = (bf16[1024,256]{1,0:T(8,128)(2,1)S(1)}, bf16[1024,256]{1,0:T(8,128)(2,1)}, u32[]{:S(2)}) copy-start(bf16[1024,256]{1,0:T(8,128)(2,1)} %refs_6_) | copy-start | bytes 1572868
  3.3 3.5 %copy-start.4 = (bf16[1024,256]{1,0:T(8,128)(2,1)S(1)}, bf16[1024,256]{1,0:T(8,128)(2,1)}, u32[]{:S(2)}) copy-start(bf16[1024,256]{1,0:T(8,128)(2,1)} %refs_6_.1) | copy-start | bytes 1572868
  3.3 3.5 %copy-start.7 = (bf16[80,1024]{1,0:T(8,128)(2,1)S(1)}, bf16[80,1024]{1,0:T(8,128)(2,1)}, u32[]{:S(2)}) copy-start(bf16[80,1024]{1,0:T(8,128)(2,1)} %gain_ref.1) | copy-start | bytes 491524
  3.3 27.0 %copy-start.1 = (bf16[256,8192]{1,0:T(8,128)(2,1)S(1)}, bf16[256,8192]{1,0:T(8,128)(2,1)}, u32[]{:S(2)}) copy-start(bf16[256,8192]{1,0:T(8,128)(2,1)} %refs_2_.5) | copy-start | bytes 12582916
  3.6 50.0 %collective-permute-start.9 = (bf16[256,4096]{1,0:T(8,128)(2,1)S(1)}, bf16[256,4096]{1,0:T(8,128)(2,1)}, u32[]{:S(2)}, u32[]{:S(2)}) collective-permute-start(bf16[256,4096]{1,0:T(8,128)(2,1)S(1)} %shard_map.86), channel_id=1, source_target_pairs={{0,2},{2,0},{4,6},{6,4},{8,10},{10,8},{12,14},{14,12},{1,3},{3,1},... | collective-permute-start | bytes 6291464 | tf_op jit(solution)/shard_map/ppermute | solution.py:417
  7.1 0.8 copy-start.2
  7.9 15.5 %collective-permute-start.1 = (bf16[272,512]{1,0:T(8,128)(2,1)S(1)}, bf16[272,512]{1,0:T(8,128)(2,1)S(1)}, u32[]{:S(2)}, u32[]{:S(2)}) collective-permute-start(bf16[272,512]{1,0:T(8,128)(2,1)S(1)} %get-tuple-element.34), channel_id=1, source_target_pairs={{0,4},{2,6},{4,0},{6,2},{8,12},{10,14},{12,8},{14,10},{1,5},{3,7},... | collective-permute-start | bytes 835592 | tf_op jit(solution)/shard_map/ppermute | solution.py:420
  9.5 19.2 %copy-start.9 = (bf16[256,8192]{1,0:T(8,128)(2,1)}, bf16[256,8192]{1,0:T(8,128)(2,1)S(1)}, u32[]{:S(2)}) copy-start(bf16[256,8192]{1,0:T(8,128)(2,1)S(1)} %collective-permute-done.refs_1_.refs_3_) | copy-start | bytes 12582916
  9.5 19.2 %collective-permute-start.2 = (bf16[272,512]{1,0:T(8,128)(2,1)S(1)}, bf16[272,512]{1,0:T(8,128)(2,1)S(1)}, u32[]{:S(2)}, u32[]{:S(2)}) collective-permute-start(bf16[272,512]{1,0:T(8,128)(2,1)S(1)} %get-tuple-element.37), channel_id=1, source_target_pairs={{0,4},{2,6},{4,0},{6,2},{8,12},{10,14},{12,8},{14,10},{1,5},{3,7},... | collective-permute-start | bytes 835592 | tf_op jit(solution)/shard_map/ppermute | solution.py:420
  11.1 20.1 %collective-permute-start.3 = (bf16[272,512]{1,0:T(8,128)(2,1)S(1)}, bf16[272,512]{1,0:T(8,128)(2,1)S(1)}, u32[]{:S(2)}, u32[]{:S(2)}) collective-permute-start(bf16[272,512]{1,0:T(8,128)(2,1)S(1)} %get-tuple-element.34), channel_id=1, source_target_pairs={{0,8},{2,10},{4,12},{6,14},{8,0},{10,2},{12,4},{14,6},{1,9},{3,11}... | collective-permute-start | bytes 835592 | tf_op jit(solution)/shard_map/ppermute | solution.py:420
  23.4 41.0 %copy-start.10 = (bf16[272,512]{1,0:T(8,128)(2,1)}, bf16[272,512]{1,0:T(8,128)(2,1)S(1)}, u32[]{:S(2)}) copy-start(bf16[272,512]{1,0:T(8,128)(2,1)S(1)} %collective-permute-done.1.refs_5_.refs_8_) | copy-start | bytes 835588
  23.4 19.4 %collective-permute-start.4 = (bf16[272,512]{1,0:T(8,128)(2,1)S(1)}, bf16[272,512]{1,0:T(8,128)(2,1)S(1)}, u32[]{:S(2)}, u32[]{:S(2)}) collective-permute-start(bf16[272,512]{1,0:T(8,128)(2,1)S(1)} %get-tuple-element.37), channel_id=1, source_target_pairs={{0,8},{2,10},{4,12},{6,14},{8,0},{10,2},{12,4},{14,6},{1,9},{3,11}... | collective-permute-start | bytes 835592 | tf_op jit(solution)/shard_map/ppermute | solution.py:420
  25.1 8.4 %collective-permute-start.5 = (bf16[272,512]{1,0:T(8,128)(2,1)S(1)}, bf16[272,512]{1,0:T(8,128)(2,1)S(1)}, u32[]{:S(2)}, u32[]{:S(2)}) collective-permute-start(bf16[272,512]{1,0:T(8,128)(2,1)S(1)} %collective-permute-done.1.refs_5_.refs_8_), channel_id=1, source_target_pairs={{0,16},{16,0},{1,17},{17,1},{2,18},{18,2},{3,19},{19,3},{4,20},{20... | collective-permute-start | bytes 835592 | tf_op jit(solution)/shard_map/ppermute | solution.py:423
  28.7 35.7 %copy-start.11 = (bf16[272,512]{1,0:T(8,128)(2,1)}, bf16[272,512]{1,0:T(8,128)(2,1)S(1)}, u32[]{:S(2)}) copy-start(bf16[272,512]{1,0:T(8,128)(2,1)S(1)} %collective-permute-done.2.refs_6_.refs_9_) | copy-start | bytes 835588
  28.7 14.0 %collective-permute-start.6 = (bf16[272,512]{1,0:T(8,128)(2,1)S(1)}, bf16[272,512]{1,0:T(8,128)(2,1)S(1)}, u32[]{:S(2)}, u32[]{:S(2)}) collective-permute-start(bf16[272,512]{1,0:T(8,128)(2,1)S(1)} %collective-permute-done.2.refs_6_.refs_9_), channel_id=1, source_target_pairs={{0,16},{16,0},{1,17},{17,1},{2,18},{18,2},{3,19},{19,3},{4,20},{20... | collective-permute-start | bytes 835592 | tf_op jit(solution)/shard_map/ppermute | solution.py:423
  31.2 33.4 %copy-start.12 = (bf16[272,512]{1,0:T(8,128)(2,1)}, bf16[272,512]{1,0:T(8,128)(2,1)S(1)}, u32[]{:S(2)}) copy-start(bf16[272,512]{1,0:T(8,128)(2,1)S(1)} %collective-permute-done.3.refs_7_.refs_10_) | copy-start | bytes 835588
  31.2 13.8 %collective-permute-start.10 = (bf16[272,512]{1,0:T(8,128)(2,1)S(1)}, bf16[272,512]{1,0:T(8,128)(2,1)S(1)}, u32[]{:S(2)}, u32[]{:S(2)}) collective-permute-start(bf16[272,512]{1,0:T(8,128)(2,1)S(1)} %collective-permute-done.3.refs_7_.refs_10_), channel_id=1, source_target_pairs={{0,4},{2,6},{4,0},{6,2},{8,12},{10,14},{12,8},{14,10},{1,5},{3,7},... | collective-permute-start | bytes 835592 | tf_op jit(solution)/shard_map/ppermute | solution.py:420
  33.4 23.9 %copy-start.14 = (bf16[272,512]{1,0:T(8,128)(2,1)}, bf16[272,512]{1,0:T(8,128)(2,1)S(1)}, u32[]{:S(2)}) copy-start(bf16[272,512]{1,0:T(8,128)(2,1)S(1)} %collective-permute-done.5.refs_9_.refs_14_) | copy-start | bytes 835588
  33.4 11.6 %collective-permute-start.7 = (bf16[272,512]{1,0:T(8,128)(2,1)S(1)}, bf16[272,512]{1,0:T(8,128)(2,1)S(1)}, u32[]{:S(2)}, u32[]{:S(2)}) collective-permute-start(bf16[272,512]{1,0:T(8,128)(2,1)S(1)} %collective-permute-done.3.refs_7_.refs_10_), channel_id=1, source_target_pairs={{0,16},{16,0},{1,17},{17,1},{2,18},{18,2},{3,19},{19,3},{4,20},{20... | collective-permute-start | bytes 835592 | tf_op jit(solution)/shard_map/ppermute | solution.py:423
  42.8 21.9 %copy-start.13 = (bf16[272,512]{1,0:T(8,128)(2,1)}, bf16[272,512]{1,0:T(8,128)(2,1)S(1)}, u32[]{:S(2)}) copy-start(bf16[272,512]{1,0:T(8,128)(2,1)S(1)} %collective-permute-done.4.refs_8_.refs_11_) | copy-start | bytes 835588
  42.8 16.4 %copy-start.15 = (bf16[272,512]{1,0:T(8,128)(2,1)}, bf16[272,512]{1,0:T(8,128)(2,1)S(1)}, u32[]{:S(2)}) copy-start(bf16[272,512]{1,0:T(8,128)(2,1)S(1)} %collective-permute-done.6.refs_10_.refs_15_) | copy-start | bytes 835588
  42.8 8.7 %collective-permute-start.11 = (bf16[272,512]{1,0:T(8,128)(2,1)S(1)}, bf16[272,512]{1,0:T(8,128)(2,1)}, u32[]{:S(2)}, u32[]{:S(2)}) collective-permute-start(bf16[272,512]{1,0:T(8,128)(2,1)S(1)} %collective-permute-done.4.refs_8_.refs_11_), channel_id=1, source_target_pairs={{0,4},{2,6},{4,0},{6,2},{8,12},{10,14},{12,8},{14,10},{1,5},{3,7},... | collective-permute-start | bytes 835592 | tf_op jit(solution)/shard_map/ppermute | solution.py:420
  43.1 14.2 %collective-permute-start.8 = (bf16[272,512]{1,0:T(8,128)(2,1)S(1)}, bf16[272,512]{1,0:T(8,128)(2,1)S(1)}, u32[]{:S(2)}, u32[]{:S(2)}) collective-permute-start(bf16[272,512]{1,0:T(8,128)(2,1)S(1)} %collective-permute-done.4.refs_8_.refs_11_), channel_id=1, source_target_pairs={{0,16},{16,0},{1,17},{17,1},{2,18},{18,2},{3,19},{19,3},{4,20},{20... | collective-permute-start | bytes 835592 | tf_op jit(solution)/shard_map/ppermute | solution.py:423
  45.0 14.1 %copy-start.18 = (bf16[272,512]{1,0:T(8,128)(2,1)}, bf16[272,512]{1,0:T(8,128)(2,1)S(1)}, u32[]{:S(2)}) copy-start(bf16[272,512]{1,0:T(8,128)(2,1)S(1)} %collective-permute-done.10.refs_12_) | copy-start | bytes 835588
  45.0 14.1 %copy-start.16 = (bf16[272,512]{1,0:T(8,128)(2,1)}, bf16[272,512]{1,0:T(8,128)(2,1)S(1)}, u32[]{:S(2)}) copy-start(bf16[272,512]{1,0:T(8,128)(2,1)S(1)} %collective-permute-done.7.refs_11_.refs_16_) | copy-start | bytes 835588
  51.5 7.7 %collective-permute-start.12 = (bf16[272,512]{1,0:T(8,128)(2,1)S(1)}, bf16[272,512]{1,0:T(8,128)(2,1)S(1)}, u32[]{:S(2)}, u32[]{:S(2)}) collective-permute-start(bf16[272,512]{1,0:T(8,128)(2,1)S(1)} %collective-permute-done.10.refs_12_), channel_id=1, source_target_pairs={{0,16},{16,0},{1,17},{17,1},{2,18},{18,2},{3,19},{19,3},{4,20},{20... | collective-permute-start | bytes 835592 | tf_op jit(solution)/shard_map/ppermute | solution.py:423
  53.7 3.7 %collective-permute-start.13 = (f32[2,256]{1,0:T(2,128)S(1)}, f32[2,256]{1,0:T(2,128)S(1)}, u32[]{:S(2)}, u32[]{:S(2)}) collective-permute-start(f32[2,256]{1,0:T(2,128)S(1)} %get-tuple-element.43), channel_id=1, source_target_pairs={{0,2},{2,0},{4,6},{6,4},{8,10},{10,8},{12,14},{14,12},{1,3},{3,1},... | collective-permute-start | bytes 6152 | tf_op jit(solution)/shard_map/ppermute | solution.py:417
  57.3 1.8 %copy-start.17 = (bf16[272,512]{1,0:T(8,128)(2,1)}, bf16[272,512]{1,0:T(8,128)(2,1)S(1)}, u32[]{:S(2)}) copy-start(bf16[272,512]{1,0:T(8,128)(2,1)S(1)} %collective-permute-done.8.refs_12_.refs_17_) | copy-start | bytes 835588
  59.1 0.7 copy-start.19
  59.1 10.6 %collective-permute-start.14 = (bf16[256,4096]{1,0:T(8,128)(2,1)}, bf16[256,4096]{1,0:T(8,128)(2,1)}, u32[]{:S(2)}, u32[]{:S(2)}) collective-permute-start(bf16[256,4096]{1,0:T(8,128)(2,1)} %collective-permute-done.9.refs_4_), channel_id=1, source_target_pairs={{0,1},{1,0},{2,3},{3,2},{4,5},{5,4},{6,7},{7,6},{8,9},{9,8},{10,11... | collective-permute-start | bytes 6291464 | tf_op jit(solution)/shard_map/ppermute | solution.py:426
  59.9 4.5 %collective-permute-start.15 = (f32[2,256]{1,0:T(2,128)S(1)}, f32[2,256]{1,0:T(2,128)S(1)}, u32[]{:S(2)}, u32[]{:S(2)}) collective-permute-start(f32[2,256]{1,0:T(2,128)S(1)} %bitcast.15), channel_id=1, source_target_pairs={{0,1},{1,0},{2,3},{3,2},{4,5},{5,4},{6,7},{7,6},{8,9},{9,8},{10,11... | collective-permute-start | bytes 6152 | tf_op jit(solution)/shard_map/ppermute | solution.py:426
  60.3 9.4 %collective-permute-start.16 = (bf16[272,512]{1,0:T(8,128)(2,1)}, bf16[272,512]{1,0:T(8,128)(2,1)}, u32[]{:S(2)}, u32[]{:S(2)}) collective-permute-start(bf16[272,512]{1,0:T(8,128)(2,1)} %collective-permute-done.11.refs_13_), channel_id=1, source_target_pairs={{0,16},{16,0},{1,17},{17,1},{2,18},{18,2},{3,19},{19,3},{4,20},{20... | collective-permute-start | bytes 835592 | tf_op jit(solution)/shard_map/ppermute | solution.py:423
  75.7 8.5 %copy-start.6 = (f32[4,2,128,128]{3,2,1,0:T(8,128)S(1)}, f32[4,2,128,128]{3,2,1,0:T(8,128)}, u32[]{:S(2)}) copy-start(f32[4,2,128,128]{3,2,1,0:T(8,128)} %get-tuple-element.47.keep_ref) | copy-start | bytes 1572868
  75.7 8.5 %copy-start.8 = (s32[8]{0:T(128)S(1)}, s32[8]{0:T(128)}, u32[]{:S(2)}) copy-start(s32[8]{0:T(128)} %owner_ref.3) | copy-start | bytes 100
  75.7 8.5 %collective-permute-start.17 = (bf16[4,2,128,128]{3,2,1,0:T(8,128)(2,1)}, bf16[4,2,128,128]{3,2,1,0:T(8,128)(2,1)S(1)}, u32[]{:S(2)}, u32[]{:S(2)}) collective-permute-start(bf16[4,2,128,128]{3,2,1,0:T(8,128)(2,1)} %get-tuple-element.48), channel_id=1, source_target_pairs={{0,2},{2,0},{4,6},{6,4},{8,10},{10,8},{12,14},{14,12},{1,3},{3,1},... | collective-permute-start | bytes 786440 | tf_op jit(solution)/shard_map/ppermute | solution.py:417
  82.5 8.1 %collective-permute-start.21 = (bf16[4,2,128,128]{3,2,1,0:T(8,128)(2,1)}, bf16[4,2,128,128]{3,2,1,0:T(8,128)(2,1)S(1)}, u32[]{:S(2)}, u32[]{:S(2)}) collective-permute-start(bf16[4,2,128,128]{3,2,1,0:T(8,128)(2,1)} %get-tuple-element.55), channel_id=1, source_target_pairs={{0,2},{2,0},{4,6},{6,4},{8,10},{10,8},{12,14},{14,12},{1,3},{3,1},... | collective-permute-start | bytes 786440 | tf_op jit(solution)/shard_map/ppermute | solution.py:417
  84.9 10.0 %collective-permute-start.18 = (bf16[256,128]{1,0:T(8,128)(2,1)S(1)}, bf16[256,128]{1,0:T(8,128)(2,1)S(1)}, u32[]{:S(2)}, u32[]{:S(2)}) collective-permute-start(bf16[256,128]{1,0:T(8,128)(2,1)S(1)} %get-tuple-element.50), channel_id=1, source_target_pairs={{0,4},{2,6},{4,0},{6,2},{8,12},{10,14},{12,8},{14,10},{1,5},{3,7},... | collective-permute-start | bytes 196616 | tf_op jit(solution)/shard_map/ppermute | solution.py:420
  85.3 9.7 %collective-permute-start.19 = (bf16[256,128]{1,0:T(8,128)(2,1)S(1)}, bf16[256,128]{1,0:T(8,128)(2,1)S(1)}, u32[]{:S(2)}, u32[]{:S(2)}) collective-permute-start(bf16[256,128]{1,0:T(8,128)(2,1)S(1)} %get-tuple-element.51), channel_id=1, source_target_pairs={{0,8},{2,10},{4,12},{6,14},{8,0},{10,2},{12,4},{14,6},{1,9},{3,11}... | collective-permute-start | bytes 196616 | tf_op jit(solution)/shard_map/ppermute | solution.py:420
  88.3 6.7 %collective-permute-start.20 = (bf16[256,128]{1,0:T(8,128)(2,1)S(1)}, bf16[256,128]{1,0:T(8,128)(2,1)S(1)}, u32[]{:S(2)}, u32[]{:S(2)}) collective-permute-start(bf16[256,128]{1,0:T(8,128)(2,1)S(1)} %get-tuple-element.52), channel_id=1, source_target_pairs={{0,12},{2,14},{4,8},{6,10},{8,4},{10,6},{12,0},{14,2},{1,13},{3,15... | collective-permute-start | bytes 196616 | tf_op jit(solution)/shard_map/ppermute | solution.py:420
  90.6 1.0 %copy-start.5 = (f32[4,2,128,128]{3,2,1,0:T(8,128)S(1)}, f32[4,2,128,128]{3,2,1,0:T(8,128)}, u32[]{:S(2)}) copy-start(f32[4,2,128,128]{3,2,1,0:T(8,128)} %get-tuple-element.54.keep_ref) | copy-start | bytes 1572868
  92.3 6.3 %collective-permute-start.23 = (bf16[256,128]{1,0:T(8,128)(2,1)S(1)}, bf16[256,128]{1,0:T(8,128)(2,1)S(1)}, u32[]{:S(2)}, u32[]{:S(2)}) collective-permute-start(bf16[256,128]{1,0:T(8,128)(2,1)S(1)} %get-tuple-element.60), channel_id=1, source_target_pairs={{0,8},{2,10},{4,12},{6,14},{8,0},{10,2},{12,4},{14,6},{1,9},{3,11}... | collective-permute-start | bytes 196616 | tf_op jit(solution)/shard_map/ppermute | solution.py:420
  93.2 6.2 %collective-permute-start.24 = (bf16[256,128]{1,0:T(8,128)(2,1)S(1)}, bf16[256,128]{1,0:T(8,128)(2,1)S(1)}, u32[]{:S(2)}, u32[]{:S(2)}) collective-permute-start(bf16[256,128]{1,0:T(8,128)(2,1)S(1)} %get-tuple-element.61), channel_id=1, source_target_pairs={{0,12},{2,14},{4,8},{6,10},{8,4},{10,6},{12,0},{14,2},{1,13},{3,15... | collective-permute-start | bytes 196616 | tf_op jit(solution)/shard_map/ppermute | solution.py:420
  95.0 5.0 %collective-permute-start.22 = (bf16[256,128]{1,0:T(8,128)(2,1)S(1)}, bf16[256,128]{1,0:T(8,128)(2,1)S(1)}, u32[]{:S(2)}, u32[]{:S(2)}) collective-permute-start(bf16[256,128]{1,0:T(8,128)(2,1)S(1)} %get-tuple-element.59), channel_id=1, source_target_pairs={{0,4},{2,6},{4,0},{6,2},{8,12},{10,14},{12,8},{14,10},{1,5},{3,7},... | collective-permute-start | bytes 196616 | tf_op jit(solution)/shard_map/ppermute | solution.py:420

commit v7 on v6

--- a/solution.py
+++ b/solution.py
@@ -10,7 +10,7 @@
 
 HD = 128
 GAIN_ROWS = 16
-VMEM_LIMIT = 61 * 2**20
+VMEM_LIMIT = 62 * 2**20
 SMALL_VMEM_LIMIT = 8 * 2**20
 
 

time: 101 us -> 101 us (level)
  local copies, waits for them, and re-layouts: 5.18 us -> 6.22 us
    ppermute x4, waiting for transfers between devices: 4.43 us -> 3.35 us  [over_x(): return lax.ppermute(values, 'tok', [(t, t ^ 1) for t in range(tok_count)])]
    unnamed x41, local copies, waits for them, and re-layouts: 4.79 us -> 5.83 us
where the time goes in v7:
time: 101 us
  waiting for transfers between devices  37.7 us (37%)
  starting transfers between devices  31.1 us (31%)
  Pallas kernels  20 us (20%)
  local copies, waits for them, and re-layouts  6.22 us (6%)
  other arithmetic  3.65 us (4%)
  between operations  2.23 us (2%)
    ppermute x12, waiting for transfers between devices, over_z(): lax.ppermute(values, 'tok', [(t, t ^ 2 * distance) for t in range(tok_cou...  30.8 us
    ppermute x12, starting transfers between devices, over_z(): lax.ppermute(values, 'tok', [(t, t ^ 2 * distance) for t in range(tok_cou...  15.9 us
    pallas_call x2, Pallas kernels, multiply(): pl.pallas_call(functools.partial(multiply_kernel, shard, counts, which),...  11.9 us
    ppermute x6, starting transfers between devices, over_y(): return lax.ppermute(values, 'group', [(0, 1), (1, 0)])  9.07 us
    unnamed x41, local copies, waits for them, and re-layouts  5.83 us
    ppermute x4, starting transfers between devices, over_x(): return lax.ppermute(values, 'tok', [(t, t ^ 1) for t in range(tok_count)])  5.48 us
    pallas_call x1, Pallas kernels, early(): pl.pallas_call(functools.partial(early_kernel, shard, counts), in_specs=[...  4.75 us
    ppermute x6, waiting for transfers between devices, over_y(): return lax.ppermute(values, 'group', [(0, 1), (1, 0)])  3.48 us
  transfers between devices with their start and end apart: 25, of which 14 were waited for; matrix products, arithmetic and copies ran while one was open for 4% of the time, Pallas kernels for 13%

profile of v7, /device:TPU:0, one launch (start us, length us, event | category | flops | bytes accessed | tf_op | source)
XLA Modules:
  0.0 100.9 jit_solution(18097072012361368687)
XLA Ops:
  0.6 0.5 collective-permute-start
  1.1 2.2 %copy-done = bf16[256,8192]{1,0:T(8,128)(2,1)S(1)} copy-done((bf16[256,8192]{1,0:T(8,128)(2,1)S(1)}, bf16[256,8192]{1,0:T(8,128)(2,1)}, u32[]{:S(2)}) %copy-start) | copy-done | bytes 4194328
  3.6 2.6 %collective-permute-start.9 = (bf16[256,4096]{1,0:T(8,128)(2,1)S(1)}, bf16[256,4096]{1,0:T(8,128)(2,1)}, u32[]{:S(2)}, u32[]{:S(2)}) collective-permute-start(bf16[256,4096]{1,0:T(8,128)(2,1)S(1)} %shard_map.86), channel_id=1, source_target_pairs={{0,2},{2,0},{4,6},{6,4},{8,10},{10,8},{12,14},{14,12},{1,3},{3,1},... | collective-permute-start | bytes 6291464 | tf_op jit(solution)/shard_map/ppermute | solution.py:417
  7.1 0.8 copy-done.2
  7.9 1.6 %collective-permute-start.1 = (bf16[272,512]{1,0:T(8,128)(2,1)S(1)}, bf16[272,512]{1,0:T(8,128)(2,1)S(1)}, u32[]{:S(2)}, u32[]{:S(2)}) collective-permute-start(bf16[272,512]{1,0:T(8,128)(2,1)S(1)} %get-tuple-element.34), channel_id=1, source_target_pairs={{0,4},{2,6},{4,0},{6,2},{8,12},{10,14},{12,8},{14,10},{1,5},{3,7},... | collective-permute-start | bytes 835592 | tf_op jit(solution)/shard_map/ppermute | solution.py:420
  9.5 1.6 %collective-permute-start.2 = (bf16[272,512]{1,0:T(8,128)(2,1)S(1)}, bf16[272,512]{1,0:T(8,128)(2,1)S(1)}, u32[]{:S(2)}, u32[]{:S(2)}) collective-permute-start(bf16[272,512]{1,0:T(8,128)(2,1)S(1)} %get-tuple-element.37), channel_id=1, source_target_pairs={{0,4},{2,6},{4,0},{6,2},{8,12},{10,14},{12,8},{14,10},{1,5},{3,7},... | collective-permute-start | bytes 835592 | tf_op jit(solution)/shard_map/ppermute | solution.py:420
  11.1 2.6 %collective-permute-start.3 = (bf16[272,512]{1,0:T(8,128)(2,1)S(1)}, bf16[272,512]{1,0:T(8,128)(2,1)S(1)}, u32[]{:S(2)}, u32[]{:S(2)}) collective-permute-start(bf16[272,512]{1,0:T(8,128)(2,1)S(1)} %get-tuple-element.34), channel_id=1, source_target_pairs={{0,8},{2,10},{4,12},{6,14},{8,0},{10,2},{12,4},{14,6},{1,9},{3,11}... | collective-permute-start | bytes 835592 | tf_op jit(solution)/shard_map/ppermute | solution.py:420
  13.7 9.7 %collective-permute-done.1.refs_5_.refs_8_ = bf16[272,512]{1,0:T(8,128)(2,1)S(1)} collective-permute-done((bf16[272,512]{1,0:T(8,128)(2,1)S(1)}, bf16[272,512]{1,0:T(8,128)(2,1)S(1)}, u32[]{:S(2)}, u32[]{:S(2)}) %collective-permute-start.1) | collective-permute-done | bytes 278560 | tf_op jit(solution)/shard_map/ppermute | solution.py:420
  23.4 1.7 %collective-permute-start.4 = (bf16[272,512]{1,0:T(8,128)(2,1)S(1)}, bf16[272,512]{1,0:T(8,128)(2,1)S(1)}, u32[]{:S(2)}, u32[]{:S(2)}) collective-permute-start(bf16[272,512]{1,0:T(8,128)(2,1)S(1)} %get-tuple-element.37), channel_id=1, source_target_pairs={{0,8},{2,10},{4,12},{6,14},{8,0},{10,2},{12,4},{14,6},{1,9},{3,11}... | collective-permute-start | bytes 835592 | tf_op jit(solution)/shard_map/ppermute | solution.py:420
  25.1 1.5 %collective-permute-start.5 = (bf16[272,512]{1,0:T(8,128)(2,1)S(1)}, bf16[272,512]{1,0:T(8,128)(2,1)S(1)}, u32[]{:S(2)}, u32[]{:S(2)}) collective-permute-start(bf16[272,512]{1,0:T(8,128)(2,1)S(1)} %collective-permute-done.1.refs_5_.refs_8_), channel_id=1, source_target_pairs={{0,16},{16,0},{1,17},{17,1},{2,18},{18,2},{3,19},{19,3},{4,20},{20... | collective-permute-start | bytes 835592 | tf_op jit(solution)/shard_map/ppermute | solution.py:423
  26.6 2.2 %collective-permute-done.2.refs_6_.refs_9_ = bf16[272,512]{1,0:T(8,128)(2,1)S(1)} collective-permute-done((bf16[272,512]{1,0:T(8,128)(2,1)S(1)}, bf16[272,512]{1,0:T(8,128)(2,1)S(1)}, u32[]{:S(2)}, u32[]{:S(2)}) %collective-permute-start.2) | collective-permute-done | bytes 278560 | tf_op jit(solution)/shard_map/ppermute | solution.py:420
  28.7 1.6 %collective-permute-start.6 = (bf16[272,512]{1,0:T(8,128)(2,1)S(1)}, bf16[272,512]{1,0:T(8,128)(2,1)S(1)}, u32[]{:S(2)}, u32[]{:S(2)}) collective-permute-start(bf16[272,512]{1,0:T(8,128)(2,1)S(1)} %collective-permute-done.2.refs_6_.refs_9_), channel_id=1, source_target_pairs={{0,16},{16,0},{1,17},{17,1},{2,18},{18,2},{3,19},{19,3},{4,20},{20... | collective-permute-start | bytes 835592 | tf_op jit(solution)/shard_map/ppermute | solution.py:423
  30.3 0.9 multiply_reduce_fusion
  31.2 0.8 collective-permute-start.10
  32.0 1.4 %collective-permute-done.5.refs_9_.refs_14_ = bf16[272,512]{1,0:T(8,128)(2,1)S(1)} collective-permute-done((bf16[272,512]{1,0:T(8,128)(2,1)S(1)}, bf16[272,512]{1,0:T(8,128)(2,1)S(1)}, u32[]{:S(2)}, u32[]{:S(2)}) %collective-permute-start.5) | collective-permute-done | bytes 278560 | tf_op jit(solution)/shard_map/ppermute | solution.py:423
  33.4 1.4 %collective-permute-start.7 = (bf16[272,512]{1,0:T(8,128)(2,1)S(1)}, bf16[272,512]{1,0:T(8,128)(2,1)S(1)}, u32[]{:S(2)}, u32[]{:S(2)}) collective-permute-start(bf16[272,512]{1,0:T(8,128)(2,1)S(1)} %collective-permute-done.3.refs_7_.refs_10_), channel_id=1, source_target_pairs={{0,16},{16,0},{1,17},{17,1},{2,18},{18,2},{3,19},{19,3},{4,20},{20... | collective-permute-start | bytes 835592 | tf_op jit(solution)/shard_map/ppermute | solution.py:423
  34.8 8.0 %collective-permute-done.4.refs_8_.refs_11_ = bf16[272,512]{1,0:T(8,128)(2,1)S(1)} collective-permute-done((bf16[272,512]{1,0:T(8,128)(2,1)S(1)}, bf16[272,512]{1,0:T(8,128)(2,1)S(1)}, u32[]{:S(2)}, u32[]{:S(2)}) %collective-permute-start.4) | collective-permute-done | bytes 278560 | tf_op jit(solution)/shard_map/ppermute | solution.py:420
  42.8 0.3 collective-permute-start.11
  43.1 1.5 %collective-permute-start.8 = (bf16[272,512]{1,0:T(8,128)(2,1)S(1)}, bf16[272,512]{1,0:T(8,128)(2,1)S(1)}, u32[]{:S(2)}, u32[]{:S(2)}) collective-permute-start(bf16[272,512]{1,0:T(8,128)(2,1)S(1)} %collective-permute-done.4.refs_8_.refs_11_), channel_id=1, source_target_pairs={{0,16},{16,0},{1,17},{17,1},{2,18},{18,2},{3,19},{19,3},{4,20},{20... | collective-permute-start | bytes 835592 | tf_op jit(solution)/shard_map/ppermute | solution.py:423
  44.6 0.4 collective-permute-done.10.refs_12_
  45.0 6.4 %collective-permute-done.11.refs_13_ = bf16[272,512]{1,0:T(8,128)(2,1)} collective-permute-done((bf16[272,512]{1,0:T(8,128)(2,1)S(1)}, bf16[272,512]{1,0:T(8,128)(2,1)}, u32[]{:S(2)}, u32[]{:S(2)}) %collective-permute-start.11) | collective-permute-done | bytes 278560 | tf_op jit(solution)/shard_map/ppermute | solution.py:420
  51.5 1.5 %collective-permute-start.12 = (bf16[272,512]{1,0:T(8,128)(2,1)S(1)}, bf16[272,512]{1,0:T(8,128)(2,1)S(1)}, u32[]{:S(2)}, u32[]{:S(2)}) collective-permute-start(bf16[272,512]{1,0:T(8,128)(2,1)S(1)} %collective-permute-done.10.refs_12_), channel_id=1, source_target_pairs={{0,16},{16,0},{1,17},{17,1},{2,18},{18,2},{3,19},{19,3},{4,20},{20... | collective-permute-start | bytes 835592 | tf_op jit(solution)/shard_map/ppermute | solution.py:423
  53.7 0.8 collective-permute-start.13
  54.4 2.9 %collective-permute-done.13 = f32[2,256]{1,0:T(2,128)S(1)} collective-permute-done((f32[2,256]{1,0:T(2,128)S(1)}, f32[2,256]{1,0:T(2,128)S(1)}, u32[]{:S(2)}, u32[]{:S(2)}) %collective-permute-start.13) | collective-permute-done | bytes 2080 | tf_op jit(solution)/shard_map/ppermute | solution.py:417
  57.3 1.8 %collective-permute-done.12.refs_18_ = bf16[272,512]{1,0:T(8,128)(2,1)S(1)} collective-permute-done((bf16[272,512]{1,0:T(8,128)(2,1)S(1)}, bf16[272,512]{1,0:T(8,128)(2,1)S(1)}, u32[]{:S(2)}, u32[]{:S(2)}) %collective-permute-start.12) | collective-permute-done | bytes 278560 | tf_op jit(solution)/shard_map/ppermute | solution.py:423
  59.2 0.7 copy-done.19
  60.3 1.5 %collective-permute-start.16 = (bf16[272,512]{1,0:T(8,128)(2,1)}, bf16[272,512]{1,0:T(8,128)(2,1)}, u32[]{:S(2)}, u32[]{:S(2)}) collective-permute-start(bf16[272,512]{1,0:T(8,128)(2,1)} %collective-permute-done.11.refs_13_), channel_id=1, source_target_pairs={{0,16},{16,0},{1,17},{17,1},{2,18},{18,2},{3,19},{19,3},{4,20},{20... | collective-permute-start | bytes 835592 | tf_op jit(solution)/shard_map/ppermute | solution.py:423
  61.9 2.2 %fusion.5 = (f32[8,128,64]{2,1,0:T(8,128)S(1)}, f32[8,128,64]{2,1,0:T(8,128)S(1)}, f32[8,128,64]{2,1,0:T(8,128)S(1)}) fusion(f32[64]{0:T(128)S(1)} %multiply_power_fusion, f32[8,128]{1,0:T(8,128)S(1)} %add_convert_fusion), kind=kLoop, calls=%fused_computation.10 | loop fusion | flops 524288 | bytes 790784 | tf_op jit(solution)/shard_map/neg | solution.py:457
  64.0 0.3 pad_maximum_fusion
  64.7 4.8 %shard_map.88.refs_1_ = f32[512,512]{1,0:T(8,128)} custom-call(bf16[256,8192]{1,0:T(8,128)(2,1)} %refs_2_.5, bf16[256,8192]{1,0:T(8,128)(2,1)} %copy-done.9, bf16[1024,256]{1,0:T(8,128)(2,1)} %refs_6_, bf16[1024,256]{1,0:T(8,128)(2,1)} %refs_6_.1, bf16[544,512]{1,0:T(8,128)(2,1)} %copy-done.2, bf16[272,512]{1,0:T(8,128)(2,1)} %copy-done.10, ...), custom_call_target="tpu_custom_call" | custom-call | tf_op jit(solution)/shard_map/pallas_call | solution.py:255
  69.7 6.0 %shard_map.89 = (f32[4,2,128,128]{3,2,1,0:T(8,128)}, bf16[4,2,128,128]{3,2,1,0:T(8,128)(2,1)}) custom-call(s32[8]{0:T(128)} %owner_ref.3, f32[512,512]{1,0:T(8,128)} %shard_map.88.refs_1_, bf16[256,8192]{1,0:T(8,128)(2,1)} %refs_2_.5, bf16[256,8192]{1,0:T(8,128)(2,1)} %copy-done.9, bf16[256,4096]{1,0:T(8,128)(2,1)} %collective-permute-done.9.refs_4_, ...), custom_call_target="tpu_custom_call" | custom-call | tf_op jit(solution)/shard_map/pallas_call | solution.py:335
  75.7 0.8 collective-permute-start.17
  76.5 6.0 %shard_map.92 = (f32[4,2,128,128]{3,2,1,0:T(8,128)}, bf16[4,2,128,128]{3,2,1,0:T(8,128)(2,1)}) custom-call(s32[8]{0:T(128)} %owner_ref.3, f32[512,512]{1,0:T(8,128)} %shard_map.88.refs_1_, bf16[256,8192]{1,0:T(8,128)(2,1)} %refs_2_.5, bf16[256,8192]{1,0:T(8,128)(2,1)} %copy-done.9, bf16[256,4096]{1,0:T(8,128)(2,1)} %collective-permute-done.9.refs_4_, ...), custom_call_target="tpu_custom_call" | custom-call | tf_op jit(solution)/shard_map/pallas_call | solution.py:335
  82.5 1.3 %collective-permute-start.21 = (bf16[4,2,128,128]{3,2,1,0:T(8,128)(2,1)}, bf16[4,2,128,128]{3,2,1,0:T(8,128)(2,1)S(1)}, u32[]{:S(2)}, u32[]{:S(2)}) collective-permute-start(bf16[4,2,128,128]{3,2,1,0:T(8,128)(2,1)} %get-tuple-element.55), channel_id=1, source_target_pairs={{0,2},{2,0},{4,6},{6,4},{8,10},{10,8},{12,14},{14,12},{1,3},{3,1},... | collective-permute-start | bytes 786440 | tf_op jit(solution)/shard_map/ppermute | solution.py:417
  84.2 1.0 %copy-done.6 = f32[4,2,128,128]{3,2,1,0:T(8,128)S(1)} copy-done((f32[4,2,128,128]{3,2,1,0:T(8,128)S(1)}, f32[4,2,128,128]{3,2,1,0:T(8,128)}, u32[]{:S(2)}) %copy-start.6) | copy-done | bytes 524312
  85.2 0.8 shard_map.90
  86.0 0.4 collective-permute-start.18
  86.3 3.0 %collective-permute-start.19 = (bf16[256,128]{1,0:T(8,128)(2,1)S(1)}, bf16[256,128]{1,0:T(8,128)(2,1)S(1)}, u32[]{:S(2)}, u32[]{:S(2)}) collective-permute-start(bf16[256,128]{1,0:T(8,128)(2,1)S(1)} %get-tuple-element.51), channel_id=1, source_target_pairs={{0,8},{2,10},{4,12},{6,14},{8,0},{10,2},{12,4},{14,6},{1,9},{3,11}... | collective-permute-start | bytes 196616 | tf_op jit(solution)/shard_map/ppermute | solution.py:420
  89.3 1.1 %collective-permute-start.20 = (bf16[256,128]{1,0:T(8,128)(2,1)S(1)}, bf16[256,128]{1,0:T(8,128)(2,1)S(1)}, u32[]{:S(2)}, u32[]{:S(2)}) collective-permute-start(bf16[256,128]{1,0:T(8,128)(2,1)S(1)} %get-tuple-element.52), channel_id=1, source_target_pairs={{0,12},{2,14},{4,8},{6,10},{8,4},{10,6},{12,0},{14,2},{1,13},{3,15... | collective-permute-start | bytes 196616 | tf_op jit(solution)/shard_map/ppermute | solution.py:420
  90.6 1.0 %copy-done.5 = f32[4,2,128,128]{3,2,1,0:T(8,128)S(1)} copy-done((f32[4,2,128,128]{3,2,1,0:T(8,128)S(1)}, f32[4,2,128,128]{3,2,1,0:T(8,128)}, u32[]{:S(2)}) %copy-start.5) | copy-done | bytes 524312
  91.6 0.6 shard_map.93
  92.3 0.9 collective-permute-start.23
  93.1 1.9 %collective-permute-start.24 = (bf16[256,128]{1,0:T(8,128)(2,1)S(1)}, bf16[256,128]{1,0:T(8,128)(2,1)S(1)}, u32[]{:S(2)}, u32[]{:S(2)}) collective-permute-start(bf16[256,128]{1,0:T(8,128)(2,1)S(1)} %get-tuple-element.61), channel_id=1, source_target_pairs={{0,12},{2,14},{4,8},{6,10},{8,4},{10,6},{12,0},{14,2},{1,13},{3,15... | collective-permute-start | bytes 196616 | tf_op jit(solution)/shard_map/ppermute | solution.py:420
  95.0 0.7 collective-permute-done.20.refs_3_
  95.9 0.7 shard_map.91
  96.6 3.0 %collective-permute-done.23.refs_2_ = bf16[256,128]{1,0:T(8,128)(2,1)S(1)} collective-permute-done((bf16[256,128]{1,0:T(8,128)(2,1)S(1)}, bf16[256,128]{1,0:T(8,128)(2,1)S(1)}, u32[]{:S(2)}, u32[]{:S(2)}) %collective-permute-start.23) | collective-permute-done | bytes 65568 | tf_op jit(solution)/shard_map/ppermute | solution.py:420
  99.6 0.6 collective-permute-done.22.refs_1_
  100.1 0.7 shard_map.94
  (69 shorter events, 2.2 us)
Async XLA Ops:
  0.6 8.9 %collective-permute-start = (bf16[256,8192]{1,0:T(8,128)(2,1)}, bf16[256,8192]{1,0:T(8,128)(2,1)S(1)}, u32[]{:S(2)}, u32[]{:S(2)}) collective-permute-start(bf16[256,8192]{1,0:T(8,128)(2,1)} %refs_2_.5), channel_id=1, source_target_pairs={{0,1},{1,0},{2,3},{3,2},{4,5},{5,4},{6,7},{7,6},{8,9},{9,8},{10,11... | collective-permute-start | bytes 12582920 | tf_op jit(solution)/shard_map/ppermute | solution.py:426
  1.1 2.2 %copy-start = (bf16[256,8192]{1,0:T(8,128)(2,1)S(1)}, bf16[256,8192]{1,0:T(8,128)(2,1)}, u32[]{:S(2)}) copy-start(bf16[256,8192]{1,0:T(8,128)(2,1)} %refs_2_.5) | copy-start | bytes 12582916
  3.3 3.5 %copy-start.3 = (bf16[1024,256]{1,0:T(8,128)(2,1)S(1)}, bf16[1024,256]{1,0:T(8,128)(2,1)}, u32[]{:S(2)}) copy-start(bf16[1024,256]{1,0:T(8,128)(2,1)} %refs_6_) | copy-start | bytes 1572868
  3.3 3.5 %copy-start.4 = (bf16[1024,256]{1,0:T(8,128)(2,1)S(1)}, bf16[1024,256]{1,0:T(8,128)(2,1)}, u32[]{:S(2)}) copy-start(bf16[1024,256]{1,0:T(8,128)(2,1)} %refs_6_.1) | copy-start | bytes 1572868
  3.3 3.5 %copy-start.7 = (bf16[80,1024]{1,0:T(8,128)(2,1)S(1)}, bf16[80,1024]{1,0:T(8,128)(2,1)}, u32[]{:S(2)}) copy-start(bf16[80,1024]{1,0:T(8,128)(2,1)} %gain_ref.1) | copy-start | bytes 491524
  3.3 27.0 %copy-start.1 = (bf16[256,8192]{1,0:T(8,128)(2,1)S(1)}, bf16[256,8192]{1,0:T(8,128)(2,1)}, u32[]{:S(2)}) copy-start(bf16[256,8192]{1,0:T(8,128)(2,1)} %refs_2_.5) | copy-start | bytes 12582916
  3.6 50.0 %collective-permute-start.9 = (bf16[256,4096]{1,0:T(8,128)(2,1)S(1)}, bf16[256,4096]{1,0:T(8,128)(2,1)}, u32[]{:S(2)}, u32[]{:S(2)}) collective-permute-start(bf16[256,4096]{1,0:T(8,128)(2,1)S(1)} %shard_map.86), channel_id=1, source_target_pairs={{0,2},{2,0},{4,6},{6,4},{8,10},{10,8},{12,14},{14,12},{1,3},{3,1},... | collective-permute-start | bytes 6291464 | tf_op jit(solution)/shard_map/ppermute | solution.py:417
  7.1 0.8 copy-start.2
  7.9 15.5 %collective-permute-start.1 = (bf16[272,512]{1,0:T(8,128)(2,1)S(1)}, bf16[272,512]{1,0:T(8,128)(2,1)S(1)}, u32[]{:S(2)}, u32[]{:S(2)}) collective-permute-start(bf16[272,512]{1,0:T(8,128)(2,1)S(1)} %get-tuple-element.34), channel_id=1, source_target_pairs={{0,4},{2,6},{4,0},{6,2},{8,12},{10,14},{12,8},{14,10},{1,5},{3,7},... | collective-permute-start | bytes 835592 | tf_op jit(solution)/shard_map/ppermute | solution.py:420
  9.5 19.2 %copy-start.9 = (bf16[256,8192]{1,0:T(8,128)(2,1)}, bf16[256,8192]{1,0:T(8,128)(2,1)S(1)}, u32[]{:S(2)}) copy-start(bf16[256,8192]{1,0:T(8,128)(2,1)S(1)} %collective-permute-done.refs_1_.refs_3_) | copy-start | bytes 12582916
  9.5 19.2 %collective-permute-start.2 = (bf16[272,512]{1,0:T(8,128)(2,1)S(1)}, bf16[272,512]{1,0:T(8,128)(2,1)S(1)}, u32[]{:S(2)}, u32[]{:S(2)}) collective-permute-start(bf16[272,512]{1,0:T(8,128)(2,1)S(1)} %get-tuple-element.37), channel_id=1, source_target_pairs={{0,4},{2,6},{4,0},{6,2},{8,12},{10,14},{12,8},{14,10},{1,5},{3,7},... | collective-permute-start | bytes 835592 | tf_op jit(solution)/shard_map/ppermute | solution.py:420
  11.1 20.1 %collective-permute-start.3 = (bf16[272,512]{1,0:T(8,128)(2,1)S(1)}, bf16[272,512]{1,0:T(8,128)(2,1)S(1)}, u32[]{:S(2)}, u32[]{:S(2)}) collective-permute-start(bf16[272,512]{1,0:T(8,128)(2,1)S(1)} %get-tuple-element.34), channel_id=1, source_target_pairs={{0,8},{2,10},{4,12},{6,14},{8,0},{10,2},{12,4},{14,6},{1,9},{3,11}... | collective-permute-start | bytes 835592 | tf_op jit(solution)/shard_map/ppermute | solution.py:420
  23.4 41.0 %copy-start.10 = (bf16[272,512]{1,0:T(8,128)(2,1)}, bf16[272,512]{1,0:T(8,128)(2,1)S(1)}, u32[]{:S(2)}) copy-start(bf16[272,512]{1,0:T(8,128)(2,1)S(1)} %collective-permute-done.1.refs_5_.refs_8_) | copy-start | bytes 835588
  23.4 19.4 %collective-permute-start.4 = (bf16[272,512]{1,0:T(8,128)(2,1)S(1)}, bf16[272,512]{1,0:T(8,128)(2,1)S(1)}, u32[]{:S(2)}, u32[]{:S(2)}) collective-permute-start(bf16[272,512]{1,0:T(8,128)(2,1)S(1)} %get-tuple-element.37), channel_id=1, source_target_pairs={{0,8},{2,10},{4,12},{6,14},{8,0},{10,2},{12,4},{14,6},{1,9},{3,11}... | collective-permute-start | bytes 835592 | tf_op jit(solution)/shard_map/ppermute | solution.py:420
  25.1 8.4 %collective-permute-start.5 = (bf16[272,512]{1,0:T(8,128)(2,1)S(1)}, bf16[272,512]{1,0:T(8,128)(2,1)S(1)}, u32[]{:S(2)}, u32[]{:S(2)}) collective-permute-start(bf16[272,512]{1,0:T(8,128)(2,1)S(1)} %collective-permute-done.1.refs_5_.refs_8_), channel_id=1, source_target_pairs={{0,16},{16,0},{1,17},{17,1},{2,18},{18,2},{3,19},{19,3},{4,20},{20... | collective-permute-start | bytes 835592 | tf_op jit(solution)/shard_map/ppermute | solution.py:423
  28.7 24.9 %copy-start.11 = (bf16[272,512]{1,0:T(8,128)(2,1)}, bf16[272,512]{1,0:T(8,128)(2,1)S(1)}, u32[]{:S(2)}) copy-start(bf16[272,512]{1,0:T(8,128)(2,1)S(1)} %collective-permute-done.2.refs_6_.refs_9_) | copy-start | bytes 835588
  28.7 14.0 %collective-permute-start.6 = (bf16[272,512]{1,0:T(8,128)(2,1)S(1)}, bf16[272,512]{1,0:T(8,128)(2,1)S(1)}, u32[]{:S(2)}, u32[]{:S(2)}) collective-permute-start(bf16[272,512]{1,0:T(8,128)(2,1)S(1)} %collective-permute-done.2.refs_6_.refs_9_), channel_id=1, source_target_pairs={{0,16},{16,0},{1,17},{17,1},{2,18},{18,2},{3,19},{19,3},{4,20},{20... | collective-permute-start | bytes 835592 | tf_op jit(solution)/shard_map/ppermute | solution.py:423
  31.2 22.4 %copy-start.12 = (bf16[272,512]{1,0:T(8,128)(2,1)}, bf16[272,512]{1,0:T(8,128)(2,1)S(1)}, u32[]{:S(2)}) copy-start(bf16[272,512]{1,0:T(8,128)(2,1)S(1)} %collective-permute-done.3.refs_7_.refs_10_) | copy-start | bytes 835588
  31.2 13.8 %collective-permute-start.10 = (bf16[272,512]{1,0:T(8,128)(2,1)S(1)}, bf16[272,512]{1,0:T(8,128)(2,1)S(1)}, u32[]{:S(2)}, u32[]{:S(2)}) collective-permute-start(bf16[272,512]{1,0:T(8,128)(2,1)S(1)} %collective-permute-done.3.refs_7_.refs_10_), channel_id=1, source_target_pairs={{0,4},{2,6},{4,0},{6,2},{8,12},{10,14},{12,8},{14,10},{1,5},{3,7},... | collective-permute-start | bytes 835592 | tf_op jit(solution)/shard_map/ppermute | solution.py:420
  33.4 23.9 %copy-start.14 = (bf16[272,512]{1,0:T(8,128)(2,1)}, bf16[272,512]{1,0:T(8,128)(2,1)S(1)}, u32[]{:S(2)}) copy-start(bf16[272,512]{1,0:T(8,128)(2,1)S(1)} %collective-permute-done.5.refs_9_.refs_14_) | copy-start | bytes 835588
  33.4 11.6 %collective-permute-start.7 = (bf16[272,512]{1,0:T(8,128)(2,1)S(1)}, bf16[272,512]{1,0:T(8,128)(2,1)S(1)}, u32[]{:S(2)}, u32[]{:S(2)}) collective-permute-start(bf16[272,512]{1,0:T(8,128)(2,1)S(1)} %collective-permute-done.3.refs_7_.refs_10_), channel_id=1, source_target_pairs={{0,16},{16,0},{1,17},{17,1},{2,18},{18,2},{3,19},{19,3},{4,20},{20... | collective-permute-start | bytes 835592 | tf_op jit(solution)/shard_map/ppermute | solution.py:423
  42.8 11.7 %copy-start.13 = (bf16[272,512]{1,0:T(8,128)(2,1)}, bf16[272,512]{1,0:T(8,128)(2,1)S(1)}, u32[]{:S(2)}) copy-start(bf16[272,512]{1,0:T(8,128)(2,1)S(1)} %collective-permute-done.4.refs_8_.refs_11_) | copy-start | bytes 835588
  42.8 16.4 %copy-start.15 = (bf16[272,512]{1,0:T(8,128)(2,1)}, bf16[272,512]{1,0:T(8,128)(2,1)S(1)}, u32[]{:S(2)}) copy-start(bf16[272,512]{1,0:T(8,128)(2,1)S(1)} %collective-permute-done.6.refs_10_.refs_15_) | copy-start | bytes 835588
  42.8 8.7 %collective-permute-start.11 = (bf16[272,512]{1,0:T(8,128)(2,1)S(1)}, bf16[272,512]{1,0:T(8,128)(2,1)}, u32[]{:S(2)}, u32[]{:S(2)}) collective-permute-start(bf16[272,512]{1,0:T(8,128)(2,1)S(1)} %collective-permute-done.4.refs_8_.refs_11_), channel_id=1, source_target_pairs={{0,4},{2,6},{4,0},{6,2},{8,12},{10,14},{12,8},{14,10},{1,5},{3,7},... | collective-permute-start | bytes 835592 | tf_op jit(solution)/shard_map/ppermute | solution.py:420
  43.1 14.2 %collective-permute-start.8 = (bf16[272,512]{1,0:T(8,128)(2,1)S(1)}, bf16[272,512]{1,0:T(8,128)(2,1)S(1)}, u32[]{:S(2)}, u32[]{:S(2)}) collective-permute-start(bf16[272,512]{1,0:T(8,128)(2,1)S(1)} %collective-permute-done.4.refs_8_.refs_11_), channel_id=1, source_target_pairs={{0,16},{16,0},{1,17},{17,1},{2,18},{18,2},{3,19},{19,3},{4,20},{20... | collective-permute-start | bytes 835592 | tf_op jit(solution)/shard_map/ppermute | solution.py:423
  45.0 14.1 %copy-start.18 = (bf16[272,512]{1,0:T(8,128)(2,1)}, bf16[272,512]{1,0:T(8,128)(2,1)S(1)}, u32[]{:S(2)}) copy-start(bf16[272,512]{1,0:T(8,128)(2,1)S(1)} %collective-permute-done.10.refs_12_) | copy-start | bytes 835588
  45.0 14.1 %copy-start.16 = (bf16[272,512]{1,0:T(8,128)(2,1)}, bf16[272,512]{1,0:T(8,128)(2,1)S(1)}, u32[]{:S(2)}) copy-start(bf16[272,512]{1,0:T(8,128)(2,1)S(1)} %collective-permute-done.7.refs_11_.refs_16_) | copy-start | bytes 835588
  51.5 7.7 %collective-permute-start.12 = (bf16[272,512]{1,0:T(8,128)(2,1)S(1)}, bf16[272,512]{1,0:T(8,128)(2,1)S(1)}, u32[]{:S(2)}, u32[]{:S(2)}) collective-permute-start(bf16[272,512]{1,0:T(8,128)(2,1)S(1)} %collective-permute-done.10.refs_12_), channel_id=1, source_target_pairs={{0,16},{16,0},{1,17},{17,1},{2,18},{18,2},{3,19},{19,3},{4,20},{20... | collective-permute-start | bytes 835592 | tf_op jit(solution)/shard_map/ppermute | solution.py:423
  53.7 3.7 %collective-permute-start.13 = (f32[2,256]{1,0:T(2,128)S(1)}, f32[2,256]{1,0:T(2,128)S(1)}, u32[]{:S(2)}, u32[]{:S(2)}) collective-permute-start(f32[2,256]{1,0:T(2,128)S(1)} %get-tuple-element.43), channel_id=1, source_target_pairs={{0,2},{2,0},{4,6},{6,4},{8,10},{10,8},{12,14},{14,12},{1,3},{3,1},... | collective-permute-start | bytes 6152 | tf_op jit(solution)/shard_map/ppermute | solution.py:417
  57.3 1.8 %copy-start.17 = (bf16[272,512]{1,0:T(8,128)(2,1)}, bf16[272,512]{1,0:T(8,128)(2,1)S(1)}, u32[]{:S(2)}) copy-start(bf16[272,512]{1,0:T(8,128)(2,1)S(1)} %collective-permute-done.8.refs_12_.refs_17_) | copy-start | bytes 835588
  59.1 0.7 copy-start.19
  59.1 10.6 %collective-permute-start.14 = (bf16[256,4096]{1,0:T(8,128)(2,1)}, bf16[256,4096]{1,0:T(8,128)(2,1)}, u32[]{:S(2)}, u32[]{:S(2)}) collective-permute-start(bf16[256,4096]{1,0:T(8,128)(2,1)} %collective-permute-done.9.refs_4_), channel_id=1, source_target_pairs={{0,1},{1,0},{2,3},{3,2},{4,5},{5,4},{6,7},{7,6},{8,9},{9,8},{10,11... | collective-permute-start | bytes 6291464 | tf_op jit(solution)/shard_map/ppermute | solution.py:426
  59.9 4.5 %collective-permute-start.15 = (f32[2,256]{1,0:T(2,128)S(1)}, f32[2,256]{1,0:T(2,128)S(1)}, u32[]{:S(2)}, u32[]{:S(2)}) collective-permute-start(f32[2,256]{1,0:T(2,128)S(1)} %bitcast.15), channel_id=1, source_target_pairs={{0,1},{1,0},{2,3},{3,2},{4,5},{5,4},{6,7},{7,6},{8,9},{9,8},{10,11... | collective-permute-start | bytes 6152 | tf_op jit(solution)/shard_map/ppermute | solution.py:426
  60.3 9.4 %collective-permute-start.16 = (bf16[272,512]{1,0:T(8,128)(2,1)}, bf16[272,512]{1,0:T(8,128)(2,1)}, u32[]{:S(2)}, u32[]{:S(2)}) collective-permute-start(bf16[272,512]{1,0:T(8,128)(2,1)} %collective-permute-done.11.refs_13_), channel_id=1, source_target_pairs={{0,16},{16,0},{1,17},{17,1},{2,18},{18,2},{3,19},{19,3},{4,20},{20... | collective-permute-start | bytes 835592 | tf_op jit(solution)/shard_map/ppermute | solution.py:423
  75.7 8.4 %copy-start.8 = (s32[8]{0:T(128)S(1)}, s32[8]{0:T(128)}, u32[]{:S(2)}) copy-start(s32[8]{0:T(128)} %owner_ref.3) | copy-start | bytes 100
  75.7 8.4 %collective-permute-start.17 = (bf16[4,2,128,128]{3,2,1,0:T(8,128)(2,1)}, bf16[4,2,128,128]{3,2,1,0:T(8,128)(2,1)S(1)}, u32[]{:S(2)}, u32[]{:S(2)}) collective-permute-start(bf16[4,2,128,128]{3,2,1,0:T(8,128)(2,1)} %get-tuple-element.48), channel_id=1, source_target_pairs={{0,2},{2,0},{4,6},{6,4},{8,10},{10,8},{12,14},{14,12},{1,3},{3,1},... | collective-permute-start | bytes 786440 | tf_op jit(solution)/shard_map/ppermute | solution.py:417
  82.5 8.1 %collective-permute-start.21 = (bf16[4,2,128,128]{3,2,1,0:T(8,128)(2,1)}, bf16[4,2,128,128]{3,2,1,0:T(8,128)(2,1)S(1)}, u32[]{:S(2)}, u32[]{:S(2)}) collective-permute-start(bf16[4,2,128,128]{3,2,1,0:T(8,128)(2,1)} %get-tuple-element.55), channel_id=1, source_target_pairs={{0,2},{2,0},{4,6},{6,4},{8,10},{10,8},{12,14},{14,12},{1,3},{3,1},... | collective-permute-start | bytes 786440 | tf_op jit(solution)/shard_map/ppermute | solution.py:417
  84.1 1.0 %copy-start.6 = (f32[4,2,128,128]{3,2,1,0:T(8,128)S(1)}, f32[4,2,128,128]{3,2,1,0:T(8,128)}, u32[]{:S(2)}) copy-start(f32[4,2,128,128]{3,2,1,0:T(8,128)} %get-tuple-element.47.keep_ref) | copy-start | bytes 1572868
  86.0 9.1 %collective-permute-start.18 = (bf16[256,128]{1,0:T(8,128)(2,1)S(1)}, bf16[256,128]{1,0:T(8,128)(2,1)S(1)}, u32[]{:S(2)}, u32[]{:S(2)}) collective-permute-start(bf16[256,128]{1,0:T(8,128)(2,1)S(1)} %get-tuple-element.50), channel_id=1, source_target_pairs={{0,4},{2,6},{4,0},{6,2},{8,12},{10,14},{12,8},{14,10},{1,5},{3,7},... | collective-permute-start | bytes 196616 | tf_op jit(solution)/shard_map/ppermute | solution.py:420
  86.3 8.7 %collective-permute-start.19 = (bf16[256,128]{1,0:T(8,128)(2,1)S(1)}, bf16[256,128]{1,0:T(8,128)(2,1)S(1)}, u32[]{:S(2)}, u32[]{:S(2)}) collective-permute-start(bf16[256,128]{1,0:T(8,128)(2,1)S(1)} %get-tuple-element.51), channel_id=1, source_target_pairs={{0,8},{2,10},{4,12},{6,14},{8,0},{10,2},{12,4},{14,6},{1,9},{3,11}... | collective-permute-start | bytes 196616 | tf_op jit(solution)/shard_map/ppermute | solution.py:420
  89.3 6.4 %collective-permute-start.20 = (bf16[256,128]{1,0:T(8,128)(2,1)S(1)}, bf16[256,128]{1,0:T(8,128)(2,1)S(1)}, u32[]{:S(2)}, u32[]{:S(2)}) collective-permute-start(bf16[256,128]{1,0:T(8,128)(2,1)S(1)} %get-tuple-element.52), channel_id=1, source_target_pairs={{0,12},{2,14},{4,8},{6,10},{8,4},{10,6},{12,0},{14,2},{1,13},{3,15... | collective-permute-start | bytes 196616 | tf_op jit(solution)/shard_map/ppermute | solution.py:420
  90.6 1.0 %copy-start.5 = (f32[4,2,128,128]{3,2,1,0:T(8,128)S(1)}, f32[4,2,128,128]{3,2,1,0:T(8,128)}, u32[]{:S(2)}) copy-start(f32[4,2,128,128]{3,2,1,0:T(8,128)} %get-tuple-element.54.keep_ref) | copy-start | bytes 1572868
  92.3 7.3 %collective-permute-start.23 = (bf16[256,128]{1,0:T(8,128)(2,1)S(1)}, bf16[256,128]{1,0:T(8,128)(2,1)S(1)}, u32[]{:S(2)}, u32[]{:S(2)}) collective-permute-start(bf16[256,128]{1,0:T(8,128)(2,1)S(1)} %get-tuple-element.60), channel_id=1, source_target_pairs={{0,8},{2,10},{4,12},{6,14},{8,0},{10,2},{12,4},{14,6},{1,9},{3,11}... | collective-permute-start | bytes 196616 | tf_op jit(solution)/shard_map/ppermute | solution.py:420
  93.1 6.4 %collective-permute-start.24 = (bf16[256,128]{1,0:T(8,128)(2,1)S(1)}, bf16[256,128]{1,0:T(8,128)(2,1)S(1)}, u32[]{:S(2)}, u32[]{:S(2)}) collective-permute-start(bf16[256,128]{1,0:T(8,128)(2,1)S(1)} %get-tuple-element.61), channel_id=1, source_target_pairs={{0,12},{2,14},{4,8},{6,10},{8,4},{10,6},{12,0},{14,2},{1,13},{3,15... | collective-permute-start | bytes 196616 | tf_op jit(solution)/shard_map/ppermute | solution.py:420
  95.7 4.4 %collective-permute-start.22 = (bf16[256,128]{1,0:T(8,128)(2,1)S(1)}, bf16[256,128]{1,0:T(8,128)(2,1)S(1)}, u32[]{:S(2)}, u32[]{:S(2)}) collective-permute-start(bf16[256,128]{1,0:T(8,128)(2,1)S(1)} %get-tuple-element.59), channel_id=1, source_target_pairs={{0,4},{2,6},{4,0},{6,2},{8,12},{10,14},{12,8},{14,10},{1,5},{3,7},... | collective-permute-start | bytes 196616 | tf_op jit(solution)/shard_map/ppermute | solution.py:420
